TPU v7x, 32 devices: a whole 2x2x4 slice. The times are simulated.
32 devices in a mesh: group: 8 (over z, x), expert: 4 (over y, core).
Axes of the slice: x: 2, y: 2, z: 4, core: 2. Of those that a mesh axis runs over, the one named last changes fastest.
Arguments:
- tokens: bfloat16 [16384, 768], P(('group', 'expert')), may hold values from -6 to 6
- gain_attn: float32 [768], replicated, may hold values from 0.5 to 1.5
- w_qkv: bfloat16 [768, 2304], replicated, may hold values from -0.21875 to 0.21875
- w_out: bfloat16 [768, 768], replicated, may hold values from -2.5 to 2.5
- gain_ffn: float32 [768], replicated, may hold values from 0.5 to 1.5
- w_router: bfloat16 [768, 16], replicated, may hold values from -0.15625 to 0.15625
- expert_gate: bfloat16 [16, 768, 2048], P('expert'), may hold values from -0.21875 to 0.21875
- expert_up: bfloat16 [16, 768, 2048], P('expert'), may hold values from -0.21875 to 0.21875
- expert_down: bfloat16 [16, 2048, 768], P('expert'), may hold values from -0.125 to 0.125
- dense_gate: bfloat16 [768, 2048], replicated, may hold values from -0.21875 to 0.21875
- dense_up: bfloat16 [768, 2048], replicated, may hold values from -0.21875 to 0.21875
- dense_down: bfloat16 [2048, 768], replicated, may hold values from -0.125 to 0.125
- expert_ids: int32 [16384, 2], P(('group', 'expert')), may hold values from 0 to 15, all different within a row
- segments: int32 [16384], P(('group', 'expert')), may hold values from 0 to 3, as said below
- cotangent: bfloat16 [16384, 768], P(('group', 'expert')), may hold values from -6 to 6
Outputs:
- mixed_out: bfloat16 [16384, 768], P(('group', 'expert'))
- grad_tokens: float32 [16384, 768], P(('group', 'expert'))
- grad_gain_attn: float32 [768], replicated
- grad_qkv: float32 [768, 2304], P('group', 'expert')
- grad_out_proj: float32 [768, 768], P('group', 'expert')
- grad_gain_ffn: float32 [768], replicated
- grad_router: float32 [768, 16], replicated
- grad_expert_gate: float32 [16, 768, 2048], P('expert', None, 'group')
- grad_expert_up: float32 [16, 768, 2048], P('expert', None, 'group')
- grad_expert_down: float32 [16, 2048, 768], P('expert', 'group')
- grad_dense_gate: float32 [768, 2048], P('group', 'expert')
- grad_dense_up: float32 [768, 2048], P('group', 'expert')
- grad_dense_down: float32 [2048, 768], P('group', 'expert')
Inputs may be any that keep to these rules, and one draw needn't show every extreme that they name: `segments`: within each sequence of 2048 tokens the document numbers start at 0, never fall and rise by one at each of three boundaries, one in each of the sequence's first three quarters. `expert_ids`: the two experts of a token differ.
All inputs are finite; a program needn't handle non-finite values.
Results may differ from a plain program's by a relative error of at most 0.017.
Values may be sent and summed in bfloat16 or wider, within the bound.
A program may use at most 320 MiB of HBM per device.

v0:
```python
import jax
import jax.numpy as jnp
from jax import lax
from jax.sharding import PartitionSpec as P

HEADS = 12
HEAD = 64
EXPERTS = 16
WINDOW = 1024
CAP = 80


epsilon = 1e-06


def shifted(x, axis, by):
    count = lax.axis_size(axis)
    pairs = [(i, i + by) for i in range(count) if 0 <= i + by < count]
    return lax.ppermute(x, axis, pairs)


def rmsnorm(values, gain_vec):
    return (
        values * lax.rsqrt(jnp.mean(values * values, axis=-1, keepdims=True) + epsilon) * gain_vec
    )


def rotate(values, places):
    half_size = values.shape[-1] // 2
    powers = jnp.arange(half_size, dtype=jnp.float32) / half_size
    angles = places[:, None] * (10000.0 ** (-powers))[None, :]
    cosine = jnp.cos(angles)[:, None, :]
    sine_part = jnp.sin(angles)[:, None, :]
    first_half = values[..., :half_size]
    second_half = values[..., half_size:]
    return jnp.concatenate(
        [
            first_half * cosine - second_half * sine_part,
            second_half * cosine + first_half * sine_part,
        ],
        axis=-1,
    )


def swiglu(gate_pre, up_pre):
    return jax.nn.silu(gate_pre) * up_pre


def route(logits, chosen):
    route_probs = jax.nn.softmax(logits, axis=-1)
    picked = jnp.sum(route_probs[:, None, :] * chosen, axis=2)
    return picked / jnp.sum(picked, axis=1, keepdims=True)


def expert_forward(arrived, expert_gate, expert_up, expert_down):
    gate_pre = jnp.einsum("erd,edf->erf", arrived, expert_gate, preferred_element_type=jnp.float32)
    up_pre = jnp.einsum("erd,edf->erf", arrived, expert_up, preferred_element_type=jnp.float32)
    activated = swiglu(gate_pre, up_pre).astype(jnp.bfloat16)
    layer_result = jnp.einsum(
        "erf,efd->erd", activated, expert_down, preferred_element_type=jnp.float32
    ).astype(jnp.bfloat16)
    return (layer_result, (gate_pre, up_pre, activated))


def expert_backward(arrived, grad_arrived, kept_values, expert_gate, expert_up, expert_down):
    gate_pre, up_pre, activated = kept_values
    grad_act = jnp.einsum(
        "erd,efd->erf", grad_arrived, expert_down, preferred_element_type=jnp.float32
    )
    grad_down = jnp.einsum(
        "erf,erd->efd", activated, grad_arrived, preferred_element_type=jnp.float32
    )
    pulled = jax.vjp(swiglu, gate_pre, up_pre)[1](grad_act)
    grad_gate_pre = pulled[0].astype(jnp.bfloat16)
    grad_up_pre = pulled[1].astype(jnp.bfloat16)
    grad_gate_w = jnp.einsum(
        "erd,erf->edf", arrived, grad_gate_pre, preferred_element_type=jnp.float32
    )
    grad_up_w = jnp.einsum("erd,erf->edf", arrived, grad_up_pre, preferred_element_type=jnp.float32)
    grad_rows = jnp.einsum(
        "erf,edf->erd", grad_gate_pre, expert_gate, preferred_element_type=jnp.float32
    )
    grad_rows = grad_rows + jnp.einsum(
        "erf,edf->erd", grad_up_pre, expert_up, preferred_element_type=jnp.float32
    )
    return (grad_rows.astype(jnp.bfloat16), (grad_gate_w, grad_up_w, grad_down))


def local(
    tokens,
    gain_attn,
    w_qkv,
    w_out,
    gain_ffn,
    w_router,
    expert_gate,
    expert_up,
    expert_down,
    dense_gate,
    dense_up,
    dense_down,
    expert_ids,
    segments,
    cotangent,
):
    row_count, model_width = tokens.shape
    layer_inputs = tokens.astype(jnp.float32)
    cot_float = cotangent.astype(jnp.float32)
    normed_attn, attn_norm_pull = jax.vjp(rmsnorm, layer_inputs, gain_attn)
    normed_low = normed_attn.astype(jnp.bfloat16)
    packed = jnp.dot(normed_low, w_qkv, preferred_element_type=jnp.float32)
    first_row = lax.axis_index("expert") * row_count
    places = (first_row + jnp.arange(row_count, dtype=jnp.int32)).astype(jnp.float32)

    def embed(packed_in):
        shaped = packed_in.reshape(row_count, 3, HEADS, HEAD)
        return (
            rotate(shaped[:, 0], places) * HEAD ** (-0.5),
            rotate(shaped[:, 1], places),
            shaped[:, 2],
        )

    (queries, keys_rot, values_in), embed_pull = jax.vjp(embed, packed)
    queries_low = queries.astype(jnp.bfloat16)
    kv_low = jnp.concatenate(
        [keys_rot.reshape(row_count, model_width), values_in.reshape(row_count, model_width)],
        axis=1,
    ).astype(jnp.bfloat16)
    seg_low = segments.astype(jnp.bfloat16)
    reach_count = (WINDOW - 1) // row_count + 1
    kv_parts = []
    seg_parts = []
    for distance in range(reach_count, 0, -1):
        moved_kv, moved_seg = shifted((kv_low, seg_low), "expert", distance)
        kv_parts.append(moved_kv)
        seg_parts.append(moved_seg)
    all_kv = jnp.concatenate(kv_parts + [kv_low], axis=0)
    all_seg = jnp.concatenate(seg_parts + [seg_low], axis=0)
    key_count = all_kv.shape[0]
    key_heads = all_kv[:, :model_width].reshape(key_count, HEADS, HEAD)
    value_heads = all_kv[:, model_width:].reshape(key_count, HEADS, HEAD)
    query_pos = first_row + jnp.arange(row_count, dtype=jnp.int32)
    key_pos = first_row - reach_count * row_count + jnp.arange(key_count, dtype=jnp.int32)
    offset = query_pos[:, None] - key_pos[None, :]
    allowed = (
        (offset >= 0)
        & (offset < WINDOW)
        & (key_pos[None, :] >= 0)
        & (seg_low[:, None] == all_seg[None, :])
    )

    def masked_scores():
        raw_scores = jnp.einsum(
            "qhd,khd->hqk", queries_low, key_heads, preferred_element_type=jnp.float32
        )
        return jnp.where(allowed[None], raw_scores, -1e30)

    scores = masked_scores()
    top_score = jnp.max(scores, axis=2, keepdims=True)
    log_total = top_score + jnp.log(jnp.sum(jnp.exp(scores - top_score), axis=2, keepdims=True))
    probs_low = jnp.exp(scores - log_total).astype(jnp.bfloat16)
    attended = jnp.einsum(
        "hqk,khd->qhd", probs_low, value_heads, preferred_element_type=jnp.float32
    )
    attended = attended.reshape(row_count, model_width).astype(jnp.bfloat16)
    hidden = layer_inputs + jnp.dot(attended, w_out, preferred_element_type=jnp.float32)
    normed_ffn, ffn_norm_pull = jax.vjp(rmsnorm, hidden, gain_ffn)
    ffn_low = normed_ffn.astype(jnp.bfloat16)
    labels = jnp.arange(EXPERTS, dtype=jnp.int32)
    chosen = (expert_ids[:, :, None] == labels[None, None, :]).astype(jnp.float32)
    logits = jnp.dot(ffn_low, w_router, preferred_element_type=jnp.float32)
    gate_share, route_pull = jax.vjp(lambda logit_rows: route(logit_rows, chosen), logits)
    flat_ids = expert_ids.reshape(2 * row_count)
    onehot = (flat_ids[:, None] == labels[None, :]).astype(jnp.int32)
    earlier = jnp.cumsum(onehot, axis=0) - onehot
    slot_index = jnp.sum(earlier * onehot, axis=1).reshape(row_count, 2)
    target = jnp.where(slot_index < CAP, expert_ids * CAP + slot_index, -1)
    slot_labels = jnp.arange(EXPERTS * CAP, dtype=jnp.int32)
    dispatch = (jnp.transpose(target)[:, :, None] == slot_labels[None, None, :]).astype(
        jnp.bfloat16
    )
    send_rows = jnp.einsum("krs,rd->sd", dispatch, ffn_low, preferred_element_type=jnp.float32)
    send_rows = send_rows.astype(jnp.bfloat16).reshape(EXPERTS, CAP, model_width)
    scaled_cot = (jnp.transpose(gate_share)[:, :, None] * cot_float[None]).astype(jnp.bfloat16)
    send_grads = jnp.einsum("krs,krd->sd", dispatch, scaled_cot, preferred_element_type=jnp.float32)
    send_grads = send_grads.astype(jnp.bfloat16).reshape(EXPERTS, CAP, model_width)
    arrived = lax.all_to_all(send_rows, "expert", split_axis=0, concat_axis=1, tiled=True)
    layer_result, kept_values = expert_forward(arrived, expert_gate, expert_up, expert_down)
    came_back = lax.all_to_all(layer_result, "expert", split_axis=1, concat_axis=0, tiled=True)
    dense_gate_pre = jnp.dot(ffn_low, dense_gate, preferred_element_type=jnp.float32)
    dense_up_pre = jnp.dot(ffn_low, dense_up, preferred_element_type=jnp.float32)
    dense_act = swiglu(dense_gate_pre, dense_up_pre).astype(jnp.bfloat16)
    dense_out = jnp.dot(dense_act, dense_down, preferred_element_type=jnp.float32)
    fetched = jnp.einsum(
        "krs,sd->krd",
        dispatch,
        came_back.reshape(EXPERTS * CAP, model_width),
        preferred_element_type=jnp.float32,
    )
    mixture = gate_share[:, 0:1] * fetched[0] + gate_share[:, 1:2] * fetched[1]
    mixed_out = (hidden + mixture + dense_out).astype(jnp.bfloat16)
    grad_dense_act = jnp.einsum(
        "rd,fd->rf", cotangent, dense_down, preferred_element_type=jnp.float32
    )
    grad_dense_down = jnp.einsum(
        "rf,rd->fd", dense_act, cotangent, preferred_element_type=jnp.float32
    )
    dense_pulled = jax.vjp(swiglu, dense_gate_pre, dense_up_pre)[1](grad_dense_act)
    grad_dense_gpre = dense_pulled[0].astype(jnp.bfloat16)
    grad_dense_upre = dense_pulled[1].astype(jnp.bfloat16)
    grad_dense_gate = jnp.einsum(
        "rd,rf->df", ffn_low, grad_dense_gpre, preferred_element_type=jnp.float32
    )
    grad_dense_up = jnp.einsum(
        "rd,rf->df", ffn_low, grad_dense_upre, preferred_element_type=jnp.float32
    )
    grad_normed = jnp.einsum(
        "rf,df->rd", grad_dense_gpre, dense_gate, preferred_element_type=jnp.float32
    )
    grad_normed = grad_normed + jnp.einsum(
        "rf,df->rd", grad_dense_upre, dense_up, preferred_element_type=jnp.float32
    )
    grad_arrived = lax.all_to_all(send_grads, "expert", split_axis=0, concat_axis=1, tiled=True)
    grad_rows, expert_terms = expert_backward(
        arrived, grad_arrived, kept_values, expert_gate, expert_up, expert_down
    )
    grad_back = lax.all_to_all(grad_rows, "expert", split_axis=1, concat_axis=0, tiled=True)
    grad_normed = grad_normed + jnp.einsum(
        "krs,sd->rd",
        dispatch,
        grad_back.reshape(EXPERTS * CAP, model_width),
        preferred_element_type=jnp.float32,
    )
    grad_gates = jnp.transpose(jnp.sum(cot_float[None] * fetched, axis=2))
    grad_logits = route_pull(grad_gates)[0].astype(jnp.bfloat16)
    grad_router = jnp.einsum("rd,re->de", ffn_low, grad_logits, preferred_element_type=jnp.float32)
    grad_normed = grad_normed + jnp.einsum(
        "re,de->rd", grad_logits, w_router, preferred_element_type=jnp.float32
    )
    grad_hidden_norm, grad_gain_ffn = ffn_norm_pull(grad_normed)
    grad_hidden = cot_float + grad_hidden_norm
    grad_hidden_low = grad_hidden.astype(jnp.bfloat16)
    grad_out_proj = jnp.einsum(
        "rd,re->de", attended, grad_hidden_low, preferred_element_type=jnp.float32
    )
    grad_attended = jnp.einsum(
        "re,de->rd", grad_hidden_low, w_out, preferred_element_type=jnp.float32
    )
    grad_attended = grad_attended.astype(jnp.bfloat16).reshape(row_count, HEADS, HEAD)
    scores = masked_scores()
    attn_probs = jnp.exp(scores - log_total)
    probs_again = attn_probs.astype(jnp.bfloat16)
    grad_probs = jnp.einsum(
        "qhd,khd->hqk", grad_attended, value_heads, preferred_element_type=jnp.float32
    )
    grad_values = jnp.einsum(
        "hqk,qhd->khd", probs_again, grad_attended, preferred_element_type=jnp.float32
    )
    row_total = jnp.sum(attn_probs * grad_probs, axis=2, keepdims=True)
    grad_scores = (attn_probs * (grad_probs - row_total)).astype(jnp.bfloat16)
    grad_queries = jnp.einsum(
        "hqk,khd->qhd", grad_scores, key_heads, preferred_element_type=jnp.float32
    )
    grad_keys = jnp.einsum(
        "hqk,qhd->khd", grad_scores, queries_low, preferred_element_type=jnp.float32
    )
    grad_kv = jnp.concatenate(
        [grad_keys.reshape(key_count, model_width), grad_values.reshape(key_count, model_width)],
        axis=1,
    )
    own_grad = grad_kv[reach_count * row_count :]
    for distance in range(1, reach_count + 1):
        begin_at = (reach_count - distance) * row_count
        rim_part = grad_kv[begin_at : begin_at + row_count]
        own_grad = own_grad + shifted(rim_part, "expert", -distance)
    grad_keys_own = own_grad[:, :model_width].reshape(row_count, HEADS, HEAD)
    grad_values_own = own_grad[:, model_width:].reshape(row_count, HEADS, HEAD)
    grad_packed = embed_pull((grad_queries, grad_keys_own, grad_values_own))[0].astype(jnp.bfloat16)
    grad_qkv = jnp.einsum("rd,re->de", normed_low, grad_packed, preferred_element_type=jnp.float32)
    grad_normed_attn = jnp.einsum(
        "re,de->rd", grad_packed, w_qkv, preferred_element_type=jnp.float32
    )
    grad_inputs_norm, grad_gain_attn = attn_norm_pull(grad_normed_attn)
    grad_tokens = grad_hidden + grad_inputs_norm
    sum_gate, sum_up, sum_down = (
        lax.psum_scatter(expert_terms[0], "group", scatter_dimension=2, tiled=True),
        lax.psum_scatter(expert_terms[1], "group", scatter_dimension=2, tiled=True),
        lax.psum_scatter(expert_terms[2], "group", scatter_dimension=1, tiled=True),
    )
    first_pass = (
        lax.psum_scatter(grad_qkv, "group", scatter_dimension=0, tiled=True),
        lax.psum_scatter(grad_out_proj, "group", scatter_dimension=0, tiled=True),
        lax.psum_scatter(grad_dense_gate, "group", scatter_dimension=0, tiled=True),
        lax.psum_scatter(grad_dense_up, "group", scatter_dimension=0, tiled=True),
        lax.psum_scatter(grad_dense_down, "group", scatter_dimension=0, tiled=True),
    )
    second_pass = (
        lax.psum_scatter(first_pass[0], "expert", scatter_dimension=1, tiled=True),
        lax.psum_scatter(first_pass[1], "expert", scatter_dimension=1, tiled=True),
        lax.psum_scatter(first_pass[2], "expert", scatter_dimension=1, tiled=True),
        lax.psum_scatter(first_pass[3], "expert", scatter_dimension=1, tiled=True),
        lax.psum_scatter(first_pass[4], "expert", scatter_dimension=1, tiled=True),
    )
    router_sum, gains_sum = lax.psum(
        (grad_router, jnp.stack([grad_gain_attn, grad_gain_ffn])), ("group", "expert")
    )
    return (
        mixed_out,
        grad_tokens,
        gains_sum[0],
        second_pass[0],
        second_pass[1],
        gains_sum[1],
        router_sum,
        sum_gate,
        sum_up,
        sum_down,
        second_pass[2],
        second_pass[3],
        second_pass[4],
    )


def solution(mesh):
    in_specs = (
        P(("group", "expert"), None),
        P(),
        P(),
        P(),
        P(),
        P(),
        P("expert", None, None),
        P("expert", None, None),
        P("expert", None, None),
        P(),
        P(),
        P(),
        P(("group", "expert"), None),
        P(("group", "expert")),
        P(("group", "expert"), None),
    )
    out_specs = (
        P(("group", "expert"), None),
        P(("group", "expert"), None),
        P(),
        P("group", "expert"),
        P("group", "expert"),
        P(),
        P(),
        P("expert", None, "group"),
        P("expert", None, "group"),
        P("expert", "group", None),
        P("group", "expert"),
        P("group", "expert"),
        P("group", "expert"),
    )
    return jax.shard_map(local, mesh=mesh, in_specs=in_specs, out_specs=out_specs, check_vma=False)
```

profile of v0, /device:TPU:0, one launch (start us, length us, event | category | flops | bytes accessed | tf_op | source)
XLA Modules:
  0.0 2398.9 jit_solution(2353488505149270933)
XLA Ops:
  39.7 9.3 reduce-window.6
  68.8 15.0 maximum_maximum_fusion
  85.6 15.0 select_reduce_fusion
  100.6 17.0 exponential_reduce_fusion
  117.7 15.5 fusion.42
  141.4 16.8 all-to-all-start.2
  171.9 10.5 all-to-all-done.2
  187.0 9.2 multiply_convert_fusion.3
  213.2 12.1 fusion.77
  232.2 19.4 multiply_convert_fusion.1
  251.6 9.4 convolution_convert_fusion.1
  268.5 12.3 fusion.82
  280.8 12.7 add_convert_fusion.1
  310.6 16.1 all-to-all-done.3
  338.4 18.7 fusion.21
  357.1 27.9 %multiply_reduce_fusion = (f32[12,512]{1,0:T(8,128)S(1)}, f32[12,512,1536]{2,1,0:T(8,128)}) fusion(f32[12,512,1536]{2,1,0:T(8,128)} %get-tuple-element.119, f32[12,512]{1,0:T(8,128)} %copy-done.30, pred[512,1536]{1,0:T(8,128)(4,1)} %copy-done.2, bf16[512,12,64]{0,2,1:T(8,128)(2,1)} %bitcast.178, bf16[1536,12,64]{0,2,1:T(8,128)(2,1)} %bitcast.181), kind=kOutput, calls=%fused_computation.1 | convolution fusion | flops 1245702144 | bytes 79478784 | tf_op jit(solution)/shard_map/qhd,khd->hqk/dot_general | solution.py:253
  384.9 24.8 %multiply_convert_fusion = bf16[12,512,1536]{2,1,0:T(8,128)(2,1)S(1)} fusion(f32[12,512,1536]{2,1,0:T(8,128)} %get-tuple-element.128, f32[12,512,1536]{2,1,0:T(8,128)} %get-tuple-element.119, f32[12,512]{1,0:T(8,128)S(1)} %get-tuple-element.127, f32[12,512]{1,0:T(8,128)S(1)} %copy-done.31, pred[512,1536]{1,0:T(8,128)(4,1)} %copy-done.2), kind=kLoop, calls=%fused_computation | loop fusion | flops 47185920 | bytes 95207424 | tf_op jit(solution)/shard_map/convert_element_type | solution.py:260
  409.7 7.9 fusion.58
  429.2 10.5 multiply_bitcast_fusion
  439.8 90.7 %collective-permute-done.5 = f32[512,1536]{0,1:T(8,128)} collective-permute-done((f32[512,1536]{0,1:T(8,128)}, f32[512,1536]{0,1:T(8,128)}, u32[]{:S(2)}, u32[]{:S(2)}) %collective-permute-start.5) | collective-permute-done | bytes 3145760 | tf_op jit(solution)/shard_map/ppermute | solution.py:19
  565.9 107.7 %reduce-scatter.20.cloned.1.call-done = f32[96,2304]{1,0:T(8,128)} async-done(((f32[768,2304]{1,0:T(8,128)}), f32[96,2304]{1,0:T(8,128)}) %reduce-scatter.20.cloned.1.call-update) | async-done | bytes 884752 | tf_op jit(solution)/shard_map/reduce_scatter | solution.py:291
  676.2 118.4 %reduce-scatter.30.cloned.1.call-done = f32[96,2048]{1,0:T(8,128)} async-done(((f32[768,2048]{1,0:T(8,128)}), f32[96,2048]{1,0:T(8,128)}) %reduce-scatter.30.cloned.1.call-update) | async-done | bytes 786448 | tf_op jit(solution)/shard_map/reduce_scatter | solution.py:293
  794.6 120.9 %reduce-scatter.34.cloned.1.call-done = f32[96,2048]{1,0:T(8,128)} async-done(((f32[768,2048]{1,0:T(8,128)}), f32[96,2048]{1,0:T(8,128)}) %reduce-scatter.34.cloned.1.call-update) | async-done | bytes 786448 | tf_op jit(solution)/shard_map/reduce_scatter | solution.py:294
  916.0 120.5 %reduce-scatter.38.cloned.1.call-done = f32[256,768]{1,0:T(8,128)} async-done(((f32[2048,768]{1,0:T(8,128)}), f32[256,768]{1,0:T(8,128)}) %reduce-scatter.38.cloned.1.call-update) | async-done | bytes 786448 | tf_op jit(solution)/shard_map/reduce_scatter | solution.py:295
  1038.9 14.1 fusion.86
  1053.1 14.8 fusion.85
  1068.1 14.8 fusion.84
  1097.1 40.6 %all-reduce.7 = (f32[2,768]{1,0:T(2,128)}, f32[768,16]{0,1:T(8,128)}) all-reduce(f32[2,768]{1,0:T(2,128)S(1)} %pad_maximum_fusion.3, f32[768,16]{0,1:T(8,128)} %fusion.90), channel_id=1, replica_groups=mesh['group'=8,'expert'=4] {'group','expert'}, use_global_device_ids=true, to_apply=%region_21.22 | all-reduce | flops 13824 | bytes 110592 | tf_op jit(solution)/shard_map/psum | solution.py:304
  1146.9 20.1 reduce-scatter.44.cloned.1.call-done
  1167.0 408.4 %reduce-scatter.28.cloned.1.call-done = f32[4,256,768]{2,1,0:T(8,128)} async-done(((f32[4,2048,768]{2,1,0:T(8,128)}), f32[4,256,768]{2,1,0:T(8,128)}) %reduce-scatter.28.cloned.1.call-update) | async-done | bytes 3145744 | tf_op jit(solution)/shard_map/reduce_scatter | solution.py:288
  1575.4 408.3 %reduce-scatter.26.cloned.1.call-done = f32[4,768,256]{2,1,0:T(8,128)} async-done(((f32[4,768,2048]{2,1,0:T(8,128)}), f32[4,768,256]{2,1,0:T(8,128)}) %reduce-scatter.26.cloned.1.call-update) | async-done | bytes 3145744 | tf_op jit(solution)/shard_map/reduce_scatter | solution.py:287
  1983.7 408.5 %reduce-scatter.24.cloned.1.call-done = f32[4,768,256]{2,1,0:T(8,128)} async-done(((f32[4,768,2048]{2,1,0:T(8,128)}), f32[4,768,256]{2,1,0:T(8,128)}) %reduce-scatter.24.cloned.1.call-update) | async-done | bytes 3145744 | tf_op jit(solution)/shard_map/reduce_scatter | solution.py:286
  (306 shorter events, 215.8 us)
Async XLA Ops:
  8.6 54.0 %collective-permute-start.3 = (bf16[512]{0:T(512)(128)(2,1)}, bf16[512]{0:T(512)(128)(2,1)}, u32[]{:S(2)}, u32[]{:S(2)}) collective-permute-start(bf16[512]{0:T(512)(128)(2,1)} %convert_element_type.111), channel_id=1, source_target_pairs={{0,1},{1,2},{2,3},{4,5},{5,6},{6,7},{8,9},{9,10},{10,11},{12,13},{... | collective-permute-start | bytes 3080 | tf_op jit(solution)/shard_map/ppermute | solution.py:19
  11.5 51.1 %collective-permute-start.2 = (bf16[512]{0:T(512)(128)(2,1)}, bf16[512]{0:T(512)(128)(2,1)}, u32[]{:S(2)}, u32[]{:S(2)}) collective-permute-start(bf16[512]{0:T(512)(128)(2,1)} %convert_element_type.111), channel_id=1, source_target_pairs={{0,2},{1,3},{4,6},{5,7},{8,10},{9,11},{12,14},{13,15},{16,18},{17,... | collective-permute-start | bytes 3080 | tf_op jit(solution)/shard_map/ppermute | solution.py:19
  29.8 35.4 %collective-permute-start.1 = (bf16[512,1536]{0,1:T(8,128)(2,1)}, bf16[512,1536]{0,1:T(8,128)(2,1)}, u32[]{:S(2)}, u32[]{:S(2)}) collective-permute-start(bf16[512,1536]{0,1:T(8,128)(2,1)} %pad_maximum_fusion.1), channel_id=1, source_target_pairs={{0,1},{1,2},{2,3},{4,5},{5,6},{6,7},{8,9},{9,10},{10,11},{12,13},{... | collective-permute-start | bytes 4718600 | tf_op jit(solution)/shard_map/ppermute | solution.py:19
  32.4 36.4 %collective-permute-start = (bf16[512,1536]{0,1:T(8,128)(2,1)}, bf16[512,1536]{0,1:T(8,128)(2,1)}, u32[]{:S(2)}, u32[]{:S(2)}) collective-permute-start(bf16[512,1536]{0,1:T(8,128)(2,1)} %pad_maximum_fusion.1), channel_id=1, source_target_pairs={{0,2},{1,3},{4,6},{5,7},{8,10},{9,11},{12,14},{13,15},{16,18},{17,... | collective-permute-start | bytes 4718600 | tf_op jit(solution)/shard_map/ppermute | solution.py:19
  65.2 52.4 %copy-start.2 = (pred[512,1536]{1,0:T(8,128)(4,1)}, pred[512,1536]{1,0:T(8,128)(4,1)S(1)}, u32[]{:S(2)}) copy-start(pred[512,1536]{1,0:T(8,128)(4,1)S(1)} %fusion.18) | copy-start | bytes 2359300
  100.6 17.1 copy-start.11
  117.6 15.6 copy-start.30
  117.6 15.6 copy-start.22
  136.2 173.6 %copy-start.52 = (f32[512]{0:T(512)}, f32[512]{0:T(512)S(1)}, u32[]{:S(2)}) copy-start(f32[512]{0:T(512)S(1)} %get-tuple-element.122) | copy-start | bytes 6148
  137.5 172.3 %copy-start.51 = (f32[512,2]{0,1:T(2,128)}, f32[512,2]{0,1:T(2,128)S(1)}, u32[]{:S(2)}) copy-start(f32[512,2]{0,1:T(2,128)S(1)} %get-tuple-element.83) | copy-start | bytes 12292
  137.5 172.3 %copy-start.53 = (f32[512]{0:T(512)}, f32[512]{0:T(512)S(1)}, u32[]{:S(2)}) copy-start(f32[512]{0:T(512)S(1)} %get-tuple-element.82) | copy-start | bytes 6148
  141.4 41.0 %all-to-all-start.2 = ((bf16[16,80,768]{2,1,0:T(8,128)(2,1)}), bf16[16,80,768]{2,1,0:T(8,128)(2,1)}, u32[]{:S(2)}, u32[]{:S(2)}) async-start(bf16[16,80,768]{2,1,0:T(8,128)(2,1)} %bitcast.200), calls=%async_computation.2 | async-start | bytes 3932160 | tf_op jit(solution)/shard_map/all_to_all | solution.py:223
  182.4 29.0 %all-to-all-start = ((bf16[16,80,768]{2,1,0:T(8,128)(2,1)}), bf16[16,80,768]{2,1,0:T(8,128)(2,1)}, u32[]{:S(2)}, u32[]{:S(2)}) async-start(bf16[16,80,768]{2,1,0:T(8,128)(2,1)} %bitcast.199), calls=%async_computation | async-start | bytes 3932160 | tf_op jit(solution)/shard_map/all_to_all | solution.py:187
  263.9 34.1 %all-to-all-start.1 = ((bf16[4,320,768]{2,0,1:T(4,128)(2,1)}), bf16[4,320,768]{2,0,1:T(4,128)(2,1)}, u32[]{:S(2)}, u32[]{:S(2)}) async-start(bf16[4,320,768]{2,0,1:T(4,128)(2,1)} %copy.110), calls=%async_computation.1 | async-start | bytes 3932160 | tf_op jit(solution)/shard_map/all_to_all | solution.py:189
  298.0 28.8 %all-to-all-start.3 = ((bf16[4,320,768]{2,0,1:T(4,128)(2,1)}), bf16[4,320,768]{2,0,1:T(4,128)(2,1)}, u32[]{:S(2)}, u32[]{:S(2)}) async-start(bf16[4,320,768]{2,0,1:T(4,128)(2,1)} %copy.114), calls=%async_computation.3 | async-start | bytes 3932160 | tf_op jit(solution)/shard_map/all_to_all | solution.py:227
  302.4 261.5 %reduce-scatter.22.cloned.1.call-start = ((), (), s32[]{:S(2)}) async-start(), calls=%async_computation.18 | async-start | bytes 2654208 | tf_op jit(solution)/shard_map/reduce_scatter | solution.py:292
  310.6 19.5 copy-start.44
  357.1 27.9 %copy-start.31 = (f32[12,512]{1,0:T(8,128)S(1)}, f32[12,512]{1,0:T(8,128)}, u32[]{:S(2)}) copy-start(f32[12,512]{1,0:T(8,128)} %copy-done.30) | copy-start | bytes 73732
  424.4 15.4 collective-permute-start.4
  425.7 104.8 %collective-permute-start.5 = (f32[512,1536]{0,1:T(8,128)}, f32[512,1536]{0,1:T(8,128)}, u32[]{:S(2)}, u32[]{:S(2)}) collective-permute-start(f32[512,1536]{0,1:T(8,128)} %get-tuple-element.92), channel_id=1, source_target_pairs={{2,0},{3,1},{6,4},{7,5},{10,8},{11,9},{14,12},{15,13},{18,16},{19,... | collective-permute-start | bytes 9437192 | tf_op jit(solution)/shard_map/ppermute | solution.py:19
  429.2 244.3 %reduce-scatter.20.cloned.1.call-start = ((), (), s32[]{:S(2)}) async-start(), calls=%async_computation.17 | async-start | bytes 7962624 | tf_op jit(solution)/shard_map/reduce_scatter | solution.py:291
  544.1 250.5 %reduce-scatter.30.cloned.1.call-start = ((), (), s32[]{:S(2)}) async-start(), calls=%async_computation.22 | async-start | bytes 7077888 | tf_op jit(solution)/shard_map/reduce_scatter | solution.py:293
  550.5 365.0 %reduce-scatter.34.cloned.1.call-start = ((), (), s32[]{:S(2)}) async-start(), calls=%async_computation.24 | async-start | bytes 7077888 | tf_op jit(solution)/shard_map/reduce_scatter | solution.py:294
  557.4 479.1 %reduce-scatter.38.cloned.1.call-start = ((), (), s32[]{:S(2)}) async-start(), calls=%async_computation.26 | async-start | bytes 7077888 | tf_op jit(solution)/shard_map/reduce_scatter | solution.py:295
  563.8 579.7 %reduce-scatter.42.cloned.1.call-start = ((), (), s32[]{:S(2)}) async-start(), calls=%async_computation.28 | async-start | bytes 491520
  565.8 579.3 %reduce-scatter.40.cloned.1.call-start = ((), (), s32[]{:S(2)}) async-start(), calls=%async_computation.27 | async-start | bytes 1474560
  676.1 470.8 %reduce-scatter.32.cloned.1.call-start = ((), (), s32[]{:S(2)}) async-start(), calls=%async_computation.23 | async-start | bytes 983040 | tf_op jit(solution)/shard_map/reduce_scatter | solution.py:300
  794.6 352.4 %reduce-scatter.36.cloned.1.call-start = ((), (), s32[]{:S(2)}) async-start(), calls=%async_computation.25 | async-start | bytes 983040 | tf_op jit(solution)/shard_map/reduce_scatter | solution.py:301
  915.6 251.4 %reduce-scatter.44.cloned.1.call-start = ((), (), s32[]{:S(2)}) async-start(), calls=%async_computation.29 | async-start | bytes 983040
  1038.9 536.5 %reduce-scatter.28.cloned.1.call-start = ((), (), s32[]{:S(2)}) async-start(), calls=%async_computation.21 | async-start | bytes 28311552 | tf_op jit(solution)/shard_map/reduce_scatter | solution.py:288
  1053.0 930.6 %reduce-scatter.26.cloned.1.call-start = ((), (), s32[]{:S(2)}) async-start(), calls=%async_computation.20 | async-start | bytes 28311552 | tf_op jit(solution)/shard_map/reduce_scatter | solution.py:287
  1067.9 1324.2 %reduce-scatter.24.cloned.1.call-start = ((), (), s32[]{:S(2)}) async-start(), calls=%async_computation.19 | async-start | bytes 28311552 | tf_op jit(solution)/shard_map/reduce_scatter | solution.py:286
  (69 other events, 324.8 us)
Sparse Core Ops, SparseCore 0:
  429.3 73.7 reduce-scatter.21
  544.2 129.2 reduce-scatter.19
  677.5 116.9 reduce-scatter.29
  798.4 117.0 reduce-scatter.33
  919.4 117.0 reduce-scatter.37
  1039.0 19.9 reduce-scatter.41
  1061.8 25.7 reduce-scatter.39
  1090.7 23.3 reduce-scatter.31
  1117.3 23.5 reduce-scatter.35
  1143.8 23.1 reduce-scatter.43
  1172.0 403.3 reduce-scatter.27
  1580.2 403.4 reduce-scatter.25
  1988.6 403.4 reduce-scatter.23
where the time goes:
time: 2410 us; the launch traced here: 2400 us
  waiting for transfers between devices  1840 us (76%)
  matrix products  296 us (12%)
  other arithmetic  106 us (4%)
  local copies, waits for them, and re-layouts  54.7 us (2%)
  starting transfers between devices  47.2 us (2%)
  blocking collectives  40.6 us (2%)
    reduce_scatter x1, waiting for transfers between devices, local(): lax.psum_scatter(expert_terms[0], 'group', scatter_dimension=2, tiled=True)  408 us
    reduce_scatter x1, waiting for transfers between devices, local(): lax.psum_scatter(expert_terms[2], 'group', scatter_dimension=1, tiled=True)  408 us
    reduce_scatter x1, waiting for transfers between devices, local(): lax.psum_scatter(expert_terms[1], 'group', scatter_dimension=2, tiled=True)  408 us
    reduce_scatter x1, waiting for transfers between devices, local(): lax.psum_scatter(grad_dense_up, 'group', scatter_dimension=0, tiled=True)  121 us
    reduce_scatter x1, waiting for transfers between devices, local(): lax.psum_scatter(grad_dense_down, 'group', scatter_dimension=0, tiled=True)  121 us
    reduce_scatter x1, waiting for transfers between devices, local(): lax.psum_scatter(grad_dense_gate, 'group', scatter_dimension=0, tiled=True)  118 us
    reduce_scatter x1, waiting for transfers between devices, local(): lax.psum_scatter(grad_qkv, 'group', scatter_dimension=0, tiled=True)  108 us
    ppermute x6, waiting for transfers between devices, shifted(): return lax.ppermute(x, axis, pairs)  94.3 us
  transfers between devices with their start and end apart: 23, of which 13 were waited for; matrix products, arithmetic and copies ran while one was open for 10% of the time, Pallas kernels for 0%

commit v1 on v0

v1 whole, which is shorter than its diff:
```python
import jax
import jax.numpy as jnp
from jax import lax
from jax.sharding import PartitionSpec as P

HEADS = 12
HEAD = 64
EXPERTS = 16
WINDOW = 1024
CAP = 80
QUARTERS = 4

epsilon = 1e-06
F32 = jnp.float32
BF16 = jnp.bfloat16


def shifted(x, axis, by):
    count = lax.axis_size(axis)
    pairs = [(i, i + by) for i in range(count) if 0 <= i + by < count]
    return lax.ppermute(x, axis, pairs)


def swap(x, group_bits, expert_bits):
    groups, experts = lax.axis_size("group"), lax.axis_size("expert")
    pairs = [
        (g * experts + e, (g ^ group_bits) * experts + (e ^ expert_bits))
        for g in range(groups)
        for e in range(experts)
    ]
    return lax.ppermute(x, ("group", "expert"), pairs)


def pair_turn(x, by):
    groups = lax.axis_size("group")
    pairs = [(g, (g + 2 * by) % groups) for g in range(groups)]
    return lax.ppermute(x, "group", pairs)


def rmsnorm(values, gain_vec):
    return (
        values * lax.rsqrt(jnp.mean(values * values, axis=-1, keepdims=True) + epsilon) * gain_vec
    )


def rotate(values, places):
    half_size = values.shape[-1] // 2
    powers = jnp.arange(half_size, dtype=jnp.float32) / half_size
    angles = places[:, None] * (10000.0 ** (-powers))[None, :]
    cosine = jnp.cos(angles)[:, None, :]
    sine_part = jnp.sin(angles)[:, None, :]
    first_half = values[..., :half_size]
    second_half = values[..., half_size:]
    return jnp.concatenate(
        [
            first_half * cosine - second_half * sine_part,
            second_half * cosine + first_half * sine_part,
        ],
        axis=-1,
    )


def swiglu(gate_pre, up_pre):
    return jax.nn.silu(gate_pre) * up_pre


def route(logits, chosen):
    route_probs = jax.nn.softmax(logits, axis=-1)
    picked = jnp.sum(route_probs[:, None, :] * chosen, axis=2)
    return picked / jnp.sum(picked, axis=1, keepdims=True)


def dot32(spec, a, b):
    return jnp.einsum(spec, a, b, preferred_element_type=F32)


def pick(x, axis, index):
    return lax.dynamic_index_in_dim(x, index, axis, keepdims=False)


def scatter_sum(x):
    groups, experts = lax.axis_size("group"), lax.axis_size("expert")
    g, e = lax.axis_index("group"), lax.axis_index("expert")
    rows, cols = x.shape
    x = x.reshape(rows, experts, cols // experts)
    bit = 1
    while bit < experts:
        mine = (e // bit) % 2
        left = x.shape[1]
        x = x.reshape(rows, left // 2, 2, cols // experts)
        moved = swap(pick(x, 2, 1 - mine).astype(BF16), 0, bit)
        x = pick(x, 2, mine) + moved.astype(F32)
        bit *= 2
    x = x.reshape(groups, rows // groups, cols // experts)
    bit = 1
    while bit < groups:
        mine = (g // bit) % 2
        left = x.shape[0]
        x = x.reshape(left // 2, 2, rows // groups, cols // experts)
        moved = swap(pick(x, 1, 1 - mine).astype(BF16), bit, 0)
        x = pick(x, 1, mine) + moved.astype(F32)
        bit *= 2
    return x.reshape(rows // groups, cols // experts)


def local(
    tokens,
    gain_attn,
    w_qkv,
    w_out,
    gain_ffn,
    w_router,
    expert_gate,
    expert_up,
    expert_down,
    dense_gate,
    dense_up,
    dense_down,
    expert_ids,
    segments,
    cotangent,
):
    row_count, model_width = tokens.shape
    ff = dense_gate.shape[1]
    groups, experts = lax.axis_size("group"), lax.axis_size("expert")
    g, e = lax.axis_index("group"), lax.axis_index("expert")
    side, outer = g % 2, g // 2
    outers = groups // 2
    own_experts = EXPERTS // experts
    half = own_experts // 2
    peers = 2 * experts
    piece = half * CAP

    labels = jnp.arange(EXPERTS, dtype=jnp.int32)
    flat_ids = expert_ids.reshape(2 * row_count)
    onehot = (flat_ids[:, None] == labels[None, :]).astype(BF16)
    pair_no = jnp.arange(2 * row_count, dtype=jnp.int32)
    before = (pair_no[None, :] < pair_no[:, None]).astype(BF16)
    earlier = dot32("ab,be->ae", before, onehot)
    slot_index = jnp.sum(earlier * onehot.astype(F32), axis=1).astype(jnp.int32)
    slot_index = slot_index.reshape(row_count, 2)
    to_expert = expert_ids // own_experts
    to_side = (expert_ids % own_experts) // half
    relative = (to_side ^ side) * experts + (to_expert ^ e)
    target = jnp.where(
        slot_index < CAP, (relative * half + expert_ids % half) * CAP + slot_index, -1
    )
    slot_labels = jnp.arange(EXPERTS * CAP, dtype=jnp.int32)
    dispatch = (jnp.transpose(target)[:, :, None] == slot_labels[None, None, :]).astype(BF16)
    either = dispatch[0] + dispatch[1]

    def spread(rows):
        parts = rows.reshape(peers, piece, -1)
        return [
            parts[r] if r == 0 else swap(parts[r], r // experts, r % experts) for r in range(peers)
        ]

    def by_expert(parts):
        stacked = jnp.stack([part.reshape(half, CAP, -1) for part in parts], axis=1)
        return stacked.reshape(half, peers * CAP, -1)

    def give_back(rows):
        parts = jnp.transpose(rows.reshape(half, peers, CAP, -1), (1, 0, 2, 3))
        parts = parts.reshape(peers, piece, -1)
        return jnp.concatenate(
            [
                parts[r] if r == 0 else swap(parts[r], r // experts, r % experts)
                for r in range(peers)
            ],
            axis=0,
        )

    send_cot = dot32("rs,rd->sd", either, cotangent).astype(BF16)
    cot_slots = by_expert(spread(send_cot))
    cot_pieces = [cot_slots] + [pair_turn(cot_slots, k) for k in range(1, outers)]

    layer_inputs = tokens.astype(F32)
    cot_float = cotangent.astype(F32)
    normed_attn, attn_norm_pull = jax.vjp(rmsnorm, layer_inputs, gain_attn)
    normed_low = normed_attn.astype(BF16)
    packed = jnp.dot(normed_low, w_qkv, preferred_element_type=F32)
    first_row = e * row_count
    places = (first_row + jnp.arange(row_count, dtype=jnp.int32)).astype(F32)

    def embed(packed_in):
        shaped = packed_in.reshape(row_count, 3, HEADS, HEAD)
        return (
            rotate(shaped[:, 0], places) * HEAD ** (-0.5),
            rotate(shaped[:, 1], places),
            shaped[:, 2],
        )

    (queries, keys_rot, values_in), embed_pull = jax.vjp(embed, packed)
    queries_low = queries.astype(BF16)
    kv_low = jnp.concatenate(
        [keys_rot.reshape(row_count, model_width), values_in.reshape(row_count, model_width)],
        axis=1,
    ).astype(BF16)
    seg_low = segments.astype(BF16)
    per_quarter = max(experts // QUARTERS, 1)
    reach_count = min((WINDOW - 1) // row_count + 1, 2 * per_quarter - 1)
    kv_parts = []
    seg_parts = []
    for distance in range(reach_count, 0, -1):
        moved_kv, moved_seg = shifted((kv_low, seg_low), "expert", distance)
        kv_parts.append(moved_kv)
        seg_parts.append(moved_seg)
    all_kv = jnp.concatenate(kv_parts + [kv_low], axis=0)
    all_seg = jnp.concatenate(seg_parts + [seg_low], axis=0)
    key_count = all_kv.shape[0]
    key_heads = all_kv[:, :model_width].reshape(key_count, HEADS, HEAD)
    value_heads = all_kv[:, model_width:].reshape(key_count, HEADS, HEAD)
    query_pos = first_row + jnp.arange(row_count, dtype=jnp.int32)
    key_pos = first_row - reach_count * row_count + jnp.arange(key_count, dtype=jnp.int32)
    offset = query_pos[:, None] - key_pos[None, :]
    allowed = (
        (offset >= 0)
        & (offset < WINDOW)
        & (key_pos[None, :] >= 0)
        & (seg_low[:, None] == all_seg[None, :])
    )

    def masked_scores():
        raw_scores = dot32("qhd,khd->hqk", queries_low, key_heads)
        return jnp.where(allowed[None], raw_scores, -1e30)

    scores = masked_scores()
    top_score = jnp.max(scores, axis=2, keepdims=True)
    log_total = top_score + jnp.log(jnp.sum(jnp.exp(scores - top_score), axis=2, keepdims=True))
    probs_low = jnp.exp(scores - log_total).astype(BF16)
    attended = dot32("hqk,khd->qhd", probs_low, value_heads)
    attended = attended.reshape(row_count, model_width).astype(BF16)
    hidden = layer_inputs + jnp.dot(attended, w_out, preferred_element_type=F32)
    normed_ffn, ffn_norm_pull = jax.vjp(rmsnorm, hidden, gain_ffn)
    ffn_low = normed_ffn.astype(BF16)
    chosen = (expert_ids[:, :, None] == labels[None, None, :]).astype(F32)
    logits = jnp.dot(ffn_low, w_router, preferred_element_type=F32)
    gate_share, route_pull = jax.vjp(lambda logit_rows: route(logit_rows, chosen), logits)

    send_rows = dot32("rs,rd->sd", either, ffn_low).astype(BF16)
    send_share = jnp.sum(
        dispatch.astype(F32) * jnp.transpose(gate_share)[:, :, None], axis=(0, 1)
    )
    row_slots = by_expert(spread(send_rows))
    share_slots = by_expert(spread(send_share[:, None]))
    row_pieces = [row_slots] + [pair_turn(row_slots, k) for k in range(1, outers)]
    share_pieces = [share_slots] + [pair_turn(share_slots, k) for k in range(1, outers)]

    dense_gate_pre = jnp.dot(ffn_low, dense_gate, preferred_element_type=F32)
    dense_up_pre = jnp.dot(ffn_low, dense_up, preferred_element_type=F32)
    dense_act = swiglu(dense_gate_pre, dense_up_pre).astype(BF16)
    dense_out = jnp.dot(dense_act, dense_down, preferred_element_type=F32)
    grad_dense_act = dot32("rd,fd->rf", cotangent, dense_down)
    grad_dense_down = dot32("rf,rd->fd", dense_act, cotangent)
    dense_pulled = jax.vjp(swiglu, dense_gate_pre, dense_up_pre)[1](grad_dense_act)
    grad_dense_gpre = dense_pulled[0].astype(BF16)
    grad_dense_upre = dense_pulled[1].astype(BF16)
    grad_dense_gate = dot32("rd,rf->df", ffn_low, grad_dense_gpre)
    grad_dense_up = dot32("rd,rf->df", ffn_low, grad_dense_upre)
    grad_normed = dot32("rf,df->rd", grad_dense_gpre, dense_gate)
    grad_normed = grad_normed + dot32("rf,df->rd", grad_dense_upre, dense_up)
    dense_sums = (
        scatter_sum(grad_dense_gate),
        scatter_sum(grad_dense_up),
        scatter_sum(grad_dense_down),
    )

    my_gate = lax.dynamic_slice_in_dim(expert_gate, side * half, half, 0)
    my_up = lax.dynamic_slice_in_dim(expert_up, side * half, half, 0)
    my_down = lax.dynamic_slice_in_dim(expert_down, side * half, half, 0)
    grad_slots = (share_slots * cot_slots.astype(F32)).astype(BF16)
    gate_pre = dot32("erd,edf->erf", row_slots, my_gate)
    up_pre = dot32("erd,edf->erf", row_slots, my_up)
    activated = swiglu(gate_pre, up_pre).astype(BF16)
    layer_result = dot32("erf,efd->erd", activated, my_down).astype(BF16)
    came_back = give_back(layer_result)
    grad_act = dot32("erd,efd->erf", grad_slots, my_down)
    pulled = jax.vjp(swiglu, gate_pre, up_pre)[1](grad_act)
    grad_gate_pre = pulled[0].astype(BF16)
    grad_up_pre = pulled[1].astype(BF16)
    grad_rows = dot32("erf,edf->erd", grad_gate_pre, my_gate)
    grad_rows = (grad_rows + dot32("erf,edf->erd", grad_up_pre, my_up)).astype(BF16)
    grad_back = give_back(grad_rows)

    fetched = dot32("krs,sd->krd", dispatch, came_back)
    mixture = gate_share[:, 0:1] * fetched[0] + gate_share[:, 1:2] * fetched[1]
    mixed_out = (hidden + mixture + dense_out).astype(BF16)
    grad_normed = grad_normed + dot32("rs,sd->rd", either, grad_back)
    grad_gates = jnp.transpose(jnp.sum(cot_float[None] * fetched, axis=2))
    grad_logits = route_pull(grad_gates)[0].astype(BF16)
    grad_router = dot32("rd,re->de", ffn_low, grad_logits)
    grad_normed = grad_normed + dot32("re,de->rd", grad_logits, w_router)
    grad_hidden_norm, grad_gain_ffn = ffn_norm_pull(grad_normed)
    grad_hidden = cot_float + grad_hidden_norm
    grad_hidden_low = grad_hidden.astype(BF16)
    grad_out_proj = dot32("rd,re->de", attended, grad_hidden_low)
    out_sum = scatter_sum(grad_out_proj)
    grad_attended = dot32("re,de->rd", grad_hidden_low, w_out)
    grad_attended = grad_attended.astype(BF16).reshape(row_count, HEADS, HEAD)
    scores = masked_scores()
    attn_probs = jnp.exp(scores - log_total)
    probs_again = attn_probs.astype(BF16)
    grad_probs = dot32("qhd,khd->hqk", grad_attended, value_heads)
    grad_values = dot32("hqk,qhd->khd", probs_again, grad_attended)
    row_total = jnp.sum(attn_probs * grad_probs, axis=2, keepdims=True)
    grad_scores = (attn_probs * (grad_probs - row_total)).astype(BF16)
    grad_queries = dot32("hqk,khd->qhd", grad_scores, key_heads)
    grad_keys = dot32("hqk,qhd->khd", grad_scores, queries_low)
    grad_kv = jnp.concatenate(
        [grad_keys.reshape(key_count, model_width), grad_values.reshape(key_count, model_width)],
        axis=1,
    )
    own_grad = grad_kv[reach_count * row_count :]
    for distance in range(1, reach_count + 1):
        begin_at = (reach_count - distance) * row_count
        rim_part = grad_kv[begin_at : begin_at + row_count].astype(BF16)
        own_grad = own_grad + shifted(rim_part, "expert", -distance).astype(F32)
    grad_keys_own = own_grad[:, :model_width].reshape(row_count, HEADS, HEAD)
    grad_values_own = own_grad[:, model_width:].reshape(row_count, HEADS, HEAD)
    grad_packed = embed_pull((grad_queries, grad_keys_own, grad_values_own))[0].astype(BF16)
    grad_qkv = dot32("rd,re->de", normed_low, grad_packed)
    qkv_sum = scatter_sum(grad_qkv)
    grad_normed_attn = dot32("re,de->rd", grad_packed, w_qkv)
    grad_inputs_norm, grad_gain_attn = attn_norm_pull(grad_normed_attn)
    grad_tokens = grad_hidden + grad_inputs_norm
    router_sum, gains_sum = lax.psum(
        (grad_router, jnp.stack([grad_gain_attn, grad_gain_ffn])), ("group", "expert")
    )

    width = ff // outers
    cut_gate = lax.dynamic_slice_in_dim(my_gate, outer * width, width, 2)
    cut_up = lax.dynamic_slice_in_dim(my_up, outer * width, width, 2)
    cut_down = lax.dynamic_slice_in_dim(my_down, outer * width, width, 1)
    all_rows = jnp.concatenate(row_pieces, axis=1)
    all_cots = jnp.concatenate(cot_pieces, axis=1)
    all_shares = jnp.concatenate(share_pieces, axis=1)
    all_grads = (all_shares * all_cots.astype(F32)).astype(BF16)
    gate_cut = dot32("erd,edf->erf", all_rows, cut_gate)
    up_cut = dot32("erd,edf->erf", all_rows, cut_up)
    act_cut = swiglu(gate_cut, up_cut).astype(BF16)
    grad_act_cut = dot32("erd,efd->erf", all_grads, cut_down)
    pulled = jax.vjp(swiglu, gate_cut, up_cut)[1](grad_act_cut)
    grad_gate_w = dot32("erd,erf->edf", all_rows, pulled[0].astype(BF16))
    grad_up_w = dot32("erd,erf->edf", all_rows, pulled[1].astype(BF16))
    grad_down_w = dot32("erf,erd->efd", act_cut, all_grads)

    def trade(x, axis):
        size = x.shape[axis] // 2
        kept = lax.dynamic_slice_in_dim(x, side * size, size, axis)
        sent = lax.dynamic_slice_in_dim(x, (1 - side) * size, size, axis)
        got = swap(sent.astype(BF16), 1, 0).astype(F32)
        whole = jnp.zeros((2,) + kept.shape, F32)
        whole = lax.dynamic_update_index_in_dim(whole, kept, side, 0)
        whole = lax.dynamic_update_index_in_dim(whole, got, 1 - side, 0)
        return whole.reshape((2 * half,) + kept.shape[1:])

    return (
        mixed_out,
        grad_tokens,
        gains_sum[0],
        qkv_sum,
        out_sum,
        gains_sum[1],
        router_sum,
        trade(grad_gate_w, 2),
        trade(grad_up_w, 2),
        trade(grad_down_w, 1),
        dense_sums[0],
        dense_sums[1],
        dense_sums[2],
    )


def solution(mesh):
    in_specs = (
        P(("group", "expert"), None),
        P(),
        P(),
        P(),
        P(),
        P(),
        P("expert", None, None),
        P("expert", None, None),
        P("expert", None, None),
        P(),
        P(),
        P(),
        P(("group", "expert"), None),
        P(("group", "expert")),
        P(("group", "expert"), None),
    )
    out_specs = (
        P(("group", "expert"), None),
        P(("group", "expert"), None),
        P(),
        P("group", "expert"),
        P("group", "expert"),
        P(),
        P(),
        P("expert", None, "group"),
        P("expert", None, "group"),
        P("expert", "group", None),
        P("group", "expert"),
        P("group", "expert"),
        P("group", "expert"),
    )
    return jax.shard_map(local, mesh=mesh, in_specs=in_specs, out_specs=out_specs, check_vma=False)
```

time: 2410 us -> 950 us (0.39)
  waiting for transfers between devices: 1840 us -> 220 us
  local copies, waits for them, and re-layouts: 54.7 us -> 155 us
  starting transfers between devices: 47.2 us -> 136 us
    reduce_scatter x10 -> x0, waiting for transfers between devices: 1690 us -> none  [the longest x1 408 us: local(): lax.psum_scatter(expert_terms[0], 'group', scatter_dimension=2, tiled=True)]
    ppermute x0 -> x72, waiting for transfers between devices: none -> 220 us  [the longest x63 190 us: swap(): return lax.ppermute(x, ('group', 'expert'), pairs)]
    ppermute x0 -> x72, starting transfers between devices: none -> 127 us  [the longest x63 70.2 us: swap(): return lax.ppermute(x, ('group', 'expert'), pairs)]
    ppermute x6 -> x3, waiting for transfers between devices: 94.3 us -> 0.01 us  [shifted(): return lax.ppermute(x, axis, pairs)]
    another operation x2 -> x19, local copies, waits for them, and re-layouts: 1.35 us -> 38.9 us  [the longest x2 18.7 us: scatter_sum(): x = x.reshape(rows, left // 2, 2, cols // experts)]
    dynamic_slice x0 -> x8, local copies, waits for them, and re-layouts: none -> 32.1 us  [pick(): return lax.dynamic_index_in_dim(x, index, axis, keepdims=False)]
    all_to_all x4 -> x0, waiting for transfers between devices: 32.1 us -> none  [the longest x1 16.1 us: local(): lax.all_to_all(grad_rows, 'expert', split_axis=1, concat_axis=0, tiled=True)]
    all_to_all x4 -> x0, starting transfers between devices: 30.5 us -> none  [the longest x1 16.8 us: local(): lax.all_to_all(send_grads, 'expert', split_axis=0, concat_axis=1, tiled=T...]
  transfers between devices with their start and end apart: 23 -> 75, of which waited for: 13 -> 30; matrix products, arithmetic and copies ran while one was open for 10% -> 55% of each run, Pallas kernels for 0% -> 0%
where the time goes in v1:
time: 950 us; the launch traced here: 940 us
  matrix products  278 us (29%)
  waiting for transfers between devices  220 us (23%)
  local copies, waits for them, and re-layouts  155 us (16%)
  starting transfers between devices  136 us (14%)
  other arithmetic  111 us (12%)
  blocking collectives  38.6 us (4%)
    dot_general x35, matrix products, dot32(): return jnp.einsum(spec, a, b, preferred_element_type=F32)  265 us
    ppermute x63, waiting for transfers between devices, swap(): return lax.ppermute(x, ('group', 'expert'), pairs)  190 us
    ppermute x63, starting transfers between devices, swap(): return lax.ppermute(x, ('group', 'expert'), pairs)  70.2 us
    ppermute x9, starting transfers between devices, pair_turn(): return lax.ppermute(x, 'group', pairs)  56.7 us
    psum x1, blocking collectives, local(): lax.psum((grad_router, jnp.stack([grad_gain_attn, grad_gain_ffn])), ('gro...  38.6 us
    dynamic_slice x8, local copies, waits for them, and re-layouts, pick(): return lax.dynamic_index_in_dim(x, index, axis, keepdims=False)  32.1 us
    ppermute x9, waiting for transfers between devices, pair_turn(): return lax.ppermute(x, 'group', pairs)  29.4 us
    unnamed x238, local copies, waits for them, and re-layouts  28.1 us
  transfers between devices with their start and end apart: 75, of which 30 were waited for; matrix products, arithmetic and copies ran while one was open for 55% of the time, Pallas kernels for 0%

profile of v1, /device:TPU:0, one launch (start us, length us, event | category | flops | bytes accessed | tf_op | source)
XLA Modules:
  0.0 939.8 jit_solution(10889686799035089507)
XLA Ops:
  75.8 10.8 %select_reduce_fusion = (f32[12,512]{1,0:T(8,128)S(1)}, f32[12,512,1024]{2,1,0:T(8,128)}) fusion(pred[512,1024]{1,0:T(8,128)(4,1)S(1)} %fusion.39, bf16[1024,12,64]{0,2,1:T(8,128)(2,1)S(1)} %bitcast.318, f32[512,12,32]{0,2,1:T(8,128)S(1)} %copy-done.34, f32[512,12,32]{0,2,1:T(8,128)S(1)} %copy-done.32), kind=kOutput, calls=%fused_computation.4 | convolution fusion | flops 819062784 | bytes 28860416 | tf_op jit(solution)/shard_map/qhd,khd->hqk/dot_general | solution.py:74
  86.7 11.5 %exponential_reduce_fusion = f32[12,512]{1,0:T(8,128)S(1)} fusion(f32[12,512,1024]{2,1,0:T(8,128)} %get-tuple-element.93, f32[12,512]{1,0:T(8,128)S(1)} %get-tuple-element.92, pred[512,1024]{1,0:T(8,128)(4,1)S(1)} %fusion.39), kind=kLoop, calls=%fused_computation.3 | loop fusion | flops 18868224 | bytes 25739264 | tf_op jit(solution)/shard_map/reduce_sum | solution.py:229
  98.3 11.0 %fusion.82 = bf16[12,64,512]{2,1,0:T(8,128)(2,1)S(1)} fusion(bf16[1024,12,64]{0,2,1:T(8,128)(2,1)S(1)} %bitcast.328, f32[12,512,1024]{2,1,0:T(8,128)} %get-tuple-element.93, f32[12,512]{1,0:T(8,128)S(1)} %log_add_fusion, pred[512,1024]{1,0:T(8,128)(4,1)S(1)} %fusion.39), kind=kOutput, calls=%fused_computation.149 | convolution fusion | flops 824573952 | bytes 28073984 | tf_op jit(solution)/shard_map/hqk,khd->qhd/dot_general | solution.py:74
  141.0 9.1 reshape_reshape.28
  150.1 7.3 constant_dynamic-slice_fusion.4
  161.9 9.5 %reshape_reshape.30 = f32[768,2,2,512]{3,2,1,0:T(2,128)} reshape(f32[768,2048]{1,0:T(8,128)} %fusion.173) | data formatting | bytes 12582912 | tf_op jit(solution)/shard_map/reshape;reshape | solution.py:90
  171.4 7.3 constant_dynamic-slice_fusion.2
  205.2 6.3 collective-permute-done.7
  217.7 7.4 fusion.15
  225.2 10.2 %fusion.19 = f32[2,640,2048]{2,1,0:T(8,128)} fusion(bf16[2,640,768]{2,1,0:T(8,128)(2,1)} %bitcast.20, bf16[4,768,2048]{2,1,0:T(8,128)(2,1)S(1)} %bitcast.342, s32[]{:T(128)S(6)} %select_n.254), kind=kOutput, calls=%fused_computation.37 | convolution fusion | flops 4026531840 | bytes 18743300 | tf_op jit(solution)/shard_map/erd,edf->erf/dot_general | solution.py:74
  235.5 11.7 %fusion.48 = bf16[2,640,768]{2,1,0:T(8,128)(2,1)} fusion(bf16[4,2048,768]{2,1,0:T(8,128)(2,1)} %param.23, s32[]{:T(128)S(6)} %select_n.254, f32[2,640,2048]{2,1,0:T(8,128)S(1)} %fusion.15, f32[2,640,2048]{2,1,0:T(8,128)} %fusion.19), kind=kOutput, calls=%fused_computation.91 | convolution fusion | flops 4043243520 | bytes 29229060 | tf_op jit(solution)/shard_map/erf,efd->erd/dot_general | solution.py:74
  314.2 11.5 %fusion.9 = f32[2,640,2048]{2,1,0:T(8,128)} fusion(bf16[4,2048,768]{2,1,0:T(8,128)(2,1)} %param.23, s32[]{:T(128)S(6)} %select_n.254, bf16[2,640,768]{2,1,0:T(8,128)(2,1)} %bitcast.52, f32[2,640]{1,0:T(2,128)} %mul.539), kind=kOutput, calls=%fused_computation.27 | convolution fusion | flops 4029480960 | bytes 18748420 | tf_op jit(solution)/shard_map/erd,efd->erf/dot_general | solution.py:74
  325.7 12.3 %fusion.13 = f32[2,640,768]{2,1,0:T(8,128)} fusion(bf16[4,768,2048]{2,1,0:T(8,128)(2,1)} %param.22, s32[]{:T(128)S(6)} %select_n.254, f32[2,640,2048]{2,1,0:T(8,128)} %fusion.9, f32[2,640,2048]{2,1,0:T(8,128)} %fusion.19), kind=kOutput, calls=%fused_computation.31 | convolution fusion | flops 4042260480 | bytes 31195140 | tf_op jit(solution)/shard_map/erf,edf->erd/dot_general | solution.py:74
  338.0 17.3 %add_convert_fusion.1 = bf16[2,640,768]{2,1,0:T(8,128)(2,1)} fusion(f32[2,640,768]{2,1,0:T(8,128)} %fusion.13, bf16[4,768,2048]{2,1,0:T(8,128)(2,1)} %param.21, s32[]{:T(128)S(6)} %select_n.254, f32[2,640,2048]{2,1,0:T(8,128)} %fusion.19, f32[2,640,2048]{2,1,0:T(8,128)} %fusion.9, f32[2,640,2048]{2,1,0:T(8,128)} %copy-done.1), kind=kOutput, calls=%fused_computation.56 | convolution fusion | flops 4057333760 | bytes 43646980 | tf_op jit(solution)/shard_map/erf,edf->erd/dot_general | solution.py:74
  357.1 28.2 %collective-permute-done.53 = f32[2,640,1]{1,0,2:T(2,128)S(1)} collective-permute-done((f32[2,640,1]{1,0,2:T(2,128)S(1)}, f32[2,640,1]{1,0,2:T(2,128)S(1)}, u32[]{:S(2)}, u32[]{:S(2)}) %collective-permute-start.53) | collective-permute-done | bytes 5152 | tf_op jit(solution)/shard_map/ppermute | solution.py:37
  385.3 43.8 %collective-permute-start.51 = (f32[2,640,1]{1,0,2:T(2,128)S(1)}, f32[2,640,1]{1,0,2:T(2,128)S(1)}, u32[]{:S(2)}, u32[]{:S(2)}) collective-permute-start(f32[2,640,1]{1,0,2:T(2,128)S(1)} %reshape.539), channel_id=1, source_target_pairs={{0,8},{4,12},{8,16},{12,20},{16,24},{20,28},{24,0},{28,4},{1,9},{5... | collective-permute-start | bytes 15368 | tf_op jit(solution)/shard_map/ppermute | solution.py:37
  433.3 9.3 fusion.76
  456.6 6.3 collective-permute-done.35
  476.0 18.2 %multiply_reduce_fusion = (f32[12,512]{1,0:T(8,128)}, f32[12,512,1024]{2,1,0:T(8,128)}) fusion(f32[12,512,1024]{2,1,0:T(8,128)} %get-tuple-element.93, f32[12,512]{1,0:T(8,128)} %copy-done.72, pred[512,1024]{1,0:T(8,128)(4,1)} %copy-done.11, bf16[512,12,64]{0,2,1:T(8,128)(2,1)} %bitcast.326, bf16[1024,12,64]{0,2,1:T(8,128)(2,1)} %bitcast.329), kind=kOutput, calls=%fused_computation.1 | convolution fusion | flops 830466048 | bytes 53264384 | tf_op jit(solution)/shard_map/qhd,khd->hqk/dot_general | solution.py:74
  494.2 13.1 %fusion.78 = f32[12,64,1024]{2,1,0:T(8,128)} fusion(bf16[512,12,64]{0,2,1:T(8,128)(2,1)} %bitcast.327, f32[12,512,1024]{2,1,0:T(8,128)} %get-tuple-element.93, f32[12,512]{1,0:T(8,128)} %copy-done.72, pred[512,1024]{1,0:T(8,128)(4,1)} %copy-done.11), kind=kOutput, calls=%fused_computation.147 | convolution fusion | flops 824180736 | bytes 29646848 | tf_op jit(solution)/shard_map/hqk,qhd->khd/dot_general | solution.py:74
  507.3 21.8 %multiply_convert_fusion = bf16[12,512,1024]{2,1,0:T(8,128)(2,1)} fusion(f32[12,512,1024]{2,1,0:T(8,128)} %get-tuple-element.102, f32[12,512,1024]{2,1,0:T(8,128)} %get-tuple-element.93, f32[12,512]{1,0:T(8,128)S(1)} %copy-done.74, f32[12,512]{1,0:T(8,128)S(1)} %copy-done.73, pred[512,1024]{1,0:T(8,128)(4,1)S(1)} %copy-done.12), kind=kLoop, calls=%fused_computation | loop fusion | flops 31457280 | bytes 63488000 | tf_op jit(solution)/shard_map/convert_element_type | solution.py:306
  529.1 9.7 %multiply_bitcast_fusion = f32[512,12,64]{0,2,1:T(8,128)} fusion(bf16[1024,12,64]{0,2,1:T(8,128)(2,1)S(1)} %bitcast.319, bf16[12,512,1024]{2,1,0:T(8,128)(2,1)} %multiply_convert_fusion), kind=kOutput, calls=%fused_computation.141 | convolution fusion | flops 805699584 | bytes 15728640 | tf_op jit(solution)/shard_map/hqk,khd->qhd/dot_general | solution.py:74
  543.8 7.0 fusion.122
  571.0 17.5 %collective-permute-done.44 = bf16[768,1,192]{0,2,1:T(8,128)(2,1)S(1)} collective-permute-done((bf16[768,1,192]{0,2,1:T(8,128)(2,1)S(1)}, bf16[768,1,192]{0,2,1:T(8,128)(2,1)S(1)}, u32[]{:S(2)}, u32[]{:S(2)}) %collective-permute-start.44) | collective-permute-done | bytes 294944 | tf_op jit(solution)/shard_map/ppermute | solution.py:31
  610.4 74.8 %collective-permute-done.46 = bf16[2,96,192]{2,1,0:T(8,128)(2,1)S(1)} collective-permute-done((bf16[2,96,192]{2,1,0:T(8,128)(2,1)S(1)}, bf16[2,96,192]{2,1,0:T(8,128)(2,1)S(1)}, u32[]{:S(2)}, u32[]{:S(2)}) %collective-permute-start.46) | collective-permute-done | bytes 73760 | tf_op jit(solution)/shard_map/ppermute | solution.py:31
  693.5 9.3 fusion.72
  702.8 9.4 fusion.74
  712.2 20.0 %fusion.26 = f32[2,768,512]{2,1,0:T(8,128)} fusion(f32[2,2560,512]{2,1,0:T(8,128)} %fusion.72, f32[2,2560,512]{2,1,0:T(8,128)} %fusion.76, f32[2,2560,512]{2,1,0:T(8,128)} %fusion.74, bf16[2,640,768]{2,1,0:T(8,128)(2,1)} %collective-permute-done.50, bf16[2,640,768]{2,1,0:T(8,128)(2,1)} %collective-permute-done.49, ...), kind=kOutput, calls=%fused_computation.45 | convolution fusion | flops 4086824960 | bytes 42467328 | tf_op jit(solution)/shard_map/erd,erf->edf/dot_general | solution.py:74
  736.0 14.0 %fusion.22 = f32[2,512,768]{2,1,0:T(8,128)} fusion(f32[2,2560,512]{2,1,0:T(8,128)} %fusion.74, f32[2,2560,512]{2,1,0:T(8,128)} %fusion.72, bf16[2,640,768]{2,1,0:T(8,128)(2,1)} %collective-permute-done.56, bf16[2,640,768]{2,1,0:T(8,128)(2,1)} %collective-permute-done.55, bf16[2,640,768]{2,1,0:T(8,128)(2,1)} %collective-permute-done.54, ...), kind=kOutput, calls=%fused_computation.40 | convolution fusion | flops 4081582080 | bytes 32002048 | tf_op jit(solution)/shard_map/erf,erd->efd/dot_general | solution.py:74
  750.0 13.8 %fusion.21 = f32[2,768,512]{2,1,0:T(8,128)} fusion(f32[2,2560,512]{2,1,0:T(8,128)} %fusion.76, f32[2,2560,512]{2,1,0:T(8,128)} %fusion.72, bf16[2,640,768]{2,1,0:T(8,128)(2,1)} %collective-permute-done.50, bf16[2,640,768]{2,1,0:T(8,128)(2,1)} %collective-permute-done.49, bf16[2,640,768]{2,1,0:T(8,128)(2,1)} %collective-permute-done.48, ...), kind=kOutput, calls=%fused_computation.39 | convolution fusion | flops 4073717760 | bytes 31981568 | tf_op jit(solution)/shard_map/erd,erf->edf/dot_general | solution.py:74
  794.0 38.6 %all-reduce.7 = (f32[2,768]{1,0:T(2,128)}, f32[768,16]{0,1:T(8,128)}) all-reduce(f32[2,768]{1,0:T(2,128)S(1)} %pad_maximum_fusion.4, f32[768,16]{0,1:T(8,128)} %fusion.175), channel_id=1, replica_groups=mesh['group'=8,'expert'=4] {'group','expert'}, use_global_device_ids=true, to_apply=%region_19.20 | all-reduce | flops 13824 | bytes 110592 | tf_op jit(solution)/shard_map/psum | solution.py:326
  902.4 7.8 collective-permute-done.39
  (566 shorter events, 431.4 us)
Async XLA Ops:
  14.8 57.5 %collective-permute-start = (bf16[512,1536]{0,1:T(8,128)(2,1)}, bf16[512,1536]{0,1:T(8,128)(2,1)}, u32[]{:S(2)}, u32[]{:S(2)}) collective-permute-start(bf16[512,1536]{0,1:T(8,128)(2,1)} %pad_maximum_fusion.2), channel_id=1, source_target_pairs={{0,1},{1,2},{2,3},{4,5},{5,6},{6,7},{8,9},{9,10},{10,11},{12,13},{... | collective-permute-start | bytes 4718600 | tf_op jit(solution)/shard_map/ppermute | solution.py:21
  18.4 23.3 %collective-permute-start.1 = (bf16[512]{0:T(512)(128)(2,1)S(1)}, bf16[512]{0:T(512)(128)(2,1)}, u32[]{:S(2)}, u32[]{:S(2)}) collective-permute-start(bf16[512]{0:T(512)(128)(2,1)S(1)} %convert_element_type.368), channel_id=1, source_target_pairs={{0,1},{1,2},{2,3},{4,5},{5,6},{6,7},{8,9},{9,10},{10,11},{12,13},{... | collective-permute-start | bytes 3080 | tf_op jit(solution)/shard_map/ppermute | solution.py:21
  68.7 362.5 %collective-permute-start.56 = (bf16[2,640,768]{2,1,0:T(8,128)(2,1)}, bf16[2,640,768]{2,1,0:T(8,128)(2,1)}, u32[]{:S(2)}, u32[]{:S(2)}) collective-permute-start(bf16[2,640,768]{2,1,0:T(8,128)(2,1)} %bitcast.52), channel_id=1, source_target_pairs={{0,24},{4,28},{8,0},{12,4},{16,8},{20,12},{24,16},{28,20},{1,25},{... | collective-permute-start | bytes 5898248 | tf_op jit(solution)/shard_map/ppermute | solution.py:37
  258.0 15.7 %collective-permute-start.14 = (bf16[160,768]{1,0:T(8,128)(2,1)S(1)}, bf16[160,768]{1,0:T(8,128)(2,1)S(1)}, u32[]{:S(2)}, u32[]{:S(2)}) collective-permute-start(bf16[160,768]{1,0:T(8,128)(2,1)S(1)} %bitcast.380), channel_id=1, source_target_pairs={{0,6},{1,7},{2,4},{3,5},{4,2},{5,3},{6,0},{7,1},{8,14},{9,15},{10,... | collective-permute-start | bytes 737288 | tf_op jit(solution)/shard_map/ppermute | solution.py:31
  299.6 132.2 %collective-permute-start.55 = (bf16[2,640,768]{2,1,0:T(8,128)(2,1)}, bf16[2,640,768]{2,1,0:T(8,128)(2,1)}, u32[]{:S(2)}, u32[]{:S(2)}) collective-permute-start(bf16[2,640,768]{2,1,0:T(8,128)(2,1)} %bitcast.52), channel_id=1, source_target_pairs={{0,16},{4,20},{8,24},{12,28},{16,0},{20,4},{24,8},{28,12},{1,17},{... | collective-permute-start | bytes 5898248 | tf_op jit(solution)/shard_map/ppermute | solution.py:37
  301.5 131.7 %collective-permute-start.54 = (bf16[2,640,768]{2,1,0:T(8,128)(2,1)}, bf16[2,640,768]{2,1,0:T(8,128)(2,1)}, u32[]{:S(2)}, u32[]{:S(2)}) collective-permute-start(bf16[2,640,768]{2,1,0:T(8,128)(2,1)} %bitcast.52), channel_id=1, source_target_pairs={{0,8},{4,12},{8,16},{12,20},{16,24},{20,28},{24,0},{28,4},{1,9},{5... | collective-permute-start | bytes 5898248 | tf_op jit(solution)/shard_map/ppermute | solution.py:37
  310.3 75.0 %collective-permute-start.53 = (f32[2,640,1]{1,0,2:T(2,128)S(1)}, f32[2,640,1]{1,0,2:T(2,128)S(1)}, u32[]{:S(2)}, u32[]{:S(2)}) collective-permute-start(f32[2,640,1]{1,0,2:T(2,128)S(1)} %reshape.539), channel_id=1, source_target_pairs={{0,24},{4,28},{8,0},{12,4},{16,8},{20,12},{24,16},{28,20},{1,25},{... | collective-permute-start | bytes 15368 | tf_op jit(solution)/shard_map/ppermute | solution.py:37
  313.1 116.0 %collective-permute-start.52 = (f32[2,640,1]{1,0,2:T(2,128)S(1)}, f32[2,640,1]{1,0,2:T(2,128)}, u32[]{:S(2)}, u32[]{:S(2)}) collective-permute-start(f32[2,640,1]{1,0,2:T(2,128)S(1)} %reshape.539), channel_id=1, source_target_pairs={{0,16},{4,20},{8,24},{12,28},{16,0},{20,4},{24,8},{28,12},{1,17},{... | collective-permute-start | bytes 15368 | tf_op jit(solution)/shard_map/ppermute | solution.py:37
  385.3 45.2 %collective-permute-start.51 = (f32[2,640,1]{1,0,2:T(2,128)S(1)}, f32[2,640,1]{1,0,2:T(2,128)S(1)}, u32[]{:S(2)}, u32[]{:S(2)}) collective-permute-start(f32[2,640,1]{1,0,2:T(2,128)S(1)} %reshape.539), channel_id=1, source_target_pairs={{0,8},{4,12},{8,16},{12,20},{16,24},{20,28},{24,0},{28,4},{1,9},{5... | collective-permute-start | bytes 15368 | tf_op jit(solution)/shard_map/ppermute | solution.py:37
  429.1 125.8 %collective-permute-start.60 = (bf16[768,2,512]{2,0,1:T(8,128)(2,1)}, bf16[768,2,512]{2,0,1:T(8,128)(2,1)}, u32[]{:S(2)}, u32[]{:S(2)}) collective-permute-start(bf16[768,2,512]{2,0,1:T(8,128)(2,1)} %bitcast.307), channel_id=1, source_target_pairs={{0,1},{1,0},{2,3},{3,2},{4,5},{5,4},{6,7},{7,6},{8,9},{9,8},{10,11... | collective-permute-start | bytes 4718600 | tf_op jit(solution)/shard_map/ppermute | solution.py:31
  430.4 134.3 %collective-permute-start.65 = (bf16[768,2,512]{2,0,1:T(8,128)(2,1)}, bf16[768,2,512]{2,0,1:T(8,128)(2,1)}, u32[]{:S(2)}, u32[]{:S(2)}) collective-permute-start(bf16[768,2,512]{2,0,1:T(8,128)(2,1)} %bitcast.308), channel_id=1, source_target_pairs={{0,1},{1,0},{2,3},{3,2},{4,5},{5,4},{6,7},{7,6},{8,9},{9,8},{10,11... | collective-permute-start | bytes 4718600 | tf_op jit(solution)/shard_map/ppermute | solution.py:31
  444.8 18.1 %collective-permute-start.35 = (bf16[160,768]{1,0:T(8,128)(2,1)S(1)}, bf16[160,768]{1,0:T(8,128)(2,1)S(1)}, u32[]{:S(2)}, u32[]{:S(2)}) collective-permute-start(bf16[160,768]{1,0:T(8,128)(2,1)S(1)} %bitcast.375), channel_id=1, source_target_pairs={{0,6},{1,7},{2,4},{3,5},{4,2},{5,3},{6,0},{7,1},{8,14},{9,15},{10,... | collective-permute-start | bytes 737288 | tf_op jit(solution)/shard_map/ppermute | solution.py:31
  451.4 16.2 %collective-permute-start.36 = (bf16[160,768]{1,0:T(8,128)(2,1)S(1)}, bf16[160,768]{1,0:T(8,128)(2,1)S(1)}, u32[]{:S(2)}, u32[]{:S(2)}) collective-permute-start(bf16[160,768]{1,0:T(8,128)(2,1)S(1)} %bitcast.374), channel_id=1, source_target_pairs={{0,7},{1,6},{2,5},{3,4},{4,3},{5,2},{6,1},{7,0},{8,15},{9,14},{10,... | collective-permute-start | bytes 737288 | tf_op jit(solution)/shard_map/ppermute | solution.py:31
  456.2 103.4 %collective-permute-start.70 = (bf16[2048,2,192]{0,2,1:T(8,128)(2,1)}, bf16[2048,2,192]{0,2,1:T(8,128)(2,1)}, u32[]{:S(2)}, u32[]{:S(2)}) collective-permute-start(bf16[2048,2,192]{0,2,1:T(8,128)(2,1)} %fusion.64), channel_id=1, source_target_pairs={{0,1},{1,0},{2,3},{3,2},{4,5},{5,4},{6,7},{7,6},{8,9},{9,8},{10,11... | collective-permute-start | bytes 4718600 | tf_op jit(solution)/shard_map/ppermute | solution.py:31
  462.9 228.5 %collective-permute-start.50 = (bf16[2,640,768]{2,1,0:T(8,128)(2,1)}, bf16[2,640,768]{2,1,0:T(8,128)(2,1)}, u32[]{:S(2)}, u32[]{:S(2)}) collective-permute-start(bf16[2,640,768]{2,1,0:T(8,128)(2,1)} %bitcast.20), channel_id=1, source_target_pairs={{0,24},{4,28},{8,0},{12,4},{16,8},{20,12},{24,16},{28,20},{1,25},{... | collective-permute-start | bytes 5898248 | tf_op jit(solution)/shard_map/ppermute | solution.py:37
  552.9 140.0 %collective-permute-start.49 = (bf16[2,640,768]{2,1,0:T(8,128)(2,1)}, bf16[2,640,768]{2,1,0:T(8,128)(2,1)}, u32[]{:S(2)}, u32[]{:S(2)}) collective-permute-start(bf16[2,640,768]{2,1,0:T(8,128)(2,1)} %bitcast.20), channel_id=1, source_target_pairs={{0,16},{4,20},{8,24},{12,28},{16,0},{20,4},{24,8},{28,12},{1,17},{... | collective-permute-start | bytes 5898248 | tf_op jit(solution)/shard_map/ppermute | solution.py:37
  554.9 138.6 %collective-permute-start.48 = (bf16[2,640,768]{2,1,0:T(8,128)(2,1)}, bf16[2,640,768]{2,1,0:T(8,128)(2,1)}, u32[]{:S(2)}, u32[]{:S(2)}) collective-permute-start(bf16[2,640,768]{2,1,0:T(8,128)(2,1)} %bitcast.20), channel_id=1, source_target_pairs={{0,8},{4,12},{8,16},{12,20},{16,24},{20,28},{24,0},{28,4},{1,9},{5... | collective-permute-start | bytes 5898248 | tf_op jit(solution)/shard_map/ppermute | solution.py:37
  559.6 216.9 %collective-permute-start.37 = (bf16[512,1536]{0,1:T(8,128)(2,1)}, bf16[512,1536]{0,1:T(8,128)(2,1)}, u32[]{:S(2)}, u32[]{:S(2)}) collective-permute-start(bf16[512,1536]{0,1:T(8,128)(2,1)} %fusion.35), channel_id=1, source_target_pairs={{1,0},{2,1},{3,2},{5,4},{6,5},{7,6},{9,8},{10,9},{11,10},{13,12},{... | collective-permute-start | bytes 4718600 | tf_op jit(solution)/shard_map/ppermute | solution.py:21
  564.7 23.8 %collective-permute-start.44 = (bf16[768,1,192]{0,2,1:T(8,128)(2,1)S(1)}, bf16[768,1,192]{0,2,1:T(8,128)(2,1)S(1)}, u32[]{:S(2)}, u32[]{:S(2)}) collective-permute-start(bf16[768,1,192]{0,2,1:T(8,128)(2,1)S(1)} %dynamic-slice_convert_fusion.11), channel_id=1, source_target_pairs={{0,2},{1,3},{2,0},{3,1},{4,6},{5,7},{6,4},{7,5},{8,10},{9,11},{10,... | collective-permute-start | bytes 884744 | tf_op jit(solution)/shard_map/ppermute | solution.py:31
  605.6 79.6 %collective-permute-start.46 = (bf16[2,96,192]{2,1,0:T(8,128)(2,1)S(1)}, bf16[2,96,192]{2,1,0:T(8,128)(2,1)S(1)}, u32[]{:S(2)}, u32[]{:S(2)}) collective-permute-start(bf16[2,96,192]{2,1,0:T(8,128)(2,1)S(1)} %fusion.117), channel_id=1, source_target_pairs={{0,8},{1,9},{2,10},{3,11},{4,12},{5,13},{6,14},{7,15},{8,0},{9,1},... | collective-permute-start | bytes 221192 | tf_op jit(solution)/shard_map/ppermute | solution.py:31
  690.3 150.4 %collective-permute-start.61 = (bf16[768,1,512]{2,0,1:T(8,128)(2,1)}, bf16[768,1,512]{2,0,1:T(8,128)(2,1)}, u32[]{:S(2)}, u32[]{:S(2)}) collective-permute-start(bf16[768,1,512]{2,0,1:T(8,128)(2,1)} %dynamic-slice_convert_fusion.4), channel_id=1, source_target_pairs={{0,2},{1,3},{2,0},{3,1},{4,6},{5,7},{6,4},{7,5},{8,10},{9,11},{10,... | collective-permute-start | bytes 2359304 | tf_op jit(solution)/shard_map/ppermute | solution.py:31
  691.4 151.6 %collective-permute-start.66 = (bf16[768,1,512]{2,0,1:T(8,128)(2,1)}, bf16[768,1,512]{2,0,1:T(8,128)(2,1)}, u32[]{:S(2)}, u32[]{:S(2)}) collective-permute-start(bf16[768,1,512]{2,0,1:T(8,128)(2,1)} %dynamic-slice_convert_fusion.3), channel_id=1, source_target_pairs={{0,2},{1,3},{2,0},{3,1},{4,6},{5,7},{6,4},{7,5},{8,10},{9,11},{10,... | collective-permute-start | bytes 2359304 | tf_op jit(solution)/shard_map/ppermute | solution.py:31
  692.9 155.8 %collective-permute-start.71 = (bf16[2048,1,192]{0,2,1:T(8,128)(2,1)}, bf16[2048,1,192]{0,2,1:T(8,128)(2,1)}, u32[]{:S(2)}, u32[]{:S(2)}) collective-permute-start(bf16[2048,1,192]{0,2,1:T(8,128)(2,1)} %dynamic-slice_convert_fusion.2), channel_id=1, source_target_pairs={{0,2},{1,3},{2,0},{3,1},{4,6},{5,7},{6,4},{7,5},{8,10},{9,11},{10,... | collective-permute-start | bytes 2359304 | tf_op jit(solution)/shard_map/ppermute | solution.py:31
  734.5 160.1 %collective-permute-start.57 = (bf16[2,768,256]{2,1,0:T(8,128)(2,1)}, bf16[2,768,256]{2,1,0:T(8,128)(2,1)}, u32[]{:S(2)}, u32[]{:S(2)}) collective-permute-start(bf16[2,768,256]{2,1,0:T(8,128)(2,1)} %dynamic-slice_convert_fusion.7), channel_id=1, source_target_pairs={{0,4},{1,5},{2,6},{3,7},{4,0},{5,1},{6,2},{7,3},{8,12},{9,13},{10,... | collective-permute-start | bytes 2359304 | tf_op jit(solution)/shard_map/ppermute | solution.py:31
  778.2 120.8 %collective-permute-start.58 = (bf16[2,768,256]{2,1,0:T(8,128)(2,1)}, bf16[2,768,256]{2,1,0:T(8,128)(2,1)}, u32[]{:S(2)}, u32[]{:S(2)}) collective-permute-start(bf16[2,768,256]{2,1,0:T(8,128)(2,1)} %dynamic-slice_convert_fusion.6), channel_id=1, source_target_pairs={{0,4},{1,5},{2,6},{3,7},{4,0},{5,1},{6,2},{7,3},{8,12},{9,13},{10,... | collective-permute-start | bytes 2359304 | tf_op jit(solution)/shard_map/ppermute | solution.py:31
  840.6 47.0 %collective-permute-start.38 = (bf16[768,2,576]{0,2,1:T(8,128)(2,1)}, bf16[768,2,576]{0,2,1:T(8,128)(2,1)}, u32[]{:S(2)}, u32[]{:S(2)}) collective-permute-start(bf16[768,2,576]{0,2,1:T(8,128)(2,1)} %fusion.55), channel_id=1, source_target_pairs={{0,1},{1,0},{2,3},{3,2},{4,5},{5,4},{6,7},{7,6},{8,9},{9,8},{10,11... | collective-permute-start | bytes 5308424 | tf_op jit(solution)/shard_map/ppermute | solution.py:31
  843.1 16.9 %collective-permute-start.62 = (bf16[4,96,512]{2,1,0:T(8,128)(2,1)}, bf16[4,96,512]{2,1,0:T(8,128)(2,1)}, u32[]{:S(2)}, u32[]{:S(2)}) collective-permute-start(bf16[4,96,512]{2,1,0:T(8,128)(2,1)} %fusion.92), channel_id=1, source_target_pairs={{0,4},{1,5},{2,6},{3,7},{4,0},{5,1},{6,2},{7,3},{8,12},{9,13},{10,... | collective-permute-start | bytes 1179656 | tf_op jit(solution)/shard_map/ppermute | solution.py:31
  864.0 52.7 %collective-permute-start.59 = (bf16[2,256,768]{2,1,0:T(8,128)(2,1)}, bf16[2,256,768]{2,1,0:T(8,128)(2,1)}, u32[]{:S(2)}, u32[]{:S(2)}) collective-permute-start(bf16[2,256,768]{2,1,0:T(8,128)(2,1)} %dynamic-slice_convert_fusion.5), channel_id=1, source_target_pairs={{0,4},{1,5},{2,6},{3,7},{4,0},{5,1},{6,2},{7,3},{8,12},{9,13},{10,... | collective-permute-start | bytes 2359304 | tf_op jit(solution)/shard_map/ppermute | solution.py:31
  887.7 31.3 %collective-permute-start.64 = (bf16[1,96,512]{2,1,0:T(8,128)(2,1)}, bf16[1,96,512]{2,1,0:T(8,128)(2,1)}, u32[]{:S(2)}, u32[]{:S(2)}) collective-permute-start(bf16[1,96,512]{2,1,0:T(8,128)(2,1)} %dynamic-slice_convert_fusion.19), channel_id=1, source_target_pairs={{0,16},{1,17},{2,18},{3,19},{4,20},{5,21},{6,22},{7,23},{8,24},{9,... | collective-permute-start | bytes 294920 | tf_op jit(solution)/shard_map/ppermute | solution.py:31
  892.0 18.1 %collective-permute-start.39 = (bf16[768,1,576]{0,2,1:T(8,128)(2,1)S(1)}, bf16[768,1,576]{0,2,1:T(8,128)(2,1)S(1)}, u32[]{:S(2)}, u32[]{:S(2)}) collective-permute-start(bf16[768,1,576]{0,2,1:T(8,128)(2,1)S(1)} %dynamic-slice_convert_fusion.1), channel_id=1, source_target_pairs={{0,2},{1,3},{2,0},{3,1},{4,6},{5,7},{6,4},{7,5},{8,10},{9,11},{10,... | collective-permute-start | bytes 2654216 | tf_op jit(solution)/shard_map/ppermute | solution.py:31
  894.7 32.8 %collective-permute-start.69 = (bf16[1,96,512]{2,1,0:T(8,128)(2,1)}, bf16[1,96,512]{2,1,0:T(8,128)(2,1)}, u32[]{:S(2)}, u32[]{:S(2)}) collective-permute-start(bf16[1,96,512]{2,1,0:T(8,128)(2,1)} %dynamic-slice_convert_fusion.18), channel_id=1, source_target_pairs={{0,16},{1,17},{2,18},{3,19},{4,20},{5,21},{6,22},{7,23},{8,24},{9,... | collective-permute-start | bytes 294920 | tf_op jit(solution)/shard_map/ppermute | solution.py:31
  898.9 36.9 %collective-permute-start.74 = (bf16[1,256,192]{1,2,0:T(8,128)(2,1)}, bf16[1,256,192]{1,2,0:T(8,128)(2,1)}, u32[]{:S(2)}, u32[]{:S(2)}) collective-permute-start(bf16[1,256,192]{1,2,0:T(8,128)(2,1)} %dynamic-slice_convert_fusion.17), channel_id=1, source_target_pairs={{0,16},{1,17},{2,18},{3,19},{4,20},{5,21},{6,22},{7,23},{8,24},{9,... | collective-permute-start | bytes 294920 | tf_op jit(solution)/shard_map/ppermute | solution.py:31
  (146 other events, 1327.8 us)

commit v2 on v0

v2 whole, which is shorter than its diff:
```python
import functools

import jax
import jax.numpy as jnp
from jax import lax
from jax.experimental import pallas as pl
from jax.experimental.pallas import tpu as pltpu
from jax.sharding import PartitionSpec as P

HEADS = 12
HEAD = 64
EXPERTS = 16
WINDOW = 1024
CAP = 80
QUARTERS = 4
LANES = 128
TILE = 256
NEG = -1e30

epsilon = 1e-06
F32 = jnp.float32
BF16 = jnp.bfloat16
MESH = pl.DeviceIdType.MESH
VMEM = pl.BlockSpec(memory_space=pltpu.VMEM)
ANY = pl.BlockSpec(memory_space=pl.ANY)
MIB = 1 << 20


def dims(spec):
    left, right = spec
    return (((left,), (right,)), ((), ()))


NN = dims((1, 0))
NT = dims((1, 1))
TN = dims((0, 0))


def mm(a, b, how=NN):
    return lax.dot_general(a, b, how, preferred_element_type=F32)


def flipped(x, mask):
    bit = 1
    while bit <= mask:
        if mask & bit:
            x = x + bit * (1 - 2 * ((x // bit) % 2))
        bit *= 2
    return x


class Layout:
    def __init__(self, groups, experts, rows):
        self.groups, self.experts, self.rows = groups, experts, rows
        self.share = EXPERTS // experts
        self.peers = self.share * experts
        self.outers = groups // self.share
        per_quarter = max(experts // QUARTERS, 1)
        self.reach = min((WINDOW - 1) // rows + 1, 2 * per_quarter - 1)

    def peer(self, number):
        group, expert = lax.axis_index("group"), lax.axis_index("expert")
        return {
            "group": flipped(group, number // self.experts),
            "expert": flipped(expert, number % self.experts),
        }


def meet(layout):
    barrier = pltpu.get_barrier_semaphore()
    for number in range(1, layout.peers):
        pl.semaphore_signal(barrier, inc=1, device_id=layout.peer(number), device_id_type=MESH)
    pl.semaphore_wait(barrier, layout.peers - 1)


def to_peers(layout, source, target, send_sems, recv_sems):
    return [
        pltpu.make_async_remote_copy(
            src_ref=source.at[number],
            dst_ref=target.at[number],
            send_sem=send_sems.at[number],
            recv_sem=recv_sems.at[number],
            device_id=layout.peer(number),
            device_id_type=MESH,
        )
        for number in range(1, layout.peers)
    ]


def rope_turn(x, cosine, sine):
    parts = []
    for begin in range(0, x.shape[1], LANES):
        part = x[:, begin : begin + LANES]
        lane = lax.broadcasted_iota(jnp.int32, part.shape, 1)
        other = jnp.where(
            lane % HEAD < HEAD // 2,
            pltpu.roll(part, LANES - HEAD // 2, 1),
            pltpu.roll(part, HEAD // 2, 1),
        )
        parts.append(part * cosine + other * sine)
    return jnp.concatenate(parts, axis=1)


def normed(x, gain):
    return x * lax.rsqrt(jnp.mean(x * x, axis=-1, keepdims=True) + epsilon) * gain


def slot_rows(ids_row, rows):
    labels = lax.broadcasted_iota(jnp.int32, (EXPERTS, rows), 0)
    first, second = labels == ids_row[0:1], labels == ids_row[1:2]
    both = jnp.where(first | second, 1.0, 0.0).astype(BF16)
    earlier_t = lax.broadcasted_iota(jnp.int32, (rows, rows), 0)
    later_t = lax.broadcasted_iota(jnp.int32, (rows, rows), 1)
    earlier = mm(both, jnp.where(earlier_t < later_t, 1.0, 0.0).astype(BF16))
    targets = []
    for mask, ids in ((first, ids_row[0:1]), (second, ids_row[1:2])):
        slot = jnp.sum(jnp.where(mask, earlier, 0.0), axis=0, keepdims=True).astype(jnp.int32)
        targets.append(jnp.where(slot < CAP, ids * CAP + slot, -1))
    return targets


def front_kernel(
    layout,
    tokens,
    gain,
    w_qkv,
    cosine,
    sine,
    ids_row,
    seg_row,
    cot,
    q_out,
    kv_out,
    att_out,
    att_t_out,
    lse_out,
    bias_out,
    target_out,
    cots_out,
    normed_low,
    send_cot,
    seg_all,
    acc,
    top,
    total,
    kv_send,
    kv_recv,
    seg_send,
    seg_recv,
    cot_send,
    cot_recv,
    own_sem,
):
    rows, width = tokens.shape
    reach, experts = layout.reach, layout.experts
    e = lax.axis_index("expert")

    x = tokens[...].astype(F32)
    normed_low[...] = normed(x, gain[...]).astype(BF16)
    seg_all[0] = seg_row[...]

    def project(step, carry):
        for part in range(3):
            columns = pl.ds(pl.multiple_of(part * width + step * TILE, TILE), TILE)
            made = mm(normed_low[...], w_qkv[:, columns])
            columns = pl.ds(pl.multiple_of(step * TILE, TILE), TILE)
            if part == 0:
                made = rope_turn(made, cosine[...], sine[...]) * HEAD ** (-0.5)
                q_out[:, columns] = made.astype(BF16)
            elif part == 1:
                made = rope_turn(made, cosine[...], sine[...])
                kv_out[0, :, columns] = made.astype(BF16)
            else:
                columns = pl.ds(pl.multiple_of(width + step * TILE, TILE), TILE)
                kv_out[0, :, columns] = made.astype(BF16)
        return carry

    lax.fori_loop(0, width // TILE, project, 0)

    meet(layout)
    halos = []
    for distance in range(1, reach + 1):
        to = {"expert": lax.rem(e + distance, experts)}
        halos.append(
            (
                pltpu.make_async_remote_copy(
                    src_ref=kv_out.at[0],
                    dst_ref=kv_out.at[distance],
                    send_sem=kv_send.at[distance],
                    recv_sem=kv_recv.at[distance],
                    device_id=to,
                    device_id_type=MESH,
                ),
                pltpu.make_async_remote_copy(
                    src_ref=seg_all.at[0],
                    dst_ref=seg_all.at[distance],
                    send_sem=seg_send.at[distance],
                    recv_sem=seg_recv.at[distance],
                    device_id=to,
                    device_id_type=MESH,
                ),
            )
        )
        for copy in halos[-1]:
            copy.start()

    targets = slot_rows(ids_row[...], rows)
    target_out[0:1] = targets[0]
    target_out[1:2] = targets[1]
    target_out[2:8] = jnp.full((6, rows), -1, jnp.int32)
    for number in range(layout.peers):
        slots = number * CAP + lax.broadcasted_iota(jnp.int32, (CAP, rows), 0)
        chosen = (slots == targets[0]) | (slots == targets[1])
        send_cot[number] = mm(jnp.where(chosen, 1.0, 0.0).astype(BF16), cot[...]).astype(BF16)
    sends = to_peers(layout, send_cot, cots_out, cot_send, cot_recv)
    for copy in sends:
        copy.start()
    own = pltpu.make_async_copy(send_cot.at[0], cots_out.at[0], own_sem)
    own.start()

    lane = lax.broadcasted_iota(jnp.int32, (rows, LANES), 1)
    for distance in range(reach + 1):
        if distance:
            for copy in halos[distance - 1]:
                copy.wait()
        seg_col = jnp.transpose(jnp.broadcast_to(seg_all[distance, 0:1], (LANES, rows)))[:, 0:1]
        key_no = lax.broadcasted_iota(jnp.int32, (rows, rows), 0) - distance * rows
        offset = lax.broadcasted_iota(jnp.int32, (rows, rows), 1) - key_no
        allowed = (
            (offset >= 0)
            & (offset < WINDOW)
            & (key_no + e * rows >= 0)
            & (seg_col == seg_all[0, 0:1])
        )
        bias_out[distance] = jnp.where(allowed, 0.0, NEG)

        def attend(pair, carry, distance=distance):
            columns = pl.ds(pl.multiple_of(pair * LANES, LANES), LANES)
            value_columns = pl.ds(pl.multiple_of(width + pair * LANES, LANES), LANES)
            queries = q_out[:, columns]
            keys = kv_out[distance, :, columns]
            values_t = jnp.transpose(kv_out[distance, :, value_columns])
            for inner in range(2):
                head = pair * 2 + inner
                mine = jnp.where((lane // HEAD) == inner, queries, jnp.zeros_like(queries))
                value_t = values_t[inner * HEAD : (inner + 1) * HEAD]
                out_rows = pl.ds(pl.multiple_of(head * HEAD, HEAD), HEAD)
                blocks = (
                    [(slice(0, rows // 2), rows // 2), (slice(rows // 2, rows), rows)]
                    if distance == 0
                    else [(slice(0, rows), rows)]
                )
                for q_cut, key_count in blocks:
                    scores = mm(keys[:key_count], mine[q_cut], NT)
                    scores = scores + bias_out[distance, :key_count, q_cut]
                    peak = jnp.max(scores, axis=0, keepdims=True)
                    if distance:
                        before = top[pl.ds(head, 1), q_cut]
                        peak = jnp.maximum(before, peak)
                    weights = jnp.exp(scores - peak)
                    amount = jnp.sum(weights, axis=0, keepdims=True)
                    part = mm(value_t[:, :key_count], weights.astype(BF16))
                    if distance:
                        shrink = jnp.exp(before - peak)
                        amount = amount + total[pl.ds(head, 1), q_cut] * shrink
                        part = part + acc[out_rows, q_cut] * shrink
                    top[pl.ds(head, 1), q_cut] = peak
                    total[pl.ds(head, 1), q_cut] = amount
                    acc[out_rows, q_cut] = part
            return carry

        lax.fori_loop(0, HEADS // 2, attend, 0)

    lse_out[...] = top[...] + jnp.log(total[...])

    def finish(pair, carry):
        out_rows = pl.ds(pl.multiple_of(pair * LANES, LANES), LANES)
        scale = jnp.concatenate(
            [
                jnp.broadcast_to(1.0 / total[pl.ds(pair * 2 + inner, 1), :], (HEAD, rows))
                for inner in range(2)
            ],
            axis=0,
        )
        made = acc[out_rows, :] * scale
        att_t_out[out_rows, :] = made.astype(BF16)
        att_out[:, out_rows] = jnp.transpose(made).astype(BF16)
        return carry

    lax.fori_loop(0, HEADS // 2, finish, 0)
    own.wait()
    for copy in sends:
        copy.wait()


def front(layout, tokens, gain, w_qkv, cosine, sine, ids_row, seg_row, cot):
    rows, width = tokens.shape
    reach, peers = layout.reach, layout.peers
    dma = pltpu.SemaphoreType.DMA
    return pl.pallas_call(
        functools.partial(front_kernel, layout),
        out_shape=[
            jax.ShapeDtypeStruct((rows, width), BF16),
            jax.ShapeDtypeStruct((reach + 1, rows, 2 * width), BF16),
            jax.ShapeDtypeStruct((rows, width), BF16),
            jax.ShapeDtypeStruct((width, rows), BF16),
            jax.ShapeDtypeStruct((EXPERTS, rows), F32),
            jax.ShapeDtypeStruct((reach + 1, rows, rows), F32),
            jax.ShapeDtypeStruct((8, rows), jnp.int32),
            jax.ShapeDtypeStruct((peers, CAP, width), BF16),
        ],
        in_specs=[VMEM] * 8,
        out_specs=[VMEM] * 7 + [ANY],
        scratch_shapes=[
            pltpu.VMEM((rows, width), BF16),
            pltpu.VMEM((peers, CAP, width), BF16),
            pltpu.VMEM((reach + 1, 8, rows), F32),
            pltpu.VMEM((width, rows), F32),
            pltpu.VMEM((EXPERTS, rows), F32),
            pltpu.VMEM((EXPERTS, rows), F32),
            dma((reach + 1,)),
            dma((reach + 1,)),
            dma((reach + 1,)),
            dma((reach + 1,)),
            dma((peers,)),
            dma((peers,)),
            dma,
        ],
        compiler_params=pltpu.CompilerParams(
            collective_id=0, has_side_effects=True, vmem_limit_bytes=56 * MIB
        ),
        cost_estimate=pl.CostEstimate(flops=1 << 30, bytes_accessed=1 << 20, transcendentals=0),
        name="front",
    )(tokens, gain, w_qkv, cosine, sine, ids_row, seg_row, cot)


def split3(x):
    high = x.astype(BF16)
    rest = x - high.astype(F32)
    middle = rest.astype(BF16)
    return high, middle, (rest - middle.astype(F32)).astype(BF16)


def silu_parts(gate_pre):
    gate = 1.0 / (1.0 + jnp.exp(-gate_pre))
    return gate_pre * gate, gate * (1.0 + gate_pre * (1.0 - gate))


def middle_kernel(
    layout,
    att,
    tokens,
    w_out,
    gain,
    w_router_t,
    ids_row,
    target_row,
    cot,
    dense_gate,
    dense_up,
    dense_down,
    hidden_out,
    low_out,
    mixed_out,
    grad_out,
    gate_out,
    up_out,
    down_out,
    rows_out,
    shares_out,
    send_rows,
    send_shares,
    low_t,
    row_send,
    row_recv,
    share_send,
    share_recv,
    own_sems,
):
    rows, width = tokens.shape
    ff = dense_gate.shape[1]
    experts = layout.experts
    hidden_out[...] = tokens[...].astype(F32) + mm(att[...], w_out[...])
    low = normed(hidden_out[...], gain[...]).astype(BF16)
    low_out[...] = low
    logits = mm(w_router_t[...], low, NT)
    route = jnp.exp(logits - jnp.max(logits, axis=0, keepdims=True))
    route = route / jnp.sum(route, axis=0, keepdims=True)
    labels = lax.broadcasted_iota(jnp.int32, (EXPERTS, rows), 0)
    picked = [
        jnp.sum(jnp.where(labels == ids_row[k : k + 1], route, 0.0), axis=0, keepdims=True)
        for k in range(2)
    ]
    both = picked[0] + picked[1]
    shares = []
    for k in range(2):
        parts = split3(picked[k] / both)
        shares.append(
            jnp.concatenate(
                [part.astype(F32) for part in parts] + [jnp.zeros((5, rows), F32)], axis=0
            ).astype(BF16)
        )
    send_shares[...] = jnp.zeros_like(send_shares)
    for number in range(layout.peers):
        slots = number * CAP + lax.broadcasted_iota(jnp.int32, (CAP, rows), 0)
        first = jnp.where(slots == target_row[0:1], 1.0, 0.0).astype(BF16)
        second = jnp.where(slots == target_row[1:2], 1.0, 0.0).astype(BF16)
        send_rows[number] = mm(first + second, low).astype(BF16)
        share = mm(shares[0], first, NT) + mm(shares[1], second, NT)
        share = jnp.sum(share, axis=0, keepdims=True)
        send_shares[number, :, :CAP] = jnp.broadcast_to(share, (8, CAP))

    meet(layout)
    sends = to_peers(layout, send_rows, rows_out, row_send, row_recv)
    sends += to_peers(layout, send_shares, shares_out, share_send, share_recv)
    sends.append(pltpu.make_async_copy(send_rows.at[0], rows_out.at[0], own_sems.at[0]))
    sends.append(pltpu.make_async_copy(send_shares.at[0], shares_out.at[0], own_sems.at[1]))
    for copy in sends:
        copy.start()

    low_t[...] = jnp.transpose(low)
    mixed_out[...] = hidden_out[...]
    grad_out[...] = jnp.zeros_like(grad_out)
    part_width = ff // experts
    per_part = part_width // TILE

    def branch(step, carry):
        columns = pl.ds(pl.multiple_of(step * TILE, TILE), TILE)
        gate_w, up_w, down_w = dense_gate[:, columns], dense_up[:, columns], dense_down[columns, :]
        gate_pre = mm(low_out[...], gate_w)
        up_pre = mm(low_out[...], up_w)
        grad_act = mm(cot[...], down_w, NT)
        silu, slope = silu_parts(gate_pre)
        act = (silu * up_pre).astype(BF16)
        grad_gate = (grad_act * up_pre * slope).astype(BF16)
        grad_up = (grad_act * silu).astype(BF16)
        mixed_out[...] += mm(act, down_w)
        grad_out[...] += mm(grad_gate, gate_w, NT) + mm(grad_up, up_w, NT)
        inside = pl.ds(pl.multiple_of((step % per_part) * TILE, TILE), TILE)
        gate_out[step // per_part, :, inside] = mm(low_t[...], grad_gate).astype(BF16)
        up_out[step // per_part, :, inside] = mm(low_t[...], grad_up).astype(BF16)
        made = mm(act, cot[...], TN).astype(BF16)
        for part in range(experts):
            cut = width // experts
            down_out[part, columns, :] = made[:, part * cut : (part + 1) * cut]
        return carry

    lax.fori_loop(0, ff // TILE, branch, 0)
    for copy in sends:
        copy.wait()


def middle(layout, att, tokens, w_out, gain, w_router_t, ids_row, target_row, cot, dense_gate, dense_up, dense_down):
    rows, width = tokens.shape
    ff = dense_gate.shape[1]
    peers, experts = layout.peers, layout.experts
    dma = pltpu.SemaphoreType.DMA
    return pl.pallas_call(
        functools.partial(middle_kernel, layout),
        out_shape=[
            jax.ShapeDtypeStruct((rows, width), F32),
            jax.ShapeDtypeStruct((rows, width), BF16),
            jax.ShapeDtypeStruct((rows, width), F32),
            jax.ShapeDtypeStruct((rows, width), F32),
            jax.ShapeDtypeStruct((experts, width, ff // experts), BF16),
            jax.ShapeDtypeStruct((experts, width, ff // experts), BF16),
            jax.ShapeDtypeStruct((experts, ff, width // experts), BF16),
            jax.ShapeDtypeStruct((peers, CAP, width), BF16),
            jax.ShapeDtypeStruct((peers, 8, LANES), F32),
        ],
        in_specs=[VMEM] * 11,
        out_specs=[VMEM] * 7 + [ANY, ANY],
        scratch_shapes=[
            pltpu.VMEM((peers, CAP, width), BF16),
            pltpu.VMEM((peers, 8, LANES), F32),
            pltpu.VMEM((width, rows), BF16),
            dma((peers,)),
            dma((peers,)),
            dma((peers,)),
            dma((peers,)),
            dma((2,)),
        ],
        compiler_params=pltpu.CompilerParams(
            collective_id=1, has_side_effects=True, vmem_limit_bytes=56 * MIB
        ),
        cost_estimate=pl.CostEstimate(flops=1 << 30, bytes_accessed=1 << 20, transcendentals=0),
        name="middle",
    )(att, tokens, w_out, gain, w_router_t, ids_row, target_row, cot, dense_gate, dense_up, dense_down)


def share_column(share_row):
    across = lax.broadcasted_iota(jnp.int32, (CAP, CAP), 1)
    down = lax.broadcasted_iota(jnp.int32, (CAP, CAP), 0)
    return jnp.sum(jnp.where(across == down, share_row, 0.0), axis=1, keepdims=True)


def own_share(layout):
    return lax.rem(lax.axis_index("group"), layout.share)


def experts_kernel(
    layout,
    rows_in,
    cots,
    shares,
    gate_any,
    up_any,
    down_any,
    back_out,
    grad_back,
    gate_w,
    up_w,
    down_w,
    scaled,
    acc,
    grad_acc,
    send_out,
    send_grad,
    load_sems,
    out_send,
    out_recv,
    grad_send,
    grad_recv,
    own_sems,
):
    peers = layout.peers
    width, ff = gate_w.shape
    mine = own_share(layout)
    loads = [
        pltpu.make_async_copy(source.at[mine], target, load_sems.at[number])
        for number, (source, target) in enumerate(
            ((gate_any, gate_w), (up_any, up_w), (down_any, down_w))
        )
    ]
    for copy in loads:
        copy.start()
    for number in range(peers):
        column = share_column(shares[number, 0:1, :CAP])
        scaled[number] = (cots[number].astype(F32) * column).astype(BF16)
    meet(layout)
    for copy in loads:
        copy.wait()

    count = 4
    chunk = 2 * TILE
    outs = to_peers(layout, send_out, back_out, out_send, out_recv)
    grads = to_peers(layout, send_grad, grad_back, grad_send, grad_recv)
    outs.insert(0, pltpu.make_async_copy(send_out.at[0], back_out.at[0], own_sems.at[0]))
    grads.insert(0, pltpu.make_async_copy(send_grad.at[0], grad_back.at[0], own_sems.at[1]))
    for block in reversed(range(peers // count)):
        pieces = slice(block * count, (block + 1) * count)
        acc[...] = jnp.zeros_like(acc)
        grad_acc[...] = jnp.zeros_like(grad_acc)

        def turn(step, carry, pieces=pieces):
            columns = pl.ds(pl.multiple_of(step * chunk, chunk), chunk)
            n = rows_in[pieces].reshape(count * CAP, width)
            grad = scaled[pieces].reshape(count * CAP, width)
            gate_pre = mm(n, gate_w[:, columns])
            up_pre = mm(n, up_w[:, columns])
            grad_act = mm(grad, down_w[columns, :], NT)
            silu, slope = silu_parts(gate_pre)
            act = (silu * up_pre).astype(BF16)
            grad_gate = (grad_act * up_pre * slope).astype(BF16)
            grad_up = (grad_act * silu).astype(BF16)
            acc[...] += mm(act, down_w[columns, :])
            grad_acc[...] += mm(grad_gate, gate_w[:, columns], NT) + mm(
                grad_up, up_w[:, columns], NT
            )
            return carry

        lax.fori_loop(0, ff // chunk, turn, 0)
        send_out[pieces] = acc[...].astype(BF16).reshape(count, CAP, width)
        send_grad[pieces] = grad_acc[...].astype(BF16).reshape(count, CAP, width)
        for copy in outs[pieces] + grads[pieces]:
            copy.start()
    for copy in outs + grads:
        copy.wait()


def run_experts(layout, rows_in, cots, shares, expert_gate, expert_up, expert_down):
    peers = layout.peers
    _, width, ff = expert_gate.shape
    dma = pltpu.SemaphoreType.DMA
    return pl.pallas_call(
        functools.partial(experts_kernel, layout),
        out_shape=[jax.ShapeDtypeStruct((peers, CAP, width), BF16)] * 2,
        in_specs=[VMEM] * 3 + [ANY] * 3,
        out_specs=[ANY] * 2,
        scratch_shapes=[
            pltpu.VMEM((width, ff), BF16),
            pltpu.VMEM((width, ff), BF16),
            pltpu.VMEM((ff, width), BF16),
            pltpu.VMEM((peers, CAP, width), BF16),
            pltpu.VMEM((4 * CAP, width), F32),
            pltpu.VMEM((4 * CAP, width), F32),
            pltpu.VMEM((peers, CAP, width), BF16),
            pltpu.VMEM((peers, CAP, width), BF16),
            dma((3,)),
            dma((peers,)),
            dma((peers,)),
            dma((peers,)),
            dma((peers,)),
            dma((2,)),
        ],
        compiler_params=pltpu.CompilerParams(
            collective_id=2, has_side_effects=True, vmem_limit_bytes=56 * MIB
        ),
        cost_estimate=pl.CostEstimate(flops=1 << 30, bytes_accessed=1 << 20, transcendentals=0),
        name="experts",
    )(rows_in, cots, shares, expert_gate, expert_up, expert_down)


def combine_kernel(
    back,
    grad_back,
    target_row,
    ids_col,
    hidden,
    mixed_in,
    grad_in,
    low,
    cot,
    gain,
    w_router,
    w_out,
    att_t,
    mixed_out,
    grad_hidden_out,
    grad_att_out,
    proj_out,
    router_out,
    gain_out,
):
    rows, width = hidden.shape
    peers = back.shape[0]
    slots = peers * CAP
    columns = jnp.transpose(
        jnp.concatenate(
            [target_row[...].astype(F32), jnp.zeros((LANES - 8, rows), F32)], axis=0
        )
    )
    slot_no = lax.broadcasted_iota(jnp.int32, (rows, slots), 1).astype(F32)
    cot_float = cot[...].astype(F32)
    logits = mm(low[...], w_router[...])
    route = jnp.exp(logits - jnp.max(logits, axis=1, keepdims=True))
    route = route / jnp.sum(route, axis=1, keepdims=True)
    labels = lax.broadcasted_iota(jnp.int32, (rows, EXPERTS), 1)
    masks = [labels == ids_col[:, k : k + 1] for k in range(2)]
    picked = [jnp.sum(jnp.where(mask, route, 0.0), axis=1, keepdims=True) for mask in masks]
    both = picked[0] + picked[1]
    chosen, shares, grads = [], [], []
    mixed = mixed_in[...]
    for k in range(2):
        chosen.append(jnp.where(slot_no == columns[:, k : k + 1], 1.0, 0.0).astype(BF16))
        fetched = mm(chosen[k], back[...].reshape(slots, width))
        shares.append(picked[k] / both)
        mixed = mixed + shares[k] * fetched
        grads.append(jnp.sum(cot_float * fetched, axis=1, keepdims=True))
    mixed_out[...] = mixed.astype(BF16)
    mean = grads[0] * shares[0] + grads[1] * shares[1]
    grad_route = jnp.zeros_like(route)
    for k in range(2):
        grad_route = grad_route + jnp.where(masks[k], (grads[k] - mean) / both, 0.0)
    grad_logits = route * (grad_route - jnp.sum(route * grad_route, axis=1, keepdims=True))
    grad_logits = grad_logits.astype(BF16)
    router_out[...] = mm(low[...], grad_logits, TN)
    grad = grad_in[...] + mm(chosen[0] + chosen[1], grad_back[...].reshape(slots, width))
    grad = grad + mm(grad_logits, w_router[...], NT)
    h = hidden[...]
    scale = lax.rsqrt(jnp.mean(h * h, axis=-1, keepdims=True) + epsilon)
    gain_out[...] = jnp.sum(grad * h * scale, axis=0, keepdims=True)
    grad = grad * gain[...]
    grad = scale * grad - h * (scale * scale * scale) * jnp.mean(grad * h, axis=-1, keepdims=True)
    grad = cot_float + grad
    grad_hidden_out[...] = grad
    grad_low = grad.astype(BF16)
    grad_att_out[...] = mm(grad_low, w_out[...], NT).astype(BF16)
    made = mm(att_t[...], grad_low).astype(BF16)
    parts = proj_out.shape[0]
    cut = width // parts
    for part in range(parts):
        proj_out[part] = made[:, part * cut : (part + 1) * cut]


def combine(layout, back, grad_back, target_row, ids_col, hidden, mixed_in, grad_in, low, cot, gain, w_router, w_out, att_t):
    rows, width = hidden.shape
    experts = layout.experts
    return pl.pallas_call(
        combine_kernel,
        out_shape=[
            jax.ShapeDtypeStruct((rows, width), BF16),
            jax.ShapeDtypeStruct((rows, width), F32),
            jax.ShapeDtypeStruct((rows, width), BF16),
            jax.ShapeDtypeStruct((experts, width, width // experts), BF16),
            jax.ShapeDtypeStruct((width, EXPERTS), F32),
            jax.ShapeDtypeStruct((1, width), F32),
        ],
        in_specs=[VMEM] * 13,
        out_specs=[VMEM] * 6,
        compiler_params=pltpu.CompilerParams(vmem_limit_bytes=56 * MIB),
        cost_estimate=pl.CostEstimate(flops=1 << 30, bytes_accessed=1 << 20, transcendentals=0),
        name="combine",
    )(back, grad_back, target_row, ids_col, hidden, mixed_in, grad_in, low, cot, gain, w_router, w_out, att_t)


def rope_back(grad, cosine, sine):
    lane = lax.broadcasted_iota(jnp.int32, grad.shape, 1)
    turned = grad * sine
    other = jnp.where(
        lane % HEAD < HEAD // 2,
        pltpu.roll(turned, LANES - HEAD // 2, 1),
        pltpu.roll(turned, HEAD // 2, 1),
    )
    return grad * cosine + other


def back_kernel(
    layout,
    q_in,
    kv_in,
    bias,
    lse,
    att_t,
    grad_att,
    tokens,
    gain,
    w_qkv,
    cosine,
    sine,
    grad_hidden,
    tokens_out,
    qkv_out,
    gain_out,
    halo_send,
    halo_recv,
    own_kv,
    packed,
    normed_t,
    send_sems,
    recv_sems,
):
    rows, width = tokens.shape
    reach, experts = layout.reach, layout.experts
    e = lax.axis_index("expert")
    pairs = HEADS // 2
    lane = lax.broadcasted_iota(jnp.int32, (rows, LANES), 1)
    meet(layout)

    def halo(distance, pair):
        return pltpu.make_async_remote_copy(
            src_ref=halo_send.at[distance - 1, pair],
            dst_ref=halo_recv.at[distance - 1, pair],
            send_sem=send_sems.at[distance - 1, pair],
            recv_sem=recv_sems.at[distance - 1, pair],
            device_id={"expert": lax.rem(e + experts - distance, experts)},
            device_id_type=MESH,
        )

    def heads(pair, carry):
        columns = pl.ds(pl.multiple_of(pair * LANES, LANES), LANES)
        value_columns = pl.ds(pl.multiple_of(width + pair * LANES, LANES), LANES)
        queries, grads = q_in[:, columns], grad_att[:, columns]
        grads_t = jnp.transpose(grads.astype(F32))
        shrunk = grads_t * att_t[columns, :].astype(F32)
        grad_q = [None, None]
        for distance in range(reach, -1, -1):
            keys = kv_in[distance, :, columns]
            values = kv_in[distance, :, value_columns]
            keys_t = jnp.transpose(keys)
            grad_k = grad_v = None
            for inner in range(2):
                head = pair * 2 + inner
                cut = slice(inner * HEAD, (inner + 1) * HEAD)
                mine = (lane // HEAD) == inner
                query = jnp.where(mine, queries, jnp.zeros_like(queries))
                grad = jnp.where(mine, grads, jnp.zeros_like(grads))
                total = jnp.sum(shrunk[cut], axis=0, keepdims=True)
                scores = mm(keys, query, NT) + bias[distance]
                probs = jnp.exp(scores - lse[pl.ds(head, 1), :])
                grad_probs = mm(values, grad, NT)
                grad_scores = (probs * (grad_probs - total)).astype(BF16)
                part_v = mm(probs.astype(BF16), grad)
                part_k = mm(grad_scores, query)
                part_q = mm(keys_t[cut], grad_scores)
                grad_v = part_v if grad_v is None else grad_v + part_v
                grad_k = part_k if grad_k is None else grad_k + part_k
                grad_q[inner] = part_q if grad_q[inner] is None else grad_q[inner] + part_q
            if distance:
                halo_send[distance - 1, pair, 0] = grad_k.astype(BF16)
                halo_send[distance - 1, pair, 1] = grad_v.astype(BF16)
                halo(distance, pair).start()
            else:
                own_kv[pair, 0] = grad_k
                own_kv[pair, 1] = grad_v
        grad = jnp.transpose(jnp.concatenate(grad_q, axis=0)) * HEAD ** (-0.5)
        packed[:, columns] = rope_back(grad, cosine[...], sine[...]).astype(BF16)
        return carry

    lax.fori_loop(0, pairs, heads, 0)
    x = tokens[...].astype(F32)
    normed_t[...] = jnp.transpose(normed(x, gain[...])).astype(BF16)

    def merge(pair, carry):
        grad_k, grad_v = own_kv[pair, 0], own_kv[pair, 1]
        for distance in range(1, reach + 1):
            halo(distance, pair).wait()
            grad_k = grad_k + halo_recv[distance - 1, pair, 0].astype(F32)
            grad_v = grad_v + halo_recv[distance - 1, pair, 1].astype(F32)
        columns = pl.ds(pl.multiple_of(width + pair * LANES, LANES), LANES)
        packed[:, columns] = rope_back(grad_k, cosine[...], sine[...]).astype(BF16)
        columns = pl.ds(pl.multiple_of(2 * width + pair * LANES, LANES), LANES)
        packed[:, columns] = grad_v.astype(BF16)
        return carry

    lax.fori_loop(0, pairs, merge, 0)
    parts = qkv_out.shape[0]
    cut = 3 * width // parts
    for part in range(parts):
        piece = packed[:, part * cut : (part + 1) * cut]
        qkv_out[part] = mm(normed_t[...], piece).astype(BF16)
    grad = mm(packed[...], w_qkv[...], NT)
    scale = lax.rsqrt(jnp.mean(x * x, axis=-1, keepdims=True) + epsilon)
    gain_out[...] = jnp.sum(grad * x * scale, axis=0, keepdims=True)
    grad = grad * gain[...]
    grad = scale * grad - x * (scale * scale * scale) * jnp.mean(grad * x, axis=-1, keepdims=True)
    tokens_out[...] = grad_hidden[...] + grad


def back(layout, q_in, kv_in, bias, lse, att_t, grad_att, tokens, gain, w_qkv, cosine, sine, grad_hidden):
    rows, width = tokens.shape
    reach, experts = layout.reach, layout.experts
    dma = pltpu.SemaphoreType.DMA
    pairs = HEADS // 2
    return pl.pallas_call(
        functools.partial(back_kernel, layout),
        out_shape=[
            jax.ShapeDtypeStruct((rows, width), F32),
            jax.ShapeDtypeStruct((experts, width, 3 * width // experts), BF16),
            jax.ShapeDtypeStruct((1, width), F32),
        ],
        in_specs=[VMEM] * 12,
        out_specs=[VMEM] * 3,
        scratch_shapes=[
            pltpu.VMEM((reach, pairs, 2, rows, LANES), BF16),
            pltpu.VMEM((reach, pairs, 2, rows, LANES), BF16),
            pltpu.VMEM((pairs, 2, rows, LANES), F32),
            pltpu.VMEM((rows, 3 * width), BF16),
            pltpu.VMEM((width, rows), BF16),
            dma((reach, pairs)),
            dma((reach, pairs)),
        ],
        compiler_params=pltpu.CompilerParams(
            collective_id=3, has_side_effects=True, vmem_limit_bytes=56 * MIB
        ),
        cost_estimate=pl.CostEstimate(flops=1 << 30, bytes_accessed=1 << 20, transcendentals=0),
        name="back",
    )(q_in, kv_in, bias, lse, att_t, grad_att, tokens, gain, w_qkv, cosine, sine, grad_hidden)


def weights_kernel(layout, *refs):
    share, outers, peers = layout.share, layout.outers, layout.peers
    row_ins, cot_ins, share_ins = refs[:outers], refs[outers : 2 * outers], refs[2 * outers : 3 * outers]
    (
        gate_any,
        up_any,
        down_any,
        gate_out,
        up_out,
        down_out,
        gate_w,
        up_w,
        gate_t,
        up_t,
        down_w,
        rows_buf,
        cots_buf,
        shares_buf,
        accs,
        sends,
        takes,
        load_sems,
        piece_sems,
        send_sems,
        recv_sems,
    ) = refs[3 * outers :]
    width = gate_w.shape[0]
    ff = gate_any.shape[2]
    span = ff // outers
    cut = ff // layout.groups
    group = lax.axis_index("group")
    mine = own_share(layout)
    begin = pl.multiple_of((group // share) * span, span)
    loads = [
        pltpu.make_async_copy(gate_any.at[mine, :, pl.ds(begin, span)], gate_w, load_sems.at[0]),
        pltpu.make_async_copy(up_any.at[mine, :, pl.ds(begin, span)], up_w, load_sems.at[1]),
        pltpu.make_async_copy(down_any.at[mine, pl.ds(begin, span), :], down_w, load_sems.at[2]),
    ]

    def fetch(outer):
        slot = outer % 2
        return [
            pltpu.make_async_copy(source, target.at[slot], piece_sems.at[slot, number])
            for number, (source, target) in enumerate(
                (
                    (row_ins[outer], rows_buf),
                    (cot_ins[outer], cots_buf),
                    (share_ins[outer], shares_buf),
                )
            )
        ]

    for copy in loads + fetch(0):
        copy.start()
    meet(layout)
    for copy in loads:
        copy.wait()
    gate_t[...] = jnp.transpose(gate_w[...])
    up_t[...] = jnp.transpose(up_w[...])
    accs[...] = jnp.zeros_like(accs)
    count = 8
    blocks = peers // count

    def add(slot, chunk, block):
        pieces = pl.ds(block * count, count)
        n = rows_buf[slot, pieces].reshape(count * CAP, width)
        grad = cots_buf[slot, pieces].reshape(count * CAP, width)
        base = pl.multiple_of(chunk * cut, cut)
        gate_pre = mm(gate_t[pl.ds(base, cut), :], n, NT)
        up_pre = mm(up_t[pl.ds(base, cut), :], n, NT)
        grad_act = mm(down_w[pl.ds(base, cut), :], grad, NT)
        silu, slope = silu_parts(gate_pre)
        act = (silu * up_pre).astype(BF16)
        grad_gate = (grad_act * up_pre * slope).astype(BF16)
        grad_up = (grad_act * silu).astype(BF16)
        accs[chunk, 0] += mm(grad_gate, n)
        accs[chunk, 1] += mm(grad_up, n)
        accs[chunk, 2] += mm(act, grad)

    copies = []
    for outer in range(outers):
        slot = outer % 2
        for copy in fetch(outer):
            copy.wait()
        if outer + 1 < outers:
            for copy in fetch(outer + 1):
                copy.start()
        for number in range(peers):
            column = share_column(shares_buf[slot, number, 0:1, :CAP])
            cots_buf[slot, number] = (cots_buf[slot, number].astype(F32) * column).astype(BF16)
        if outer + 1 < outers:

            def step(number, carry, slot=slot):
                add(slot, number // blocks, number % blocks)
                return carry

            lax.fori_loop(0, share * blocks, step, 0)
            continue
        for turn in [*range(share - 1, 0, -1), 0]:
            owner = flipped(mine, turn)

            def step(number, carry, slot=slot, owner=owner):
                add(slot, owner, number)
                return carry

            lax.fori_loop(0, blocks, step, 0)
            if turn:
                for which in range(3):
                    sends[turn - 1, which] = accs[owner, which].astype(BF16)
                    copy = pltpu.make_async_remote_copy(
                        src_ref=sends.at[turn - 1, which],
                        dst_ref=takes.at[turn - 1, which],
                        send_sem=send_sems.at[turn - 1, which],
                        recv_sem=recv_sems.at[turn - 1, which],
                        device_id={"group": flipped(group, turn)},
                        device_id_type=MESH,
                    )
                    copy.start()
                    copies.append((turn, which, copy))
            else:
                gate_out[owner] = jnp.transpose(accs[owner, 0])
                up_out[owner] = jnp.transpose(accs[owner, 1])
                down_out[owner] = accs[owner, 2]
    for turn, which, copy in copies:
        copy.wait()
        owner = flipped(mine, turn)
        got = takes[turn - 1, which].astype(F32)
        if which == 2:
            down_out[owner] = got
        else:
            (gate_out, up_out)[which][owner] = jnp.transpose(got)


def weights(layout, row_ins, cot_ins, share_ins, expert_gate, expert_up, expert_down):
    share, outers, peers = layout.share, layout.outers, layout.peers
    experts, width, ff = expert_gate.shape
    span = ff // outers
    cut = ff // layout.groups
    dma = pltpu.SemaphoreType.DMA
    return pl.pallas_call(
        functools.partial(weights_kernel, layout),
        out_shape=[
            jax.ShapeDtypeStruct((experts, width, cut), F32),
            jax.ShapeDtypeStruct((experts, width, cut), F32),
            jax.ShapeDtypeStruct((experts, cut, width), F32),
        ],
        in_specs=[ANY] * (3 * outers + 3),
        out_specs=[VMEM] * 3,
        scratch_shapes=[
            pltpu.VMEM((width, span), BF16),
            pltpu.VMEM((width, span), BF16),
            pltpu.VMEM((span, width), BF16),
            pltpu.VMEM((span, width), BF16),
            pltpu.VMEM((span, width), BF16),
            pltpu.VMEM((2, peers, CAP, width), BF16),
            pltpu.VMEM((2, peers, CAP, width), BF16),
            pltpu.VMEM((2, peers, 8, LANES), F32),
            pltpu.VMEM((share, 3, cut, width), F32),
            pltpu.VMEM((share - 1, 3, cut, width), BF16),
            pltpu.VMEM((share - 1, 3, cut, width), BF16),
            dma((3,)),
            dma((2, 3)),
            dma((share - 1, 3)),
            dma((share - 1, 3)),
        ],
        compiler_params=pltpu.CompilerParams(
            collective_id=4, has_side_effects=True, vmem_limit_bytes=60 * MIB
        ),
        cost_estimate=pl.CostEstimate(flops=1 << 30, bytes_accessed=1 << 20, transcendentals=0),
        name="weights",
    )(*row_ins, *cot_ins, *share_ins, expert_gate, expert_up, expert_down)


def swap(x, group_bits):
    groups = lax.axis_size("group")
    return lax.ppermute(x, "group", [(g, g ^ group_bits) for g in range(groups)])


def gathered(layout, x):
    return [x] + [swap(x, layout.share * k) for k in range(1, layout.outers)]


def scatter_sum(parts):
    made = parts.reshape(-1, parts.shape[-1])
    return lax.psum_scatter(made, ("expert", "group"), scatter_dimension=0, tiled=True).astype(F32)


def local(
    tokens,
    gain_attn,
    w_qkv,
    w_out,
    gain_ffn,
    w_router,
    expert_gate,
    expert_up,
    expert_down,
    dense_gate,
    dense_up,
    dense_down,
    expert_ids,
    segments,
    cotangent,
):
    rows, width = tokens.shape
    layout = Layout(lax.axis_size("group"), lax.axis_size("expert"), rows)
    group, expert = lax.axis_index("group"), lax.axis_index("expert")
    share = layout.share
    relative = ((expert_ids % share) ^ (group % share)) * layout.experts
    relative = relative + ((expert_ids // share) ^ expert)
    fill = jnp.full((6, rows), -1, jnp.int32)
    relative_row = jnp.concatenate([jnp.transpose(relative), fill], axis=0)
    ids_row = jnp.concatenate([jnp.transpose(expert_ids), fill], axis=0)
    seg_row = jnp.broadcast_to(segments.astype(F32)[None], (8, rows))
    places = (expert * rows + jnp.arange(rows, dtype=jnp.int32)).astype(F32)
    lane = jnp.arange(LANES)
    power = (lane % (HEAD // 2)).astype(F32) / (HEAD // 2)
    angles = places[:, None] * (10000.0 ** (-power))[None]
    cosine = jnp.cos(angles)
    sine = jnp.sin(angles) * jnp.where(lane % HEAD < HEAD // 2, -1.0, 1.0)[None]

    q, kv, att, att_t, lse, bias, target, cots = front(
        layout, tokens, gain_attn[None], w_qkv, cosine, sine, relative_row, seg_row, cotangent
    )
    all_cots = gathered(layout, cots)
    hidden, low, mixed, grad_low, gate_terms, up_terms, down_terms, rows_in, shares = middle(
        layout,
        att,
        tokens,
        w_out,
        gain_ffn[None],
        jnp.transpose(w_router),
        ids_row,
        target,
        cotangent,
        dense_gate,
        dense_up,
        dense_down,
    )
    all_rows = gathered(layout, rows_in)
    all_shares = gathered(layout, shares)
    gate_sum, up_sum, down_sum = map(scatter_sum, (gate_terms, up_terms, down_terms))
    came_back, grad_back = run_experts(
        layout, rows_in, cots, shares, expert_gate, expert_up, expert_down
    )
    mixed_out, grad_hidden, grad_att, proj_terms, router_term, gain_term = combine(
        layout,
        came_back,
        grad_back,
        target,
        expert_ids,
        hidden,
        mixed,
        grad_low,
        low,
        cotangent,
        gain_ffn[None],
        w_router,
        w_out,
        att_t,
    )
    proj_sum = scatter_sum(proj_terms)
    grad_tokens, qkv_terms, attn_gain_term = back(
        layout,
        q,
        kv,
        bias,
        lse,
        att_t,
        grad_att,
        tokens,
        gain_attn[None],
        w_qkv,
        cosine,
        sine,
        grad_hidden,
    )
    qkv_sum = scatter_sum(qkv_terms)
    router_sum, gain_ffn_sum, gain_attn_sum = lax.psum(
        (router_term, gain_term, attn_gain_term), ("group", "expert")
    )
    grad_gate_w, grad_up_w, grad_down_w = weights(
        layout, all_rows, all_cots, all_shares, expert_gate, expert_up, expert_down
    )
    return (
        mixed_out,
        grad_tokens,
        gain_attn_sum[0],
        qkv_sum,
        proj_sum,
        gain_ffn_sum[0],
        router_sum,
        grad_gate_w,
        grad_up_w,
        grad_down_w,
        gate_sum,
        up_sum,
        down_sum,
    )


def solution(mesh):
    in_specs = (
        P(("group", "expert"), None),
        P(),
        P(),
        P(),
        P(),
        P(),
        P("expert", None, None),
        P("expert", None, None),
        P("expert", None, None),
        P(),
        P(),
        P(),
        P(("group", "expert"), None),
        P(("group", "expert")),
        P(("group", "expert"), None),
    )
    out_specs = (
        P(("group", "expert"), None),
        P(("group", "expert"), None),
        P(),
        P("group", "expert"),
        P("group", "expert"),
        P(),
        P(),
        P("expert", None, "group"),
        P("expert", None, "group"),
        P("expert", "group", None),
        P("group", "expert"),
        P("group", "expert"),
        P("group", "expert"),
    )
    return jax.shard_map(local, mesh=mesh, in_specs=in_specs, out_specs=out_specs, check_vma=False)
```

time: 2410 us -> 921 us (0.38)
  waiting for transfers between devices: 1840 us -> 335 us
  Pallas kernels: 0 us -> 319 us
  matrix products: 296 us -> 0 us
  blocking collectives: 40.6 us -> 200 us
  other arithmetic: 106 us -> 11.1 us
  starting transfers between devices: 47.2 us -> 5.71 us
  local copies, waits for them, and re-layouts: 54.7 us -> 27.4 us
    reduce_scatter x10 -> x5, waiting for transfers between devices: 1690 us -> 334 us  [scatter_sum(): lax.psum_scatter(made, ('expert', 'group'), scatter_dimension=0, tiled=True)]
    pallas_call x0 -> x6, Pallas kernels: none -> 319 us  [the longest x1 94.4 us: weights(): pl.pallas_call(functools.partial(weights_kernel, layout), out_shape=[jax....]
    dot_general x37 -> x0, matrix products: 296 us -> none  [the longest x1 27.9 us: local(): jnp.einsum('qhd,khd->hqk', grad_attended, value_heads, preferred_element_...]
    psum x1, blocking collectives: 40.6 us -> 200 us  [local(): lax.psum((router_term, gain_term, attn_gain_term), ('group', 'expert'))]
    ppermute x6 -> x3, waiting for transfers between devices: 94.3 us -> 0.01 us  [swap(): lax.ppermute(x, 'group', [(g, g ^ group_bits) for g in range(groups)])]
    all_to_all x4 -> x0, waiting for transfers between devices: 32.1 us -> none  [the longest x1 16.1 us: local(): lax.all_to_all(grad_rows, 'expert', split_axis=1, concat_axis=0, tiled=True)]
    all_to_all x4 -> x0, starting transfers between devices: 30.5 us -> none  [the longest x1 16.8 us: local(): lax.all_to_all(send_grads, 'expert', split_axis=0, concat_axis=1, tiled=T...]
  transfers between devices with their start and end apart: 23 -> 8, of which waited for: 13 -> 4; matrix products, arithmetic and copies ran while one was open for 10% -> 1% of each run, Pallas kernels for 0% -> 14%
where the time goes in v2:
time: 921 us; the launch traced here: 913 us
  waiting for transfers between devices  335 us (36%)
  Pallas kernels  319 us (35%)
  blocking collectives  200 us (22%)
  local copies, waits for them, and re-layouts  27.4 us (3%)
  between operations  14.2 us (2%)
  other arithmetic  11.1 us (1%)
    reduce_scatter x5, waiting for transfers between devices, scatter_sum(): lax.psum_scatter(made, ('expert', 'group'), scatter_dimension=0, tiled=True)  334 us
    psum x1, blocking collectives, local(): lax.psum((router_term, gain_term, attn_gain_term), ('group', 'expert'))  200 us
    pallas_call x1, Pallas kernels, weights(): pl.pallas_call(functools.partial(weights_kernel, layout), out_shape=[jax....  94.4 us
    pallas_call x1, Pallas kernels, run_experts(): pl.pallas_call(functools.partial(experts_kernel, layout), out_shape=[jax....  69.9 us
    pallas_call x1, Pallas kernels, front(): pl.pallas_call(functools.partial(front_kernel, layout), out_shape=[jax.Sh...  59.8 us
    pallas_call x1, Pallas kernels, middle(): pl.pallas_call(functools.partial(middle_kernel, layout), out_shape=[jax.S...  46.1 us
    pallas_call x1, Pallas kernels, back(): pl.pallas_call(functools.partial(back_kernel, layout), out_shape=[jax.Sha...  36.2 us
  transfers between devices with their start and end apart: 8, of which 4 were waited for; matrix products, arithmetic and copies ran while one was open for 1% of the time, Pallas kernels for 14%

profile of v2, /device:TPU:0, one launch (start us, length us, event | category | flops | bytes accessed | tf_op | source)
XLA Modules:
  0.0 912.9 jit_solution(6585292178324931110)
XLA Ops:
  8.0 1.3 broadcast_in_dim.14.gain
  9.2 1.3 broadcast_in_dim.30.gain
  10.5 1.5 copy.28.ids_col
  13.3 1.3 concatenate.7.ids_row
  14.6 1.6 copy.29.w_router
  16.2 1.8 fusion
  18.6 59.8 %front.1 = (bf16[512,768]{1,0:T(8,128)(2,1)}, bf16[2,512,1536]{2,1,0:T(8,128)(2,1)}, bf16[512,768]{1,0:T(8,128)(2,1)}, bf16[768,512]{1,0:T(8,128)(2,1)}, f32[16,...) custom-call(bf16[512,768]{1,0:T(8,128)(2,1)} %tokens.5, ...), custom_call_target="tpu_custom_call" | custom-call | flops 1073741824 | bytes 1048576 | tf_op jit(solution)/shard_map/front/pallas_call | solution.py:300
  78.4 46.1 %middle.1 = (f32[512,768]{1,0:T(8,128)}, bf16[512,768]{1,0:T(8,128)(2,1)}, f32[512,768]{1,0:T(8,128)}, f32[512,768]{1,0:T(8,128)}, bf16[4,768,512]{2,1,0:T(8,128...) custom-call(bf16[512,768]{1,0:T(8,128)(2,1)} %get-tuple-element.44.a, ...), custom_call_target="tpu_custom_call" | custom-call | flops 1073741824 | bytes 1048576 | tf_op jit(solution)/shard_map/middle/pallas_call | solution.py:458
  124.5 69.9 %experts.1 = (bf16[16,80,768]{2,1,0:T(8,128)(2,1)}, bf16[16,80,768]{2,1,0:T(8,128)(2,1)}) custom-call(bf16[16,80,768]{2,1,0:T(8,128)(2,1)} %get-tuple-element.46.rows_in.refs_0_, bf16[16,80,768]{2,1,0:T(8,128)(2,1)} %get-tuple-element.47.cots.refs_2_, f32[16,8,128]{2,1,0:T(8,128)} %get-tuple-element.48.shares.refs_4_, bf16[4,768,2048]{2,1,0:T(8,128)(2,1)} %refs_6_.1, ...), custom_call_target="tpu_custom_call" | custom-call | flops 1073741824 | bytes 1048576 | tf_op jit(solution)/shard_map/experts/pallas_call | solution.py:585
  194.4 12.8 %combine.1 = (bf16[512,768]{1,0:T(8,128)(2,1)}, f32[512,768]{1,0:T(8,128)}, bf16[512,768]{1,0:T(8,128)(2,1)}, bf16[4,768,192]{2,1,0:T(8,128)(2,1)}, f32[768,16]{1,0:T(8,128)}, /*index=5*/f32[1,768]{1,0:T(1,128)}) custom-call(bf16[16,80,768]{2,1,0:T(8,128)(2,1)} %get-tuple-element.49.back, bf16[16,80,768]{2,1,0:T(8,128)(2,1)} %get-tuple-element.50.grad_back, ...), custom_call_target="tpu_custom_call" | custom-call | flops 1073741824 | bytes 1048576 | tf_op jit(solution)/shard_map/combine/pallas_call | solution.py:689
  208.8 6.0 copy.30
  214.8 36.2 %back.1 = (f32[512,768]{1,0:T(8,128)}, bf16[4,768,576]{2,1,0:T(8,128)(2,1)}, f32[1,768]{1,0:T(1,128)}) custom-call(bf16[512,768]{1,0:T(8,128)(2,1)} %get-tuple-element.57.q_in, bf16[2,512,1536]{2,1,0:T(8,128)(2,1)} %get-tuple-element.58.kv_in, f32[2,512,512]{2,1,0:T(8,128)} %get-tuple-element.59.bias, f32[16,512]{1,0:T(8,128)} %get-tuple-element.60.lse, ...), custom_call_target="tpu_custom_call" | custom-call | flops 1073741824 | bytes 1048576 | tf_op jit(solution)/shard_map/back/pallas_call | solution.py:835
  251.1 1.5 copy-done
  252.5 2.6 collective-permute-start.1
  255.5 2.6 collective-permute-start.2
  258.1 200.4 %all-reduce.2 = (f32[768]{0:T(1024)}, f32[768]{0:T(1024)}, f32[768,16]{1,0:T(8,128)S(1)}) all-reduce(f32[768]{0:T(1024)S(1)} %reduce, f32[768]{0:T(1024)S(1)} %reduce.1, f32[768,16]{1,0:T(8,128)S(1)} %copy-done.4), channel_id=1, replica_groups=mesh['group'=8,'expert'=4] {'group','expert'}, use_global_device_ids=true, to_apply=%region_0.1 | all-reduce | flops 13824 | bytes 110592 | tf_op jit(solution)/shard_map/psum | solution.py:1139
  459.3 1.4 convert_element_type.36
  461.4 94.4 %weights.1 = (f32[4,768,256]{2,1,0:T(8,128)}, f32[4,768,256]{2,1,0:T(8,128)}, f32[4,256,768]{2,1,0:T(8,128)}) custom-call(bf16[16,80,768]{2,1,0:T(8,128)(2,1)} %get-tuple-element.46.rows_in.refs_0_, bf16[16,80,768]{2,1,0:T(8,128)(2,1)} %collective-permute-done.refs_1_, bf16[16,80,768]{2,1,0:T(8,128)(2,1)} %get-tuple-element.47.cots.refs_2_, ...), custom_call_target="tpu_custom_call" | custom-call | flops 1073741824 | bytes 1048576 | tf_op jit(solution)/shard_map/weights/pallas_call | solution.py:1000
  555.8 17.8 %reduce-scatter.12.cloned.1.call-done = bf16[96,512]{1,0:T(8,128)(2,1)} async-done(((bf16[3072,512]{1,0:T(8,128)(2,1)}), bf16[96,512]{1,0:T(8,128)(2,1)}) %reduce-scatter.12.cloned.1.call-update) | async-done | bytes 98320 | tf_op jit(solution)/shard_map/reduce_scatter | solution.py:1045
  573.6 1.6 convert_element_type.38
  575.2 104.3 %reduce-scatter.10.cloned.1.call-done = bf16[96,512]{1,0:T(8,128)(2,1)} async-done(((bf16[3072,512]{1,0:T(8,128)(2,1)}), bf16[96,512]{1,0:T(8,128)(2,1)}) %reduce-scatter.10.cloned.1.call-update) | async-done | bytes 98320 | tf_op jit(solution)/shard_map/reduce_scatter | solution.py:1045
  679.5 1.6 convert_element_type.37
  681.1 104.8 %reduce-scatter.14.cloned.1.call-done = bf16[256,192]{0,1:T(8,128)(2,1)} async-done(((bf16[8192,192]{0,1:T(8,128)(2,1)}), bf16[256,192]{0,1:T(8,128)(2,1)}) %reduce-scatter.14.cloned.1.call-update) | async-done | bytes 98320 | tf_op jit(solution)/shard_map/reduce_scatter | solution.py:1045
  785.9 1.6 convert_element_type.39
  787.5 106.7 %reduce-scatter.6.cloned.1.call-done = bf16[96,576]{1,0:T(8,128)(2,1)} async-done(((bf16[3072,576]{1,0:T(8,128)(2,1)}), bf16[96,576]{1,0:T(8,128)(2,1)}) %reduce-scatter.6.cloned.1.call-update) | async-done | bytes 110608 | tf_op jit(solution)/shard_map/reduce_scatter | solution.py:1045
  894.1 1.6 convert_element_type.35
  895.8 2.7 copy.36
  898.4 1.7 copy.37
  900.1 1.4 copy-done.2
  901.4 1.7 copy.38
  903.1 1.4 copy-done.1
  904.5 1.7 copy.39
  (39 shorter events, 6.0 us)
Async XLA Ops:
  7.2 452.1 %reduce-scatter.8.cloned.1.call-start = ((), (), s32[]{:S(2)}) async-start(), calls=%async_computation.6 | async-start | bytes 1622016 | tf_op jit(solution)/shard_map/reduce_scatter | solution.py:1045
  207.2 366.4 %reduce-scatter.12.cloned.1.call-start = ((), (), s32[]{:S(2)}) async-start(), calls=%async_computation.8 | async-start | bytes 3244032 | tf_op jit(solution)/shard_map/reduce_scatter | solution.py:1045
  208.0 471.5 %reduce-scatter.10.cloned.1.call-start = ((), (), s32[]{:S(2)}) async-start(), calls=%async_computation.7 | async-start | bytes 3244032 | tf_op jit(solution)/shard_map/reduce_scatter | solution.py:1045
  208.7 577.2 %reduce-scatter.14.cloned.1.call-start = ((), (), s32[]{:S(2)}) async-start(), calls=%async_computation.9 | async-start | bytes 3244032 | tf_op jit(solution)/shard_map/reduce_scatter | solution.py:1045
  214.8 679.4 %reduce-scatter.6.cloned.1.call-start = ((), (), s32[]{:S(2)}) async-start(), calls=%async_computation.5 | async-start | bytes 4055040 | tf_op jit(solution)/shard_map/reduce_scatter | solution.py:1045
  251.0 1.5 copy-start
  251.0 4.5 copy-start.5
  251.0 7.0 copy-start.8
  251.0 7.1 copy-start.7
  251.0 7.1 copy-start.4
  252.5 208.2 %collective-permute-start.1 = (bf16[16,80,768]{2,1,0:T(8,128)(2,1)S(1)}, bf16[16,80,768]{2,1,0:T(8,128)(2,1)}, u32[]{:S(2)}, u32[]{:S(2)}) collective-permute-start(bf16[16,80,768]{2,1,0:T(8,128)(2,1)S(1)} %copy-done), channel_id=1, source_target_pairs={{0,16},{4,20},{8,24},{12,28},{16,0},{20,4},{24,8},{28,12},{1,17},{... | collective-permute-start | bytes 5898248 | tf_op jit(solution)/shard_map/ppermute | solution.py:1036
  255.1 205.6 %collective-permute-start = (bf16[16,80,768]{2,1,0:T(8,128)(2,1)}, bf16[16,80,768]{2,1,0:T(8,128)(2,1)}, u32[]{:S(2)}, u32[]{:S(2)}) collective-permute-start(bf16[16,80,768]{2,1,0:T(8,128)(2,1)} %get-tuple-element.46.rows_in.refs_0_), channel_id=1, source_target_pairs={{0,16},{4,20},{8,24},{12,28},{16,0},{20,4},{24,8},{28,12},{1,17},{... | collective-permute-start | bytes 5898248 | tf_op jit(solution)/shard_map/ppermute | solution.py:1036
  255.5 205.3 %collective-permute-start.2 = (f32[16,8,128]{2,1,0:T(8,128)S(1)}, f32[16,8,128]{2,1,0:T(8,128)S(1)}, u32[]{:S(2)}, u32[]{:S(2)}) collective-permute-start(f32[16,8,128]{2,1,0:T(8,128)S(1)} %copy-done.5), channel_id=1, source_target_pairs={{0,16},{4,20},{8,24},{12,28},{16,0},{20,4},{24,8},{28,12},{1,17},{... | collective-permute-start | bytes 196616 | tf_op jit(solution)/shard_map/ppermute | solution.py:1036
  460.8 0.6 copy-start.6
  555.8 342.6 %copy-start.3 = (f32[4,768,256]{2,1,0:T(8,128)S(1)}, f32[4,768,256]{2,1,0:T(8,128)}, u32[]{:S(2)}) copy-start(f32[4,768,256]{2,1,0:T(8,128)} %get-tuple-element.115) | copy-start | bytes 9437188
  898.4 3.0 copy-start.2
  901.4 3.0 copy-start.1
Sparse Core Ops, SparseCore 0:
  207.3 246.1 reduce-scatter.7
  459.0 114.5 reduce-scatter.11
  579.0 100.4 reduce-scatter.9
  685.4 100.4 reduce-scatter.13
  791.1 102.9 reduce-scatter.5

commit v3 on v2

--- a/solution.py
+++ b/solution.py
@@ -15,7 +15,10 @@
 QUARTERS = 4
 LANES = 128
 TILE = 256
+SMALL = EXPERTS + 8
 NEG = -1e30
+FAR_COTS = (3, 11, 16)
+FAR_ROWS = (5, 13, 16)
 
 epsilon = 1e-06
 F32 = jnp.float32
@@ -58,6 +61,9 @@
         per_quarter = max(experts // QUARTERS, 1)
         self.reach = min((WINDOW - 1) // rows + 1, 2 * per_quarter - 1)
 
+    def far(self, number):
+        return {"group": flipped(lax.axis_index("group"), number * self.share)}
+
     def peer(self, number):
         group, expert = lax.axis_index("group"), lax.axis_index("expert")
         return {
@@ -70,7 +76,9 @@
     barrier = pltpu.get_barrier_semaphore()
     for number in range(1, layout.peers):
         pl.semaphore_signal(barrier, inc=1, device_id=layout.peer(number), device_id_type=MESH)
-    pl.semaphore_wait(barrier, layout.peers - 1)
+    for number in range(1, layout.outers):
+        pl.semaphore_signal(barrier, inc=1, device_id=layout.far(number), device_id_type=MESH)
+    pl.semaphore_wait(barrier, layout.peers + layout.outers - 2)
 
 
 def to_peers(layout, source, target, send_sems, recv_sems):
@@ -85,6 +93,69 @@
         )
         for number in range(1, layout.peers)
     ]
+
+
+def to_far(layout, source, target, low, high, send_sems, recv_sems):
+    return [
+        pltpu.make_async_remote_copy(
+            src_ref=source.at[low:high],
+            dst_ref=target.at[number - 1],
+            send_sem=send_sems.at[number - 1],
+            recv_sem=recv_sems.at[number - 1],
+            device_id=layout.far(number),
+            device_id_type=MESH,
+        )
+        for number in range(1, layout.outers)
+    ]
+
+
+def far_shape(layout, count, width):
+    return jax.ShapeDtypeStruct((layout.outers - 1, count, CAP, width), BF16)
+
+
+def bit_of(axis, bit):
+    return (lax.axis_index(axis) // bit) % 2
+
+
+class Halving:
+    def __init__(self, axis, bit, held, taken, send_sems, recv_sems):
+        self.bit = bit_of(axis, bit)
+        self.held, self.taken = held, taken
+        self.copies = [
+            pltpu.make_async_remote_copy(
+                src_ref=held.at[2 * block + 1 - self.bit],
+                dst_ref=taken.at[block],
+                send_sem=send_sems.at[block],
+                recv_sem=recv_sems.at[block],
+                device_id={axis: flipped(lax.axis_index(axis), bit)},
+                device_id_type=MESH,
+            )
+            for block in range(taken.shape[0])
+        ]
+
+    def start(self):
+        for copy in self.copies:
+            copy.start()
+
+    def add(self, last=None):
+        for block, copy in enumerate(self.copies):
+            copy.wait()
+            mine = 2 * block + self.bit
+            if last is not None:
+                last[...] = self.taken[block].astype(F32) + self.held[mine].astype(F32)
+            elif len(self.taken.shape) == 3:
+                self.taken[block] = (
+                    self.taken[block].astype(F32) + self.held[mine].astype(F32)
+                ).astype(BF16)
+            else:
+
+                def one(number, carry, block=block, mine=mine):
+                    self.taken[block, number] = (
+                        self.taken[block, number].astype(F32) + self.held[mine, number].astype(F32)
+                    ).astype(BF16)
+                    return carry
+
+                lax.fori_loop(0, self.taken.shape[1], one, 0)
 
 
 def rope_turn(x, cosine, sine):
@@ -137,6 +208,7 @@
     bias_out,
     target_out,
     cots_out,
+    far_out,
     normed_low,
     send_cot,
     seg_all,
@@ -150,6 +222,8 @@
     cot_send,
     cot_recv,
     own_sem,
+    far_send,
+    far_recv,
 ):
     rows, width = tokens.shape
     reach, experts = layout.reach, layout.experts
@@ -223,6 +297,13 @@
         if distance:
             for copy in halos[distance - 1]:
                 copy.wait()
+        if distance == 1:
+            own.wait()
+            for copy in sends[: FAR_COTS[0] - 1]:
+                copy.wait()
+            far = to_far(layout, cots_out, far_out, 0, FAR_COTS[0], far_send, far_recv)
+            for copy in far:
+                copy.start()
         seg_col = jnp.transpose(jnp.broadcast_to(seg_all[distance, 0:1], (LANES, rows)))[:, 0:1]
         key_no = lax.broadcasted_iota(jnp.int32, (rows, rows), 0) - distance * rows
         offset = lax.broadcasted_iota(jnp.int32, (rows, rows), 1) - key_no
@@ -288,8 +369,7 @@
         return carry
 
     lax.fori_loop(0, HEADS // 2, finish, 0)
-    own.wait()
-    for copy in sends:
+    for copy in sends[FAR_COTS[0] - 1 :] + far:
         copy.wait()
 
 
@@ -308,9 +388,10 @@
             jax.ShapeDtypeStruct((reach + 1, rows, rows), F32),
             jax.ShapeDtypeStruct((8, rows), jnp.int32),
             jax.ShapeDtypeStruct((peers, CAP, width), BF16),
+            far_shape(layout, FAR_COTS[0], width),
         ],
         in_specs=[VMEM] * 8,
-        out_specs=[VMEM] * 7 + [ANY],
+        out_specs=[VMEM] * 7 + [ANY] * 2,
         scratch_shapes=[
             pltpu.VMEM((rows, width), BF16),
             pltpu.VMEM((peers, CAP, width), BF16),
@@ -325,6 +406,8 @@
             dma((peers,)),
             dma((peers,)),
             dma,
+            dma((layout.outers - 1,)),
+            dma((layout.outers - 1,)),
         ],
         compiler_params=pltpu.CompilerParams(
             collective_id=0, has_side_effects=True, vmem_limit_bytes=56 * MIB
@@ -359,6 +442,7 @@
     dense_gate,
     dense_up,
     dense_down,
+    cots,
     hidden_out,
     low_out,
     mixed_out,
@@ -368,18 +452,30 @@
     down_out,
     rows_out,
     shares_out,
+    far_out,
     send_rows,
     send_shares,
     low_t,
+    gate_held,
+    up_held,
+    down_held,
     row_send,
     row_recv,
     share_send,
     share_recv,
     own_sems,
+    far_send,
+    far_recv,
+    half_send,
+    half_recv,
 ):
     rows, width = tokens.shape
     ff = dense_gate.shape[1]
     experts = layout.experts
+    meet(layout)
+    far = to_far(layout, cots, far_out, FAR_COTS[0], FAR_COTS[1], far_send, far_recv)
+    for copy in far:
+        copy.start()
     hidden_out[...] = tokens[...].astype(F32) + mm(att[...], w_out[...])
     low = normed(hidden_out[...], gain[...]).astype(BF16)
     low_out[...] = low
@@ -410,7 +506,6 @@
         share = jnp.sum(share, axis=0, keepdims=True)
         send_shares[number, :, :CAP] = jnp.broadcast_to(share, (8, CAP))
 
-    meet(layout)
     sends = to_peers(layout, send_rows, rows_out, row_send, row_recv)
     sends += to_peers(layout, send_shares, shares_out, share_send, share_recv)
     sends.append(pltpu.make_async_copy(send_rows.at[0], rows_out.at[0], own_sems.at[0]))
@@ -423,9 +518,19 @@
     grad_out[...] = jnp.zeros_like(grad_out)
     part_width = ff // experts
     per_part = part_width // TILE
+    half = experts // 2
+    odd = bit_of("expert", 1)
+    halvings = [
+        Halving("expert", 1, held, taken, half_send.at[number], half_recv.at[number])
+        for number, (held, taken) in enumerate(
+            ((gate_held, gate_out), (up_held, up_out), (down_held, down_out))
+        )
+    ]
 
     def branch(step, carry):
-        columns = pl.ds(pl.multiple_of(step * TILE, TILE), TILE)
+        place = step // per_part
+        part = 2 * (place % half) + (odd + 1 + place // half) % 2
+        columns = pl.ds(pl.multiple_of(part * part_width + (step % per_part) * TILE, TILE), TILE)
         gate_w, up_w, down_w = dense_gate[:, columns], dense_up[:, columns], dense_down[columns, :]
         gate_pre = mm(low_out[...], gate_w)
         up_pre = mm(low_out[...], up_w)
@@ -437,20 +542,28 @@
         mixed_out[...] += mm(act, down_w)
         grad_out[...] += mm(grad_gate, gate_w, NT) + mm(grad_up, up_w, NT)
         inside = pl.ds(pl.multiple_of((step % per_part) * TILE, TILE), TILE)
-        gate_out[step // per_part, :, inside] = mm(low_t[...], grad_gate).astype(BF16)
-        up_out[step // per_part, :, inside] = mm(low_t[...], grad_up).astype(BF16)
+        gate_held[part, :, inside] = mm(low_t[...], grad_gate).astype(BF16)
+        up_held[part, :, inside] = mm(low_t[...], grad_up).astype(BF16)
         made = mm(act, cot[...], TN).astype(BF16)
-        for part in range(experts):
+        for other in range(experts):
             cut = width // experts
-            down_out[part, columns, :] = made[:, part * cut : (part + 1) * cut]
+            down_held[other, columns, :] = made[:, other * cut : (other + 1) * cut]
         return carry
 
-    lax.fori_loop(0, ff // TILE, branch, 0)
+    lax.fori_loop(0, ff // (2 * TILE), branch, 0)
+    for halving in halvings[:2]:
+        halving.start()
+    lax.fori_loop(ff // (2 * TILE), ff // TILE, branch, 0)
+    halvings[2].start()
+    for halving in halvings:
+        halving.add()
+    for copy in far:
+        copy.wait()
     for copy in sends:
         copy.wait()
 
 
-def middle(layout, att, tokens, w_out, gain, w_router_t, ids_row, target_row, cot, dense_gate, dense_up, dense_down):
+def middle(layout, att, tokens, w_out, gain, w_router_t, ids_row, target_row, cot, dense_gate, dense_up, dense_down, cots):
     rows, width = tokens.shape
     ff = dense_gate.shape[1]
     peers, experts = layout.peers, layout.experts
@@ -462,30 +575,38 @@
             jax.ShapeDtypeStruct((rows, width), BF16),
             jax.ShapeDtypeStruct((rows, width), F32),
             jax.ShapeDtypeStruct((rows, width), F32),
-            jax.ShapeDtypeStruct((experts, width, ff // experts), BF16),
-            jax.ShapeDtypeStruct((experts, width, ff // experts), BF16),
-            jax.ShapeDtypeStruct((experts, ff, width // experts), BF16),
+            jax.ShapeDtypeStruct((experts // 2, width, ff // experts), BF16),
+            jax.ShapeDtypeStruct((experts // 2, width, ff // experts), BF16),
+            jax.ShapeDtypeStruct((experts // 2, ff, width // experts), BF16),
             jax.ShapeDtypeStruct((peers, CAP, width), BF16),
             jax.ShapeDtypeStruct((peers, 8, LANES), F32),
+            far_shape(layout, FAR_COTS[1] - FAR_COTS[0], width),
         ],
-        in_specs=[VMEM] * 11,
-        out_specs=[VMEM] * 7 + [ANY, ANY],
+        in_specs=[VMEM] * 11 + [ANY],
+        out_specs=[VMEM] * 7 + [ANY] * 3,
         scratch_shapes=[
             pltpu.VMEM((peers, CAP, width), BF16),
             pltpu.VMEM((peers, 8, LANES), F32),
             pltpu.VMEM((width, rows), BF16),
+            pltpu.VMEM((experts, width, ff // experts), BF16),
+            pltpu.VMEM((experts, width, ff // experts), BF16),
+            pltpu.VMEM((experts, ff, width // experts), BF16),
             dma((peers,)),
             dma((peers,)),
             dma((peers,)),
             dma((peers,)),
             dma((2,)),
+            dma((layout.outers - 1,)),
+            dma((layout.outers - 1,)),
+            dma((3, experts // 2)),
+            dma((3, experts // 2)),
         ],
         compiler_params=pltpu.CompilerParams(
             collective_id=1, has_side_effects=True, vmem_limit_bytes=56 * MIB
         ),
         cost_estimate=pl.CostEstimate(flops=1 << 30, bytes_accessed=1 << 20, transcendentals=0),
         name="middle",
-    )(att, tokens, w_out, gain, w_router_t, ids_row, target_row, cot, dense_gate, dense_up, dense_down)
+    )(att, tokens, w_out, gain, w_router_t, ids_row, target_row, cot, dense_gate, dense_up, dense_down, cots)
 
 
 def share_column(share_row):
@@ -506,8 +627,20 @@
     gate_any,
     up_any,
     down_any,
+    gate_held,
+    up_held,
+    down_held,
+    rows_any,
+    cots_any,
+    shares_any,
     back_out,
     grad_back,
+    gate_sum,
+    up_sum,
+    down_sum,
+    far_cots,
+    far_rows,
+    far_shares,
     gate_w,
     up_w,
     down_w,
@@ -522,6 +655,11 @@
     grad_send,
     grad_recv,
     own_sems,
+    far_send,
+    far_recv,
+    half_send,
+    half_recv,
+    *steps,
 ):
     peers = layout.peers
     width, ff = gate_w.shape
@@ -534,25 +672,55 @@
     ]
     for copy in loads:
         copy.start()
+    meet(layout)
+    far = (
+        to_far(layout, cots_any, far_cots, FAR_COTS[1], FAR_COTS[2], far_send.at[0], far_recv.at[0])
+        + to_far(layout, rows_any, far_rows, 0, FAR_ROWS[0], far_send.at[1], far_recv.at[1])
+        + to_far(layout, shares_any, far_shares, 0, peers, far_send.at[2], far_recv.at[2])
+    )
+    for copy in far:
+        copy.start()
+    chains = []
+    for number, (held, made) in enumerate(
+        ((gate_held, gate_sum), (up_held, up_sum), (down_held, down_sum))
+    ):
+        chain, bit, level = [], 2, 0
+        while bit < layout.experts:
+            last = 2 * bit == layout.experts
+            taken = made if last else steps[number]
+            chain.append(
+                Halving(
+                    "expert",
+                    bit,
+                    held,
+                    taken,
+                    half_send.at[number, level],
+                    half_recv.at[number, level],
+                )
+            )
+            held, bit, level = taken, 2 * bit, level + 1
+        chains.append(chain)
+    for chain in chains:
+        chain[0].start()
     for number in range(peers):
         column = share_column(shares[number, 0:1, :CAP])
         scaled[number] = (cots[number].astype(F32) * column).astype(BF16)
-    meet(layout)
     for copy in loads:
         copy.wait()
 
-    count = 4
     chunk = 2 * TILE
     outs = to_peers(layout, send_out, back_out, out_send, out_recv)
     grads = to_peers(layout, send_grad, grad_back, grad_send, grad_recv)
     outs.insert(0, pltpu.make_async_copy(send_out.at[0], back_out.at[0], own_sems.at[0]))
     grads.insert(0, pltpu.make_async_copy(send_grad.at[0], grad_back.at[0], own_sems.at[1]))
-    for block in reversed(range(peers // count)):
-        pieces = slice(block * count, (block + 1) * count)
-        acc[...] = jnp.zeros_like(acc)
-        grad_acc[...] = jnp.zeros_like(grad_acc)
-
-        def turn(step, carry, pieces=pieces):
+    high = peers
+    for count in (8, 4, 4):
+        pieces = slice(high - count, high)
+        high -= count
+        acc[: count * CAP] = jnp.zeros((count * CAP, width), F32)
+        grad_acc[: count * CAP] = jnp.zeros((count * CAP, width), F32)
+
+        def turn(step, carry, pieces=pieces, count=count):
             columns = pl.ds(pl.multiple_of(step * chunk, chunk), chunk)
             n = rows_in[pieces].reshape(count * CAP, width)
             grad = scaled[pieces].reshape(count * CAP, width)
@@ -563,37 +731,54 @@
             act = (silu * up_pre).astype(BF16)
             grad_gate = (grad_act * up_pre * slope).astype(BF16)
             grad_up = (grad_act * silu).astype(BF16)
-            acc[...] += mm(act, down_w[columns, :])
-            grad_acc[...] += mm(grad_gate, gate_w[:, columns], NT) + mm(
+            acc[: count * CAP] += mm(act, down_w[columns, :])
+            grad_acc[: count * CAP] += mm(grad_gate, gate_w[:, columns], NT) + mm(
                 grad_up, up_w[:, columns], NT
             )
             return carry
 
         lax.fori_loop(0, ff // chunk, turn, 0)
-        send_out[pieces] = acc[...].astype(BF16).reshape(count, CAP, width)
-        send_grad[pieces] = grad_acc[...].astype(BF16).reshape(count, CAP, width)
+        send_out[pieces] = acc[: count * CAP].astype(BF16).reshape(count, CAP, width)
+        send_grad[pieces] = grad_acc[: count * CAP].astype(BF16).reshape(count, CAP, width)
         for copy in outs[pieces] + grads[pieces]:
             copy.start()
-    for copy in outs + grads:
+    for level in range(len(chains[0])):
+        for chain in chains:
+            chain[level].add()
+            if level + 1 < len(chain):
+                chain[level + 1].start()
+    for copy in outs + grads + far:
         copy.wait()
 
 
-def run_experts(layout, rows_in, cots, shares, expert_gate, expert_up, expert_down):
-    peers = layout.peers
+def run_experts(layout, rows_in, cots, shares, expert_gate, expert_up, expert_down, sums):
+    peers, outers = layout.peers, layout.outers
     _, width, ff = expert_gate.shape
     dma = pltpu.SemaphoreType.DMA
+    half = layout.experts // 2
+    levels = half.bit_length() - 1
+    last = [jax.ShapeDtypeStruct((1,) + one.shape[1:], BF16) for one in sums]
+    steps = []
+    if levels == 2:
+        steps = [pltpu.VMEM((half // 2,) + one.shape[1:], BF16) for one in sums]
     return pl.pallas_call(
         functools.partial(experts_kernel, layout),
-        out_shape=[jax.ShapeDtypeStruct((peers, CAP, width), BF16)] * 2,
-        in_specs=[VMEM] * 3 + [ANY] * 3,
-        out_specs=[ANY] * 2,
+        out_shape=[jax.ShapeDtypeStruct((peers, CAP, width), BF16)] * 2
+        + last
+        + [
+            far_shape(layout, FAR_COTS[2] - FAR_COTS[1], width),
+            far_shape(layout, FAR_ROWS[0], width),
+            jax.ShapeDtypeStruct((outers - 1, peers, 8, LANES), F32),
+        ],
+        in_specs=[VMEM] * 3 + [ANY] * 3 + [VMEM] * 3 + [ANY] * 3,
+        out_specs=[ANY] * 2 + [VMEM] * 3 + [ANY] * 3,
         scratch_shapes=[
             pltpu.VMEM((width, ff), BF16),
             pltpu.VMEM((width, ff), BF16),
             pltpu.VMEM((ff, width), BF16),
             pltpu.VMEM((peers, CAP, width), BF16),
-            pltpu.VMEM((4 * CAP, width), F32),
-            pltpu.VMEM((4 * CAP, width), F32),
+            pltpu.VMEM((8 * CAP, width), F32),
+            pltpu.VMEM((8 * CAP, width), F32),
             pltpu.VMEM((peers, CAP, width), BF16),
             pltpu.VMEM((peers, CAP, width), BF16),
             dma((3,)),
@@ -602,13 +787,29 @@
             dma((peers,)),
             dma((peers,)),
             dma((2,)),
+            dma((3, outers - 1)),
+            dma((3, outers - 1)),
+            dma((3, levels, half // 2)),
+            dma((3, levels, half // 2)),
+            *steps,
         ],
         compiler_params=pltpu.CompilerParams(
-            collective_id=2, has_side_effects=True, vmem_limit_bytes=56 * MIB
+            collective_id=2, has_side_effects=True, vmem_limit_bytes=58 * MIB
         ),
         cost_estimate=pl.CostEstimate(flops=1 << 30, bytes_accessed=1 << 20, transcendentals=0),
         name="experts",
-    )(rows_in, cots, shares, expert_gate, expert_up, expert_down)
+    )(
+        rows_in,
+        cots,
+        shares,
+        expert_gate,
+        expert_up,
+        expert_down,
+        *sums,
+        rows_in,
+        cots,
+        shares,
+    )
 
 
 def combine_kernel(
@@ -629,8 +830,7 @@
     grad_hidden_out,
     grad_att_out,
     proj_out,
-    router_out,
-    gain_out,
+    small_out,
 ):
     rows, width = hidden.shape
     peers = back.shape[0]
@@ -664,12 +864,13 @@
         grad_route = grad_route + jnp.where(masks[k], (grads[k] - mean) / both, 0.0)
     grad_logits = route * (grad_route - jnp.sum(route * grad_route, axis=1, keepdims=True))
     grad_logits = grad_logits.astype(BF16)
-    router_out[...] = mm(low[...], grad_logits, TN)
+    small_out[...] = jnp.zeros_like(small_out)
+    small_out[:EXPERTS] = mm(grad_logits, low[...], TN)
     grad = grad_in[...] + mm(chosen[0] + chosen[1], grad_back[...].reshape(slots, width))
     grad = grad + mm(grad_logits, w_router[...], NT)
     h = hidden[...]
     scale = lax.rsqrt(jnp.mean(h * h, axis=-1, keepdims=True) + epsilon)
-    gain_out[...] = jnp.sum(grad * h * scale, axis=0, keepdims=True)
+    small_out[EXPERTS : EXPERTS + 1] = jnp.sum(grad * h * scale, axis=0, keepdims=True)
     grad = grad * gain[...]
     grad = scale * grad - h * (scale * scale * scale) * jnp.mean(grad * h, axis=-1, keepdims=True)
     grad = cot_float + grad
@@ -693,11 +894,10 @@
             jax.ShapeDtypeStruct((rows, width), F32),
             jax.ShapeDtypeStruct((rows, width), BF16),
             jax.ShapeDtypeStruct((experts, width, width // experts), BF16),
-            jax.ShapeDtypeStruct((width, EXPERTS), F32),
-            jax.ShapeDtypeStruct((1, width), F32),
+            jax.ShapeDtypeStruct((SMALL, width), F32),
         ],
         in_specs=[VMEM] * 13,
-        out_specs=[VMEM] * 6,
+        out_specs=[VMEM] * 5,
         compiler_params=pltpu.CompilerParams(vmem_limit_bytes=56 * MIB),
         cost_estimate=pl.CostEstimate(flops=1 << 30, bytes_accessed=1 << 20, transcendentals=0),
         name="combine",
@@ -729,9 +929,17 @@
     cosine,
     sine,
     grad_hidden,
+    gate_held,
+    up_held,
+    down_held,
+    rows_any,
     tokens_out,
     qkv_out,
     gain_out,
+    gate_sum,
+    up_sum,
+    down_sum,
+    far_out,
     halo_send,
     halo_recv,
     own_kv,
@@ -739,6 +947,10 @@
     normed_t,
     send_sems,
     recv_sems,
+    far_send,
+    far_recv,
+    half_send,
+    half_recv,
 ):
     rows, width = tokens.shape
     reach, experts = layout.reach, layout.experts
@@ -746,6 +958,17 @@
     pairs = HEADS // 2
     lane = lax.broadcasted_iota(jnp.int32, (rows, LANES), 1)
     meet(layout)
+    far = to_far(layout, rows_any, far_out, FAR_ROWS[0], FAR_ROWS[1], far_send, far_recv)
+    for copy in far:
+        copy.start()
+    halvings = [
+        Halving("group", 1, held, taken, half_send.at[number], half_recv.at[number])
+        for number, (held, taken) in enumerate(
+            ((gate_held, gate_sum), (up_held, up_sum), (down_held, down_sum))
+        )
+    ]
+    for halving in halvings:
+        halving.start()
 
     def halo(distance, pair):
         return pltpu.make_async_remote_copy(
@@ -825,9 +1048,13 @@
     grad = grad * gain[...]
     grad = scale * grad - x * (scale * scale * scale) * jnp.mean(grad * x, axis=-1, keepdims=True)
     tokens_out[...] = grad_hidden[...] + grad
-
-
-def back(layout, q_in, kv_in, bias, lse, att_t, grad_att, tokens, gain, w_qkv, cosine, sine, grad_hidden):
+    for halving in halvings:
+        halving.add()
+    for copy in far:
+        copy.wait()
+
+
+def back(layout, q_in, kv_in, bias, lse, att_t, grad_att, tokens, gain, w_qkv, cosine, sine, grad_hidden, sums, rows_in):
     rows, width = tokens.shape
     reach, experts = layout.reach, layout.experts
     dma = pltpu.SemaphoreType.DMA
@@ -838,9 +1065,11 @@
             jax.ShapeDtypeStruct((rows, width), F32),
             jax.ShapeDtypeStruct((experts, width, 3 * width // experts), BF16),
             jax.ShapeDtypeStruct((1, width), F32),
+            *[jax.ShapeDtypeStruct((layout.groups // 2,) + one.shape[1:], BF16) for one in sums],
+            far_shape(layout, FAR_ROWS[1] - FAR_ROWS[0], width),
         ],
-        in_specs=[VMEM] * 12,
-        out_specs=[VMEM] * 3,
+        in_specs=[VMEM] * 15 + [ANY],
+        out_specs=[VMEM] * 6 + [ANY],
         scratch_shapes=[
             pltpu.VMEM((reach, pairs, 2, rows, LANES), BF16),
             pltpu.VMEM((reach, pairs, 2, rows, LANES), BF16),
@@ -849,25 +1078,41 @@
             pltpu.VMEM((width, rows), BF16),
             dma((reach, pairs)),
             dma((reach, pairs)),
+            dma((layout.outers - 1,)),
+            dma((layout.outers - 1,)),
+            dma((3, layout.groups // 2)),
+            dma((3, layout.groups // 2)),
         ],
         compiler_params=pltpu.CompilerParams(
             collective_id=3, has_side_effects=True, vmem_limit_bytes=56 * MIB
         ),
         cost_estimate=pl.CostEstimate(flops=1 << 30, bytes_accessed=1 << 20, transcendentals=0),
         name="back",
-    )(q_in, kv_in, bias, lse, att_t, grad_att, tokens, gain, w_qkv, cosine, sine, grad_hidden)
+    )(q_in, kv_in, bias, lse, att_t, grad_att, tokens, gain, w_qkv, cosine, sine, grad_hidden, *sums, rows_in)
 
 
 def weights_kernel(layout, *refs):
     share, outers, peers = layout.share, layout.outers, layout.peers
-    row_ins, cot_ins, share_ins = refs[:outers], refs[outers : 2 * outers], refs[2 * outers : 3 * outers]
     (
+        rows_own,
+        cots_own,
+        shares_own,
+        rows_a,
+        rows_b,
+        cots_a,
+        cots_b,
+        cots_c,
+        shares_far,
         gate_any,
         up_any,
         down_any,
-        gate_out,
-        up_out,
-        down_out,
+        *terms,
+    ) = refs[:17]
+    small_in = refs[17]
+    rows_c, gate_out, up_out, down_out = refs[18:22]
+    sums_out = refs[22:27]
+    small_out = refs[27]
+    (
         gate_w,
         up_w,
         gate_t,
@@ -879,11 +1124,18 @@
         accs,
         sends,
         takes,
+        small_sums,
+        small_takes,
         load_sems,
         piece_sems,
         send_sems,
         recv_sems,
-    ) = refs[3 * outers :]
+        far_send,
+        far_recv,
+        small_send,
+        small_recv,
+    ) = refs[28:49]
+    rest = list(refs[49:])
     width = gate_w.shape[0]
     ff = gate_any.shape[2]
     span = ff // outers
@@ -897,22 +1149,86 @@
         pltpu.make_async_copy(down_any.at[mine, pl.ds(begin, span), :], down_w, load_sems.at[2]),
     ]
 
-    def fetch(outer):
-        slot = outer % 2
+    def fetch(turn, outer):
+        slot = (turn * outers + outer) % 2
+        row_cuts, cot_cuts = (0, *FAR_ROWS), (0, *FAR_COTS)
+        if outer == 0:
+            sources = [
+                (rows_own, rows_buf.at[slot]),
+                (cots_own, cots_buf.at[slot]),
+                (shares_own, shares_buf.at[slot]),
+            ]
+        else:
+            sources = [
+                (one.at[outer - 1], target.at[slot, cuts[place] : cuts[place + 1]])
+                for parts, cuts, target in (
+                    ((rows_a, rows_b, rows_c), row_cuts, rows_buf),
+                    ((cots_a, cots_b, cots_c), cot_cuts, cots_buf),
+                )
+                for place, one in enumerate(parts)
+            ]
+            sources.append((shares_far.at[outer - 1], shares_buf.at[slot]))
         return [
-            pltpu.make_async_copy(source, target.at[slot], piece_sems.at[slot, number])
-            for number, (source, target) in enumerate(
-                (
-                    (row_ins[outer], rows_buf),
-                    (cot_ins[outer], cots_buf),
-                    (share_ins[outer], shares_buf),
-                )
-            )
+            pltpu.make_async_copy(source, target, piece_sems.at[slot, number])
+            for number, (source, target) in enumerate(sources)
         ]
 
-    for copy in loads + fetch(0):
+    for copy in loads + fetch(0, 0):
         copy.start()
     meet(layout)
+    far = to_far(layout, rows_own, rows_c, FAR_ROWS[1], FAR_ROWS[2], far_send, far_recv)
+    for copy in far:
+        copy.start()
+
+    expert_bits = [("expert", 1 << n) for n in range(layout.experts.bit_length() - 1)]
+    group_bits = [("group", 1 << n) for n in range(layout.groups.bit_length() - 1)]
+    chains = []
+    for number, term in enumerate(terms):
+        bits = group_bits[1:] if number < 3 else expert_bits + group_bits
+        held, chain = term, []
+        for axis, bit in bits:
+            if axis == "group" and len(held.shape) == 4:
+                held = held.at[0]
+            taken, to_sems, from_sems = rest.pop(0), rest.pop(0), rest.pop(0)
+            chain.append(Halving(axis, bit, held, taken, to_sems, from_sems))
+            held = taken
+        chains.append(chain)
+    small_sums[0] = small_in[...]
+
+    def small_copy(level):
+        axis, bit = (expert_bits + group_bits)[level]
+        return pltpu.make_async_remote_copy(
+            src_ref=small_sums.at[level],
+            dst_ref=small_takes.at[level],
+            send_sem=small_send.at[level],
+            recv_sem=small_recv.at[level],
+            device_id={axis: flipped(lax.axis_index(axis), bit)},
+            device_id_type=MESH,
+        )
+
+    levels = len(expert_bits + group_bits)
+
+    def advance(level):
+        for number, chain in enumerate(chains):
+            if 0 < level <= len(chain):
+                chain[level - 1].add(sums_out[number] if level == len(chain) else None)
+            if level < len(chain):
+                chain[level].start()
+        if level:
+            small_copy(level - 1).wait()
+            made = small_sums[level - 1] + small_takes[level - 1]
+            if level < levels:
+                small_sums[level] = made
+            else:
+                small_out[...] = made
+        if level < levels:
+            small_copy(level).start()
+
+    advance(0)
+    points = share * outers
+    marks = [max(0, (points * at) // 8 - 1) for at in (2, 6, 7, 8)]
+    done = 1
+
     for copy in loads:
         copy.wait()
     gate_t[...] = jnp.transpose(gate_w[...])
@@ -933,54 +1249,64 @@
         act = (silu * up_pre).astype(BF16)
         grad_gate = (grad_act * up_pre * slope).astype(BF16)
         grad_up = (grad_act * silu).astype(BF16)
-        accs[chunk, 0] += mm(grad_gate, n)
-        accs[chunk, 1] += mm(grad_up, n)
-        accs[chunk, 2] += mm(act, grad)
+        accs[0] += mm(grad_gate, n)
+        accs[1] += mm(grad_up, n)
+        accs[2] += mm(act, grad)
 
     copies = []
-    for outer in range(outers):
-        slot = outer % 2
-        for copy in fetch(outer):
-            copy.wait()
-        if outer + 1 < outers:
-            for copy in fetch(outer + 1):
-                copy.start()
-        for number in range(peers):
-            column = share_column(shares_buf[slot, number, 0:1, :CAP])
-            cots_buf[slot, number] = (cots_buf[slot, number].astype(F32) * column).astype(BF16)
-        if outer + 1 < outers:
-
-            def step(number, carry, slot=slot):
-                add(slot, number // blocks, number % blocks)
+    turns = [*range(share - 1, 0, -1), 0]
+    for place, turn in enumerate(turns):
+        owner = flipped(mine, turn)
+        accs[...] = jnp.zeros_like(accs)
+        for outer in range(outers):
+            slot = (place * outers + outer) % 2
+            if place == 0 and outer:
+                if outer == 1:
+                    for copy in far:
+                        copy.wait()
+                for copy in fetch(place, outer):
+                    copy.start()
+            for copy in fetch(place, outer):
+                copy.wait()
+            following = place * outers + outer + 1
+            if outers <= following < points:
+                for copy in fetch(following // outers, following % outers):
+                    copy.start()
+
+            def scale(number, carry, slot=slot):
+                column = share_column(shares_buf[slot, number, 0:1, :CAP])
+                cots_buf[slot, number] = (cots_buf[slot, number].astype(F32) * column).astype(BF16)
                 return carry
-
-            lax.fori_loop(0, share * blocks, step, 0)
-            continue
-        for turn in [*range(share - 1, 0, -1), 0]:
-            owner = flipped(mine, turn)
 
             def step(number, carry, slot=slot, owner=owner):
                 add(slot, owner, number)
                 return carry
 
+            lax.fori_loop(0, peers, scale, 0)
             lax.fori_loop(0, blocks, step, 0)
-            if turn:
-                for which in range(3):
-                    sends[turn - 1, which] = accs[owner, which].astype(BF16)
-                    copy = pltpu.make_async_remote_copy(
-                        src_ref=sends.at[turn - 1, which],
-                        dst_ref=takes.at[turn - 1, which],
-                        send_sem=send_sems.at[turn - 1, which],
-                        recv_sem=recv_sems.at[turn - 1, which],
-                        device_id={"group": flipped(group, turn)},
-                        device_id_type=MESH,
-                    )
-                    copy.start()
-                    copies.append((turn, which, copy))
-            else:
-                gate_out[owner] = jnp.transpose(accs[owner, 0])
-                up_out[owner] = jnp.transpose(accs[owner, 1])
-                down_out[owner] = accs[owner, 2]
+            while done <= len(marks) and marks[done - 1] <= place * outers + outer:
+                if done < levels:
+                    advance(done)
+                done += 1
+        if turn:
+            for which in range(3):
+                sends[turn - 1, which] = accs[which].astype(BF16)
+                copy = pltpu.make_async_remote_copy(
+                    src_ref=sends.at[turn - 1, which],
+                    dst_ref=takes.at[turn - 1, which],
+                    send_sem=send_sems.at[turn - 1, which],
+                    recv_sem=recv_sems.at[turn - 1, which],
+                    device_id={"group": flipped(group, turn)},
+                    device_id_type=MESH,
+                )
+                copy.start()
+                copies.append((turn, which, copy))
+        else:
+            gate_out[owner] = jnp.transpose(accs[0])
+            up_out[owner] = jnp.transpose(accs[1])
+            down_out[owner] = accs[2]
+    for level in range(done, levels + 1):
+        advance(level)
     for turn, which, copy in copies:
         copy.wait()
         owner = flipped(mine, turn)
@@ -991,21 +1317,40 @@
             (gate_out, up_out)[which][owner] = jnp.transpose(got)
 
 
-def weights(layout, row_ins, cot_ins, share_ins, expert_gate, expert_up, expert_down):
+def weights(layout, own, rows_far, cots_far, shares_far, expert_weights, terms, small):
     share, outers, peers = layout.share, layout.outers, layout.peers
-    experts, width, ff = expert_gate.shape
+    experts, width, ff = expert_weights[0].shape
     span = ff // outers
     cut = ff // layout.groups
     dma = pltpu.SemaphoreType.DMA
+    expert_levels = layout.experts.bit_length() - 1
+    group_levels = layout.groups.bit_length() - 1
+    levels = expert_levels + group_levels
+    scratch, outs = [], []
+    for number, term in enumerate(terms):
+        block = term.shape[-2:]
+        shapes = []
+        if number >= 3:
+            shapes += [
+                (layout.experts >> n, layout.groups) + block for n in range(1, expert_levels + 1)
+            ]
+        first = 2 if number < 3 else 1
+        shapes += [(layout.groups >> n,) + block for n in range(first, group_levels + 1)]
+        for shape in shapes:
+            scratch += [pltpu.VMEM(shape, BF16), dma((shape[0],)), dma((shape[0],))]
+        outs.append(jax.ShapeDtypeStruct(block, F32))
     return pl.pallas_call(
         functools.partial(weights_kernel, layout),
         out_shape=[
+            far_shape(layout, FAR_ROWS[2] - FAR_ROWS[1], width),
             jax.ShapeDtypeStruct((experts, width, cut), F32),
             jax.ShapeDtypeStruct((experts, width, cut), F32),
             jax.ShapeDtypeStruct((experts, cut, width), F32),
+            *outs,
+            jax.ShapeDtypeStruct((SMALL, width), F32),
         ],
-        in_specs=[ANY] * (3 * outers + 3),
-        out_specs=[VMEM] * 3,
+        in_specs=[ANY] * 12 + [VMEM] * 6,
+        out_specs=[ANY] + [VMEM] * 9,
         scratch_shapes=[
             pltpu.VMEM((width, span), BF16),
             pltpu.VMEM((width, span), BF16),
@@ -1015,34 +1360,32 @@
             pltpu.VMEM((2, peers, CAP, width), BF16),
             pltpu.VMEM((2, peers, CAP, width), BF16),
             pltpu.VMEM((2, peers, 8, LANES), F32),
-            pltpu.VMEM((share, 3, cut, width), F32),
+            pltpu.VMEM((3, cut, width), F32),
             pltpu.VMEM((share - 1, 3, cut, width), BF16),
             pltpu.VMEM((share - 1, 3, cut, width), BF16),
+            pltpu.VMEM((levels, SMALL, width), F32),
+            pltpu.VMEM((levels, SMALL, width), F32),
             dma((3,)),
-            dma((2, 3)),
+            dma((2, 7)),
             dma((share - 1, 3)),
             dma((share - 1, 3)),
+            dma((outers - 1,)),
+            dma((outers - 1,)),
+            dma((levels,)),
+            dma((levels,)),
+            *scratch,
         ],
         compiler_params=pltpu.CompilerParams(
             collective_id=4, has_side_effects=True, vmem_limit_bytes=60 * MIB
         ),
         cost_estimate=pl.CostEstimate(flops=1 << 30, bytes_accessed=1 << 20, transcendentals=0),
         name="weights",
-    )(*row_ins, *cot_ins, *share_ins, expert_gate, expert_up, expert_down)
-
-
-def swap(x, group_bits):
-    groups = lax.axis_size("group")
-    return lax.ppermute(x, "group", [(g, g ^ group_bits) for g in range(groups)])
-
-
-def gathered(layout, x):
-    return [x] + [swap(x, layout.share * k) for k in range(1, layout.outers)]
-
-
-def scatter_sum(parts):
-    made = parts.reshape(-1, parts.shape[-1])
-    return lax.psum_scatter(made, ("expert", "group"), scatter_dimension=0, tiled=True).astype(F32)
+    )(*own, *rows_far, *cots_far, shares_far, *expert_weights, *terms, small)
+
+
+def by_group(layout, terms):
+    parts, rows, width = terms.shape
+    return terms.reshape(parts, layout.groups, rows // layout.groups, width)
 
 
 def local(
@@ -1079,11 +1422,10 @@
     cosine = jnp.cos(angles)
     sine = jnp.sin(angles) * jnp.where(lane % HEAD < HEAD // 2, -1.0, 1.0)[None]
 
-    q, kv, att, att_t, lse, bias, target, cots = front(
+    q, kv, att, att_t, lse, bias, target, cots, cots_a = front(
         layout, tokens, gain_attn[None], w_qkv, cosine, sine, relative_row, seg_row, cotangent
     )
-    all_cots = gathered(layout, cots)
-    hidden, low, mixed, grad_low, gate_terms, up_terms, down_terms, rows_in, shares = middle(
+    hidden, low, mixed, grad_low, gate_terms, up_terms, down_terms, rows_in, shares, cots_b = middle(
         layout,
         att,
         tokens,
@@ -1096,14 +1438,19 @@
         dense_gate,
         dense_up,
         dense_down,
+        cots,
     )
-    all_rows = gathered(layout, rows_in)
-    all_shares = gathered(layout, shares)
-    gate_sum, up_sum, down_sum = map(scatter_sum, (gate_terms, up_terms, down_terms))
-    came_back, grad_back = run_experts(
-        layout, rows_in, cots, shares, expert_gate, expert_up, expert_down
+    came_back, grad_back, *sums, cots_c, rows_a, shares_far = run_experts(
+        layout,
+        rows_in,
+        cots,
+        shares,
+        expert_gate,
+        expert_up,
+        expert_down,
+        (gate_terms, up_terms, down_terms),
     )
-    mixed_out, grad_hidden, grad_att, proj_terms, router_term, gain_term = combine(
+    mixed_out, grad_hidden, grad_att, proj_terms, small = combine(
         layout,
         came_back,
         grad_back,
@@ -1119,8 +1466,7 @@
         w_out,
         att_t,
     )
-    proj_sum = scatter_sum(proj_terms)
-    grad_tokens, qkv_terms, attn_gain_term = back(
+    grad_tokens, qkv_terms, attn_gain_term, *sums, rows_b = back(
         layout,
         q,
         kv,
@@ -1134,25 +1480,31 @@
         cosine,
         sine,
         grad_hidden,
+        [by_group(layout, one)[0] for one in sums],
+        rows_in,
     )
-    qkv_sum = scatter_sum(qkv_terms)
-    router_sum, gain_ffn_sum, gain_attn_sum = lax.psum(
-        (router_term, gain_term, attn_gain_term), ("group", "expert")
-    )
-    grad_gate_w, grad_up_w, grad_down_w = weights(
-        layout, all_rows, all_cots, all_shares, expert_gate, expert_up, expert_down
+    small = lax.dynamic_update_slice(small, attn_gain_term, (EXPERTS + 1, 0))
+    _, gate_w, up_w, down_w, gate_sum, up_sum, down_sum, proj_sum, qkv_sum, small = weights(
+        layout,
+        (rows_in, cots, shares),
+        (rows_a, rows_b),
+        (cots_a, cots_b, cots_c),
+        shares_far,
+        (expert_gate, expert_up, expert_down),
+        [*sums, by_group(layout, proj_terms), by_group(layout, qkv_terms)],
+        small,
     )
     return (
         mixed_out,
         grad_tokens,
-        gain_attn_sum[0],
+        small[EXPERTS + 1],
         qkv_sum,
         proj_sum,
-        gain_ffn_sum[0],
-        router_sum,
-        grad_gate_w,
-        grad_up_w,
-        grad_down_w,
+        small[EXPERTS],
+        jnp.transpose(small[:EXPERTS]),
+        gate_w,
+        up_w,
+        down_w,
         gate_sum,
         up_sum,
         down_sum,

time: 921 us -> 466 us (0.51)
  waiting for transfers between devices: 335 us -> 0 us
  blocking collectives: 200 us -> 0 us
  Pallas kernels: 319 us -> 429 us
  between operations: 14.2 us -> 1.2 us
    reduce_scatter x5 -> x0, waiting for transfers between devices: 334 us -> none  [scatter_sum(): lax.psum_scatter(made, ('expert', 'group'), scatter_dimension=0, tiled=True)]
    psum x1 -> x0, blocking collectives: 200 us -> none  [local(): lax.psum((router_term, gain_term, attn_gain_term), ('group', 'expert'))]
    pallas_call x1, Pallas kernels: 69.9 us -> 107 us  [run_experts(): pl.pallas_call(functools.partial(experts_kernel, layout), out_shape=[jax....]
    pallas_call x1, Pallas kernels: 94.4 us -> 116 us  [weights(): pl.pallas_call(functools.partial(weights_kernel, layout), out_shape=[far_...]
    pallas_call x1, Pallas kernels: 46.1 us -> 65.4 us  [middle(): pl.pallas_call(functools.partial(middle_kernel, layout), out_shape=[jax.S...]
    pallas_call x1, Pallas kernels: 36.2 us -> 55.2 us  [back(): pl.pallas_call(functools.partial(back_kernel, layout), out_shape=[jax.Sha...]
    pallas_call x1, Pallas kernels: 59.8 us -> 71.7 us  [front(): pl.pallas_call(functools.partial(front_kernel, layout), out_shape=[jax.Sh...]
  transfers between devices with their start and end apart: 8 -> 0, of which waited for: 4 -> 0; matrix products, arithmetic and copies ran while one was open for 1% -> 0% of each run, Pallas kernels for 14% -> 0%
where the time goes in v3:
time: 466 us; the launch traced here: 458 us
  Pallas kernels  429 us (92%)
  local copies, waits for them, and re-layouts  24.6 us (5%)
    pallas_call x1, Pallas kernels, weights(): pl.pallas_call(functools.partial(weights_kernel, layout), out_shape=[far_...  116 us
    pallas_call x1, Pallas kernels, run_experts(): pl.pallas_call(functools.partial(experts_kernel, layout), out_shape=[jax....  107 us
    pallas_call x1, Pallas kernels, front(): pl.pallas_call(functools.partial(front_kernel, layout), out_shape=[jax.Sh...  71.7 us
    pallas_call x1, Pallas kernels, middle(): pl.pallas_call(functools.partial(middle_kernel, layout), out_shape=[jax.S...  65.4 us
    pallas_call x1, Pallas kernels, back(): pl.pallas_call(functools.partial(back_kernel, layout), out_shape=[jax.Sha...  55.2 us
    unnamed x31, local copies, waits for them, and re-layouts  16.7 us
    pallas_call x1, Pallas kernels, combine(): pl.pallas_call(combine_kernel, out_shape=[jax.ShapeDtypeStruct((rows, wid...  13.1 us

profile of v3, /device:TPU:0, one launch (start us, length us, event | category | flops | bytes accessed | tf_op | source)
XLA Modules:
  0.0 457.8 jit_solution(7321831086796207502)
XLA Ops:
  0.7 0.7 add_bitcast_fusion
  1.4 0.6 concatenate.6.ids_row
  2.0 1.8 fusion
  3.8 1.3 broadcast_in_dim.14.gain
  5.1 0.7 convert_element_type.19
  5.8 0.6 broadcast_in_dim.29.seg_row
  6.4 71.7 %front.1 = (bf16[512,768]{1,0:T(8,128)(2,1)}, bf16[2,512,1536]{2,1,0:T(8,128)(2,1)}, bf16[512,768]{1,0:T(8,128)(2,1)}, bf16[768,512]{1,0:T(8,128)(2,1)}, f32[16,...) custom-call(bf16[512,768]{1,0:T(8,128)(2,1)} %tokens.5, ...), custom_call_target="tpu_custom_call" | custom-call | flops 1073741824 | bytes 1048576 | tf_op jit(solution)/shard_map/front/pallas_call | solution.py:380
  78.1 0.6 broadcast_in_dim.30.gain
  78.7 0.6 concatenate.7.ids_row
  79.3 65.4 %middle.1 = (f32[512,768]{1,0:T(8,128)}, bf16[512,768]{1,0:T(8,128)(2,1)}, f32[512,768]{1,0:T(8,128)}, f32[512,768]{1,0:T(8,128)}, bf16[2,768,512]{2,1,0:T(8,128...) custom-call(bf16[512,768]{1,0:T(8,128)(2,1)} %get-tuple-element.61.a, ...), custom_call_target="tpu_custom_call" | custom-call | flops 1073741824 | bytes 1048576 | tf_op jit(solution)/shard_map/middle/pallas_call | solution.py:571
  144.7 0.0 copy-start.6
  144.7 107.0 %experts.1 = (bf16[16,80,768]{2,1,0:T(8,128)(2,1)}, bf16[16,80,768]{2,1,0:T(8,128)(2,1)}, bf16[1,768,512]{2,1,0:T(8,128)(2,1)}, bf16[1,768,512]{2,1,0:T(8,128)(2...) custom-call(bf16[16,80,768]{2,1,0:T(8,128)(2,1)} %get-tuple-element., ...), custom_call_target="tpu_custom_call" | custom-call | flops 1073741824 | bytes 1048576 | tf_op jit(solution)/shard_map/experts/pallas_call | solution.py:764
  251.7 0.9 copy.28.ids_col
  252.6 0.8 copy.29.w_router
  253.4 13.1 %combine.1 = (bf16[512,768]{1,0:T(8,128)(2,1)}, f32[512,768]{1,0:T(8,128)}, bf16[512,768]{1,0:T(8,128)(2,1)}, bf16[4,768,192]{2,1,0:T(8,128)(2,1)}, f32[24,768]{1,0:T(8,128)}) custom-call(bf16[16,80,768]{2,1,0:T(8,128)(2,1)} %get-tuple-element.69.back, bf16[16,80,768]{2,1,0:T(8,128)(2,1)} %get-tuple-element.70.grad_back, ...), custom_call_target="tpu_custom_call" | custom-call | flops 1073741824 | bytes 1048576 | tf_op jit(solution)/shard_map/combine/pallas_call | solution.py:890
  266.5 55.2 %back.1 = (f32[512,768]{1,0:T(8,128)}, bf16[4,768,576]{2,1,0:T(8,128)(2,1)}, f32[1,768]{1,0:T(1,128)}, bf16[4,96,512]{2,1,0:T(8,128)(2,1)}, bf16[4,96,512]{2,1,0...) custom-call(bf16[512,768]{1,0:T(8,128)(2,1)} %get-tuple-element.77.q_in, ...), custom_call_target="tpu_custom_call" | custom-call | flops 1073741824 | bytes 1048576 | tf_op jit(solution)/shard_map/back/pallas_call | solution.py:1062
  321.7 1.4 dynamic_update_slice.3.refs_17_
  323.1 116.4 %weights.1 = (bf16[1,3,80,768]{3,2,1,0:T(8,128)(2,1)}, f32[4,768,256]{2,1,0:T(8,128)}, f32[4,768,256]{2,1,0:T(8,128)}, f32[4,256,768]{2,1,0:T(8,128)}, f32[96,51...) custom-call(bf16[16,80,768]{2,1,0:T(8,128)(2,1)} %get-tuple-element., ...), custom_call_target="tpu_custom_call" | custom-call | flops 1073741824 | bytes 1048576 | tf_op jit(solution)/shard_map/weights/pallas_call | solution.py:1342
  439.5 1.9 copy.30
  441.4 1.4 slice_bitcast_fusion
  442.9 1.4 slice_reduce_fusion
  444.3 2.7 copy.40
  446.9 0.7 copy.41
  447.6 0.0 copy-done.7
  447.6 0.6 copy.42
  448.3 1.7 copy.43
  450.0 1.4 copy-done.1
  451.3 1.7 copy.44
  453.0 1.4 copy-done
  454.3 1.7 copy.45
  456.0 0.7 copy.46
  456.7 0.7 copy.47
  (18 shorter events, 0.0 us)
Async XLA Ops:
  6.4 71.7 %copy-start.9 = (f32[768]{0:T(1024)S(1)}, f32[768]{0:T(1024)}, u32[]{:S(2)}) copy-start(f32[768]{0:T(1024)} %param.19) | copy-start | bytes 9220
  6.4 72.3 %copy-start.8 = (s32[512,2]{0,1:T(2,128)S(1)}, s32[512,2]{0,1:T(2,128)}, u32[]{:S(2)}) copy-start(s32[512,2]{0,1:T(2,128)} %param.27) | copy-start | bytes 12292
  144.7 107.9 %copy-start.6 = (bf16[768,16]{0,1:T(8,128)(2,1)S(1)}, bf16[768,16]{0,1:T(8,128)(2,1)}, u32[]{:S(2)}) copy-start(bf16[768,16]{0,1:T(8,128)(2,1)} %param.20) | copy-start | bytes 73732
  439.5 7.4 %copy-start.3 = (f32[96,576]{1,0:T(8,128)S(1)}, f32[96,576]{1,0:T(8,128)}, u32[]{:S(2)}) copy-start(f32[96,576]{1,0:T(8,128)} %get-tuple-element.144) | copy-start | bytes 663556
  439.5 8.1 %copy-start.7 = (f32[96,192]{1,0:T(8,128)S(1)}, f32[96,192]{1,0:T(8,128)}, u32[]{:S(2)}) copy-start(f32[96,192]{1,0:T(8,128)} %get-tuple-element.145) | copy-start | bytes 221188
  439.5 8.7 %copy-start.2 = (f32[4,768,256]{2,1,0:T(8,128)S(1)}, f32[4,768,256]{2,1,0:T(8,128)}, u32[]{:S(2)}) copy-start(f32[4,768,256]{2,1,0:T(8,128)} %get-tuple-element.148) | copy-start | bytes 9437188
  448.3 3.0 copy-start.1
  451.3 3.0 copy-start
  454.3 1.7 copy-start.5
  454.3 2.3 copy-start.4
